TPU v7x, 32 devices: a whole 2x2x4 slice. The times are simulated.
32 devices in a mesh: groups: 2 (over y), node: 2 (over x), local: 4 (over z), rep: 2 (over core).
Axes of the slice: x: 2, y: 2, z: 4, core: 2. Of those that a mesh axis runs over, the one named last changes fastest.
Arguments:
- tokens: bfloat16 [4096, 3584], P(('groups', 'node', 'local', 'rep')), parts along dimension 0, may hold values from -6 to 6
- cotangent: bfloat16 [4096, 3584], P(('groups', 'node', 'local', 'rep')), parts along dimension 0, may hold values from -6 to 6
- expert_ids: int32 [4096, 1], P(('groups', 'node', 'local', 'rep')), parts along dimension 0, may hold values from 0 to 1
- gate_values: float32 [4096, 1], P(('groups', 'node', 'local', 'rep')), parts along dimension 0, may hold values from 0.1 to 1
- w_gate: bfloat16 [2, 3584, 1024], P('node', 'local', 'rep'), may hold values from -0.09375 to 0.09375
- w_up: bfloat16 [2, 3584, 1024], P('node', 'local', 'rep'), may hold values from -0.09375 to 0.09375
- feedback: bfloat16 [2, 1024, 3584], P('node', 'rep', 'local'), may hold values from -8 to 8
Outputs:
- grad_down: bfloat16 [4, 1024, 3584], P(('groups', 'node'), 'rep', 'local'), parts along dimension 0
There are 2 independent parts, one for each index of `groups`. A program takes and returns all parts, laid end to end along the dimension named above; an argument that names none is the same for every part. Nothing has to cross between parts.
All inputs are finite; a program needn't handle non-finite values.
Results may differ from a plain program's by a relative error of at most 0.012.
Values may be sent and summed in bfloat16 or wider, within the bound.
No kernel may reach another device: no remote copies, remote signals or barrier semaphores. Data moves between devices by JAX's collectives and lax.ppermute only.
A program may use at most 64 MiB of HBM per device.

v0:
```python
import jax
import jax.numpy as jnp
from jax import lax
from jax.sharding import PartitionSpec as P


def swapped(value, axis, distance):
    mask = 2**distance
    pairs = [(source, source ^ mask) for source in range(lax.axis_size(axis))]
    return lax.ppermute(value, axis, pairs)


def local(tokens, cotangent, expert_ids, gate_values, w_gate, w_up, feedback):
    token_count, model_width = tokens.shape
    top_count = expert_ids.shape[1]
    node_count = lax.axis_size("node")
    capacity = max(2, token_count * top_count // node_count)
    flat_ids = expert_ids.reshape(-1)
    onehot = (flat_ids[:, None] == jnp.arange(node_count, dtype=jnp.int32)[None, :]).astype(
        jnp.int32
    )
    before = jnp.cumsum(onehot, axis=0) - onehot
    slot_rank = jnp.sum(before * onehot, axis=1)
    target = jnp.where(slot_rank < capacity, flat_ids * capacity + slot_rank, node_count * capacity)
    source_row = jnp.arange(token_count * top_count, dtype=jnp.int32) // top_count
    scaled = (gate_values[:, :, None] * cotangent[:, None, :].astype(jnp.float32)).astype(
        jnp.bfloat16
    )
    scaled = scaled.reshape(token_count * top_count, model_width)
    empty_rows = jnp.zeros((node_count * capacity, model_width), jnp.bfloat16)
    send_tokens = (
        empty_rows.at[target]
        .set(tokens[source_row], mode="drop")
        .reshape(node_count, capacity, model_width)
    )
    send_scaled = (
        empty_rows.at[target].set(scaled, mode="drop").reshape(node_count, capacity, model_width)
    )
    recv_tokens, recv_scaled = (
        lax.all_to_all(send_tokens, "node", split_axis=0, concat_axis=0, tiled=True),
        lax.all_to_all(send_scaled, "node", split_axis=0, concat_axis=0, tiled=True),
    )
    other_tokens, other_scaled = swapped((recv_tokens, recv_scaled), "rep", 0)
    x_rows = jnp.concatenate(
        [recv_tokens.reshape(-1, model_width), other_tokens.reshape(-1, model_width)], axis=0
    )
    dy_rows = jnp.concatenate(
        [recv_scaled.reshape(-1, model_width), other_scaled.reshape(-1, model_width)], axis=0
    )
    gate_full, up_full = (
        lax.all_gather(w_gate, "local", axis=1, tiled=True),
        lax.all_gather(w_up, "local", axis=1, tiled=True),
    )
    gate_mat = gate_full[0]
    up_mat = up_full[0]
    pre_gate = jnp.dot(x_rows, gate_mat, preferred_element_type=jnp.float32)
    pre_up = jnp.dot(x_rows, up_mat, preferred_element_type=jnp.float32)
    hidden = (jax.nn.silu(pre_gate) * pre_up).astype(jnp.bfloat16)
    term_grad = lax.dot_general(
        hidden, dy_rows, (((0,), (0,)), ((), ())), preferred_element_type=jnp.float32
    )
    compressed = lax.optimization_barrier(term_grad.astype(jnp.bfloat16)).astype(jnp.float32)
    summed = lax.psum_scatter(
        compressed.astype(jnp.bfloat16), "local", scatter_dimension=1, tiled=True
    ).astype(jnp.float32)
    grad_down = (summed + feedback[0].astype(jnp.float32)).astype(jnp.bfloat16)[None]
    return grad_down


def solution(mesh):
    placed = (
        P(("groups", "node", "local", "rep"), None),
        P(("groups", "node", "local", "rep"), None),
        P(("groups", "node", "local", "rep"), None),
        P(("groups", "node", "local", "rep"), None),
        P("node", "local", "rep"),
        P("node", "local", "rep"),
        P("node", "rep", "local"),
    )
    return jax.shard_map(
        local,
        mesh=mesh,
        in_specs=placed,
        out_specs=P(("groups", "node"), "rep", "local"),
        check_vma=False,
    )
```

profile of v0, /device:TPU:0, one launch (start us, length us, event | category | flops | bytes accessed | tf_op | source)
XLA Modules:
  0.0 245.2 jit_solution(4162277884053559893)
XLA Ops:
  6.5 0.7 all-gather.5.cloned.1.call-update
  7.3 0.0 all-gather.3.cloned.1.call-start
  7.3 0.7 all-gather.3.cloned.1.call-update
  8.0 0.7 fusion.20
  8.8 0.2 reduce_window_sum.11
  8.9 0.8 select_reduce_fusion
  9.8 0.7 fusion.21
  10.4 5.5 %scatter_custom_fusion = bf16[128,3584]{1,0:T(8,128)(2,1)} fusion(s32[128]{0:T(128)S(1)} %fusion.21, bf16[128,3584]{1,0:T(8,128)(2,1)S(1)} %copy-done, s32[1024]{0:T(1024)S(1)} %pad_clamp_fusion, bf16[]{:T(256)} %constant.24.clone.1), kind=kCustom, calls=%fused_computation.17 | custom fusion | bytes 917506 | tf_op jit(solution)/shard_map/scatter | solution.py:33
  16.0 4.2 %all-to-all-start = ((bf16[2,64,3584]{2,1,0:T(8,128)(2,1)}), bf16[2,64,3584]{2,1,0:T(8,128)(2,1)S(1)}, u32[]{:S(2)}, u32[]{:S(2)}) async-start(bf16[2,64,3584]{2,1,0:T(8,128)(2,1)} %bitcast.3), calls=%async_computation | async-start | bytes 1835008 | tf_op jit(solution)/shard_map/all_to_all | solution.py:40
  20.2 2.9 %scatter_custom_fusion.1 = bf16[128,3584]{1,0:T(8,128)(2,1)} fusion(s32[128]{0:T(128)S(1)} %fusion.21, bf16[128,3584]{1,0:T(8,128)(2,1)S(1)} %copy-done.1, f32[128]{0:T(128)S(1)} %bitcast.43, bf16[]{:T(256)} %constant.24.clone.1), kind=kCustom, calls=%fused_computation.15 | custom fusion | flops 1376256 | bytes 1835522 | tf_op jit(solution)/shard_map/scatter | solution.py:37
  23.1 10.2 %all-to-all-done = bf16[2,64,3584]{2,1,0:T(8,128)(2,1)S(1)} async-done(((bf16[2,64,3584]{2,1,0:T(8,128)(2,1)}), bf16[2,64,3584]{2,1,0:T(8,128)(2,1)S(1)}, u32[]{:S(2)}, u32[]{:S(2)}) %all-to-all-start) | async-done | bytes 917536 | tf_op jit(solution)/shard_map/all_to_all | solution.py:40
  33.2 3.6 %all-to-all-start.1 = ((bf16[2,64,3584]{2,1,0:T(8,128)(2,1)}), bf16[2,64,3584]{2,1,0:T(8,128)(2,1)S(1)}, u32[]{:S(2)}, u32[]{:S(2)}) async-start(bf16[2,64,3584]{2,1,0:T(8,128)(2,1)} %bitcast.9), calls=%async_computation.1 | async-start | bytes 1835008 | tf_op jit(solution)/shard_map/all_to_all | solution.py:41
  36.8 0.0 reduce-scatter.4.cloned.1.call-start
  36.8 0.1 collective-permute-start
  36.9 11.9 %all-to-all-done.1 = bf16[2,64,3584]{2,1,0:T(8,128)(2,1)S(1)} async-done(((bf16[2,64,3584]{2,1,0:T(8,128)(2,1)}), bf16[2,64,3584]{2,1,0:T(8,128)(2,1)S(1)}, u32[]{:S(2)}, u32[]{:S(2)}) %all-to-all-start.1) | async-done | bytes 917536 | tf_op jit(solution)/shard_map/all_to_all | solution.py:41
  48.8 35.0 %all-gather.5.cloned.1.call-done = bf16[1,3584,512]{2,1,0:T(8,128)(2,1)} async-done(((bf16[1,896,512]{2,1,0:T(8,128)(2,1)}), bf16[1,3584,512]{2,1,0:T(8,128)(2,1)}) %all-gather.5.cloned.1.call-update) | async-done | bytes 3670032 | tf_op jit(solution)/shard_map/all_gather | solution.py:52
  83.8 3.4 %fusion = f32[256,512]{1,0:T(8,128)S(1)} fusion(bf16[1,3584,512]{2,1,0:T(8,128)(2,1)} %all-gather.5.cloned.1.call-done, bf16[128,3584]{1,0:T(8,128)(2,1)} %bitcast.5, bf16[128,3584]{1,0:T(8,128)(2,1)S(1)} %bitcast.37), kind=kOutput, calls=%fused_computation.4 | convolution fusion | flops 943194112 | bytes 6029312 | tf_op jit(solution)/shard_map/dot_general | solution.py:57
  87.2 68.9 %all-gather.3.cloned.1.call-done = bf16[1,3584,512]{2,1,0:T(8,128)(2,1)} async-done(((bf16[1,896,512]{2,1,0:T(8,128)(2,1)}), bf16[1,3584,512]{2,1,0:T(8,128)(2,1)}) %all-gather.3.cloned.1.call-update) | async-done | bytes 3670032 | tf_op jit(solution)/shard_map/all_gather | solution.py:51
  156.1 6.7 %convolution_convert_fusion = bf16[512,3584]{1,0:T(8,128)(2,1)} fusion(bf16[128,3584]{1,0:T(8,128)(2,1)} %bitcast.11, bf16[128,3584]{1,0:T(8,128)(2,1)S(1)} %bitcast.39, f32[256,512]{1,0:T(8,128)S(1)} %fusion, bf16[1,3584,512]{2,1,0:T(8,128)(2,1)} %all-gather.3.cloned.1.call-done, bf16[128,3584]{1,0:T(8,128)(2,1)} %bitcast.5, bf16[128,3584]{1,0:T(8,128)(2,1)S(1)} %bitcast.38), kind=kOutput, calls=%fused_computation.3 | convolution fusion | flops 1889009664 | bytes 11534336 | tf_op jit(solution)/shard_map/dot_general | solution.py:59
  162.8 5.9 %copy.8 = bf16[512,3584]{0,1:T(8,128)(2,1)} copy(bf16[512,3584]{1,0:T(8,128)(2,1)} %convolution_convert_fusion) | data formatting | bytes 7340032
  168.8 0.0 reduce-scatter.4.cloned.1.call-update
  168.8 67.2 %reduce-scatter.4.cloned.1.call-done = bf16[896,512]{1,0:T(8,128)(2,1)} async-done(((bf16[3584,512]{1,0:T(8,128)(2,1)}), bf16[896,512]{1,0:T(8,128)(2,1)}) %reduce-scatter.4.cloned.1.call-update) | async-done | bytes 917520
  236.0 1.5 copy.9
  237.5 1.1 fusion.9
  (14 shorter events, 0.0 us)
Async XLA Ops:
  6.5 3.9 %copy-start = (bf16[128,3584]{1,0:T(8,128)(2,1)S(1)}, bf16[128,3584]{1,0:T(8,128)(2,1)}, u32[]{:S(2)}) copy-start(bf16[128,3584]{1,0:T(8,128)(2,1)} %param.7) | copy-start | bytes 2752516
  6.5 13.6 %copy-start.3 = (f32[128,1]{0,1:T(1,128)S(1)}, f32[128,1]{0,1:T(1,128)}, u32[]{:S(2)}) copy-start(f32[128,1]{0,1:T(1,128)} %param.10) | copy-start | bytes 1540
  6.5 13.6 %copy-start.1 = (bf16[128,3584]{1,0:T(8,128)(2,1)S(1)}, bf16[128,3584]{1,0:T(8,128)(2,1)}, u32[]{:S(2)}) copy-start(bf16[128,3584]{1,0:T(8,128)(2,1)} %param.8) | copy-start | bytes 2752516
  6.5 77.2 %all-gather.5.cloned.1.call-start = ((), (), s32[]{:S(2)}) async-start(), calls=%async_computation.4 | async-start | bytes 4587520 | tf_op jit(solution)/shard_map/all_gather | solution.py:52
  7.3 148.8 %all-gather.3.cloned.1.call-start = ((), (), s32[]{:S(2)}) async-start(), calls=%async_computation.3 | async-start | bytes 4587520 | tf_op jit(solution)/shard_map/all_gather | solution.py:51
  16.0 17.3 %all-to-all-start = ((bf16[2,64,3584]{2,1,0:T(8,128)(2,1)}), bf16[2,64,3584]{2,1,0:T(8,128)(2,1)S(1)}, u32[]{:S(2)}, u32[]{:S(2)}) async-start(bf16[2,64,3584]{2,1,0:T(8,128)(2,1)} %bitcast.3), calls=%async_computation | async-start | bytes 1835008 | tf_op jit(solution)/shard_map/all_to_all | solution.py:40
  33.2 15.6 %all-to-all-start.1 = ((bf16[2,64,3584]{2,1,0:T(8,128)(2,1)}), bf16[2,64,3584]{2,1,0:T(8,128)(2,1)S(1)}, u32[]{:S(2)}, u32[]{:S(2)}) async-start(bf16[2,64,3584]{2,1,0:T(8,128)(2,1)} %bitcast.9), calls=%async_computation.1 | async-start | bytes 1835008 | tf_op jit(solution)/shard_map/all_to_all | solution.py:41
  36.8 199.2 %reduce-scatter.4.cloned.1.call-start = ((), (), s32[]{:S(2)}) async-start(), calls=%async_computation.5 | async-start | bytes 4587520
  36.8 11.9 %collective-permute-start = (bf16[2,64,3584]{2,1,0:T(8,128)(2,1)S(1)}, bf16[2,64,3584]{2,1,0:T(8,128)(2,1)}, u32[]{:S(2)}, u32[]{:S(2)}) collective-permute-start(bf16[2,64,3584]{2,1,0:T(8,128)(2,1)S(1)} %all-to-all-done), channel_id=1, source_target_pairs={{0,1},{1,0},{2,3},{3,2},{4,5},{5,4},{6,7},{7,6},{8,9},{9,8},{10,11... | collective-permute-start | bytes 2752520 | tf_op jit(solution)/shard_map/ppermute | solution.py:10
  48.8 38.4 %collective-permute-start.1 = (bf16[2,64,3584]{2,1,0:T(8,128)(2,1)S(1)}, bf16[2,64,3584]{2,1,0:T(8,128)(2,1)}, u32[]{:S(2)}, u32[]{:S(2)}) collective-permute-start(bf16[2,64,3584]{2,1,0:T(8,128)(2,1)S(1)} %all-to-all-done.1), channel_id=1, source_target_pairs={{0,1},{1,0},{2,3},{3,2},{4,5},{5,4},{6,7},{7,6},{8,9},{9,8},{10,11... | collective-permute-start | bytes 2752520 | tf_op jit(solution)/shard_map/ppermute | solution.py:10
  168.8 68.7 %copy-start.2 = (bf16[1,512,896]{2,1,0:T(8,128)(2,1)S(1)}, bf16[1,512,896]{2,1,0:T(8,128)(2,1)}, u32[]{:S(2)}) copy-start(bf16[1,512,896]{2,1,0:T(8,128)(2,1)} %param.13) | copy-start | bytes 2752516
Sparse Core Ops, SparseCore 0:
  8.9 74.7 all-gather.4
  85.3 70.7 all-gather.2
  168.9 67.0 reduce-scatter.3
where the time goes:
time: 246 us; the launch traced here: 245 us
  waiting for transfers between devices  195 us (79%)
  between operations  13.2 us (5%)
  local copies, waits for them, and re-layouts  13 us (5%)
  matrix products  10.2 us (4%)
  starting transfers between devices  7.92 us (3%)
  other arithmetic  6.43 us (3%)
    all_gather x1, waiting for transfers between devices, local(): lax.all_gather(w_gate, 'local', axis=1, tiled=True)  68.9 us
    unnamed x4, waiting for transfers between devices  68.6 us
    all_gather x1, waiting for transfers between devices, local(): lax.all_gather(w_up, 'local', axis=1, tiled=True)  35 us
    all_to_all x1, waiting for transfers between devices, local(): lax.all_to_all(send_scaled, 'node', split_axis=0, concat_axis=0, tiled=True)  11.9 us
    all_to_all x1, waiting for transfers between devices, local(): lax.all_to_all(send_tokens, 'node', split_axis=0, concat_axis=0, tiled=True)  10.2 us
    unnamed x10, local copies, waits for them, and re-layouts  7.47 us
    dot_general x1, matrix products, local(): lax.dot_general(hidden, dy_rows, (((0,), (0,)), ((), ())), preferred_elem...  6.73 us
    scatter x1, local copies, waits for them, and re-layouts, local(): send_tokens = empty_rows.at[target].set(tokens[source_row], mode='drop')....  5.52 us
  transfers between devices with their start and end apart: 7, of which 5 were waited for; matrix products, arithmetic and copies ran while one was open for 6% of the time, Pallas kernels for 0%

commit v1 on v0

v1 whole, which is shorter than its diff:
```python
import functools

import jax
import jax.numpy as jnp
from jax import lax
from jax.experimental import pallas as pl
from jax.experimental.pallas import tpu as pltpu
from jax.sharding import PartitionSpec as P


def swapped(value, axis):
    return lax.ppermute(value, axis, [(s, s ^ 1) for s in range(lax.axis_size(axis))])


def dispatch_kernel(nodes, blocks, capacity, ids_ref, gate_ref, x_ref, c_ref, sx_ref, sy_ref):
    pairs = ids_ref.shape[1]
    width = x_ref.shape[1] // blocks
    ids = ids_ref[...]
    row = lax.broadcasted_iota(jnp.int32, (pairs, pairs), 0)
    col = lax.broadcasted_iota(jnp.int32, (pairs, pairs), 1)
    earlier = (row < col).astype(jnp.bfloat16)
    slots = lax.broadcasted_iota(jnp.int32, (capacity, pairs), 0)
    for node in range(nodes):
        named = ids == node
        rank = jnp.dot(
            jnp.broadcast_to(named, (8, pairs)).astype(jnp.bfloat16),
            earlier,
            preferred_element_type=jnp.float32,
        )[:1].astype(jnp.int32)
        pick = jnp.where((rank == slots) & named, 1.0, 0.0)
        gate = jnp.sum(pick * gate_ref[...], axis=1, keepdims=True)
        pick = pick.astype(jnp.bfloat16)
        for block in range(blocks):
            cols = slice(block * width, (block + 1) * width)
            x_rows = jnp.dot(pick, x_ref[:, cols], preferred_element_type=jnp.float32)
            c_rows = jnp.dot(pick, c_ref[:, cols], preferred_element_type=jnp.float32)
            sx_ref[node * blocks + block] = x_rows.astype(jnp.bfloat16)
            sy_ref[node * blocks + block] = (gate * c_rows).astype(jnp.bfloat16)


def dispatch(ids, gates, tokens, cotangent, nodes, blocks, capacity):
    width = tokens.shape[1] // blocks
    out = jax.ShapeDtypeStruct((nodes * blocks, capacity, width), jnp.bfloat16)
    vmem = pl.BlockSpec(memory_space=pltpu.VMEM)
    return pl.pallas_call(
        functools.partial(dispatch_kernel, nodes, blocks, capacity),
        out_shape=(out, out),
        in_specs=[vmem] * 4,
        out_specs=(vmem, vmem),
        compiler_params=pltpu.CompilerParams(vmem_limit_bytes=32 << 20),
    )(ids, gates, tokens, cotangent)


def local(tokens, cotangent, expert_ids, gate_values, w_gate, w_up, feedback):
    token_count = tokens.shape[0]
    top_count = expert_ids.shape[1]
    nodes, blocks = lax.axis_size("node"), lax.axis_size("local")
    capacity = max(2, token_count * top_count // nodes)
    width = tokens.shape[1] // blocks
    if top_count > 1:
        tokens = jnp.repeat(tokens, top_count, axis=0)
        cotangent = jnp.repeat(cotangent, top_count, axis=0)
    send_x, send_y = dispatch(
        expert_ids.reshape(1, -1),
        gate_values.reshape(1, -1),
        tokens,
        cotangent,
        nodes,
        blocks,
        capacity,
    )
    axes = ("node", "local")
    own_x = lax.all_to_all(send_x, axes, 0, 0, tiled=True).reshape(-1, width)
    own_y = lax.all_to_all(send_y, axes, 0, 0, tiled=True).reshape(-1, width)
    x_rows = jnp.concatenate([own_x, swapped(own_x, "rep")], axis=0)
    y_rows = jnp.concatenate([own_y, swapped(own_y, "rep")], axis=0)
    weights = jnp.concatenate([w_gate[0], w_up[0]], axis=1)
    partial = jnp.dot(x_rows, weights, preferred_element_type=jnp.float32).astype(jnp.bfloat16)
    pre = lax.psum_scatter(partial, "local", scatter_dimension=0, tiled=True).astype(jnp.float32)
    pre_gate, pre_up = jnp.split(pre, 2, axis=1)
    hidden = (jax.nn.silu(pre_gate) * pre_up).astype(jnp.bfloat16)
    hidden = lax.all_gather(hidden, "local", axis=0, tiled=True)
    grad = lax.dot_general(
        hidden, y_rows, (((0,), (0,)), ((), ())), preferred_element_type=jnp.float32
    )
    return (grad + feedback[0].astype(jnp.float32)).astype(jnp.bfloat16)[None]


def solution(mesh):
    rows = P(("groups", "node", "local", "rep"), None)
    weights = P("node", "local", "rep")
    return jax.shard_map(
        local,
        mesh=mesh,
        in_specs=(rows, rows, rows, rows, weights, weights, P("node", "rep", "local")),
        out_specs=P(("groups", "node"), "rep", "local"),
        check_vma=False,
    )
```

time: 246 us -> 149 us (0.61)
  waiting for transfers between devices: 195 us -> 86.1 us
  blocking collectives: 0 us -> 30.9 us
  local copies, waits for them, and re-layouts: 13 us -> 3.68 us
  other arithmetic: 6.43 us -> 2.02 us
  starting transfers between devices: 7.92 us -> 3.68 us
  matrix products: 10.2 us -> 7.11 us
    all_gather x2 -> x1, waiting for transfers between devices: 104 us -> 27.4 us  [local(): hidden = lax.all_gather(hidden, 'local', axis=0, tiled=True)]
    unnamed x4 -> x2, waiting for transfers between devices: 68.6 us -> 0.03 us
    reduce_scatter x0 -> x1, waiting for transfers between devices: none -> 53.8 us  [local(): lax.psum_scatter(partial, 'local', scatter_dimension=0, tiled=True)]
    all_to_all x0 -> x1, blocking collectives: none -> 30.9 us  [local(): own_x = lax.all_to_all(send_x, axes, 0, 0, tiled=True).reshape(-1, width)]
    all_to_all x2 -> x1, waiting for transfers between devices: 22 us -> 0.01 us  [local(): own_y = lax.all_to_all(send_y, axes, 0, 0, tiled=True).reshape(-1, width)]
    scatter x1 -> x0, local copies, waits for them, and re-layouts: 5.52 us -> none  [local(): send_tokens = empty_rows.at[target].set(tokens[source_row], mode='drop')....]
    ppermute x2, waiting for transfers between devices: 0.01 us -> 4.93 us  [swapped(): lax.ppermute(value, axis, [(s, s ^ 1) for s in range(lax.axis_size(axis))])]
    all_to_all x2 -> x1, starting transfers between devices: 7.77 us -> 3.57 us  [local(): own_y = lax.all_to_all(send_y, axes, 0, 0, tiled=True).reshape(-1, width)]
  transfers between devices with their start and end apart: 7 -> 5, of which waited for: 5 -> 4; matrix products, arithmetic and copies ran while one was open for 6% -> 1% of each run, Pallas kernels for 0% -> 0%
where the time goes in v1:
time: 149 us
  waiting for transfers between devices  86.1 us (58%)
  blocking collectives  30.9 us (21%)
  between operations  13.4 us (9%)
  matrix products  7.11 us (5%)
  starting transfers between devices  3.68 us (2%)
  local copies, waits for them, and re-layouts  3.68 us (2%)
  other arithmetic  2.02 us (1%)
  Pallas kernels  1.91 us (1%)
    reduce_scatter x1, waiting for transfers between devices, local(): lax.psum_scatter(partial, 'local', scatter_dimension=0, tiled=True)  53.8 us
    all_to_all x1, blocking collectives, local(): own_x = lax.all_to_all(send_x, axes, 0, 0, tiled=True).reshape(-1, width)  30.9 us
    all_gather x1, waiting for transfers between devices, local(): hidden = lax.all_gather(hidden, 'local', axis=0, tiled=True)  27.4 us
    ppermute x2, waiting for transfers between devices, swapped(): lax.ppermute(value, axis, [(s, s ^ 1) for s in range(lax.axis_size(axis))])  4.93 us
    dot_general x1, matrix products, local(): jnp.dot(x_rows, weights, preferred_element_type=jnp.float32)  3.68 us
    unnamed x14, local copies, waits for them, and re-layouts  3.68 us
    all_to_all x1, starting transfers between devices, local(): own_y = lax.all_to_all(send_y, axes, 0, 0, tiled=True).reshape(-1, width)  3.57 us
    dot_general x1, matrix products, local(): lax.dot_general(hidden, y_rows, (((0,), (0,)), ((), ())), preferred_eleme...  3.43 us
  transfers between devices with their start and end apart: 5, of which 4 were waited for; matrix products, arithmetic and copies ran while one was open for 1% of the time, Pallas kernels for 0%

profile of v1, /device:TPU:0, one launch (start us, length us, event | category | flops | bytes accessed | tf_op | source)
XLA Modules:
  0.0 148.8 jit_solution(1336465803373552490)
XLA Ops:
  6.5 0.0 reduce-scatter.2.cloned.1.call-start
  6.5 1.2 copy-done
  7.7 1.2 copy-done.1
  8.9 0.7 copy-done.2
  9.6 0.7 copy-done.3
  10.2 1.9 %shard_map.73 = (bf16[8,64,896]{2,1,0:T(8,128)(2,1)S(1)}, bf16[8,64,896]{2,1,0:T(8,128)(2,1)}) custom-call(s32[1,128]{1,0:T(1,128)S(1)} %bitcast.12, f32[1,128]{1,0:T(1,128)S(1)} %bitcast.13, bf16[128,3584]{1,0:T(8,128)(2,1)S(1)} %copy-done, bf16[128,3584]{1,0:T(8,128)(2,1)S(1)} %copy-done.1), custom_call_target="tpu_custom_call" | custom-call | tf_op jit(solution)/shard_map/pallas_call | solution.py:45
  12.1 30.9 %all_to_all.10 = bf16[8,64,896]{2,1,0:T(8,128)(2,1)S(1)} all-to-all(bf16[8,64,896]{2,1,0:T(8,128)(2,1)S(1)} %get-tuple-element.7), channel_id=1, replica_groups=mesh['groups'=2,'node'=2,'local'=4,'rep'=2] {'node','local'}, dimensions={0} | all-to-all | bytes 1835008 | tf_op jit(solution)/shard_map/all_to_all | solution.py:73
  43.0 0.0 collective-permute-start
  43.0 2.5 %collective-permute-done = bf16[512,896]{1,0:T(8,128)(2,1)S(1)} collective-permute-done((bf16[512,896]{1,0:T(8,128)(2,1)S(1)}, bf16[512,896]{1,0:T(8,128)(2,1)S(1)}, u32[]{:S(2)}, u32[]{:S(2)}) %collective-permute-start) | collective-permute-done | bytes 917536 | tf_op jit(solution)/shard_map/ppermute | solution.py:12
  45.4 0.0 copy-done.4
  45.5 3.7 %convolution_convert_fusion = bf16[1024,1024]{1,0:T(8,128)(2,1)} fusion(bf16[512,896]{1,0:T(8,128)(2,1)S(1)} %collective-permute-done, bf16[512,896]{1,0:T(8,128)(2,1)S(1)} %bitcast.17, bf16[896,512]{1,0:T(8,128)(2,1)S(1)} %bitcast.18, bf16[896,512]{1,0:T(8,128)(2,1)S(1)} %bitcast.19), kind=kOutput, calls=%fused_computation | convolution fusion | flops 1887436800 | bytes 5767168 | tf_op jit(solution)/shard_map/dot_general | solution.py:78
  49.1 0.0 reduce-scatter.2.cloned.1.call-update
  49.2 3.6 %all-to-all-start.1 = ((bf16[8,64,896]{2,1,0:T(8,128)(2,1)}), bf16[8,64,896]{2,1,0:T(8,128)(2,1)S(1)}, u32[]{:S(2)}, u32[]{:S(2)}) async-start(bf16[8,64,896]{2,1,0:T(8,128)(2,1)} %get-tuple-element.8), calls=%async_computation.2 | async-start | bytes 1835008 | tf_op jit(solution)/shard_map/all_to_all | solution.py:74
  52.7 0.0 copy-start.6
  52.7 0.0 all-gather.2.cloned.1.call-start
  52.8 53.8 %reduce-scatter.2.cloned.1.call-done = bf16[256,1024]{1,0:T(8,128)(2,1)} async-done(((bf16[1024,1024]{1,0:T(8,128)(2,1)}), bf16[256,1024]{1,0:T(8,128)(2,1)}) %reduce-scatter.2.cloned.1.call-update) | async-done | bytes 524304 | tf_op jit(solution)/shard_map/reduce_scatter | solution.py:79
  106.6 1.1 convert_element_type.19
  107.8 0.9 fusion.16
  108.6 0.0 all-gather.2.cloned.1.call-update
  108.7 0.0 all-to-all-done.1
  108.7 0.1 collective-permute-start.1
  108.8 2.5 %collective-permute-done.1 = bf16[512,896]{1,0:T(8,128)(2,1)S(1)} collective-permute-done((bf16[512,896]{1,0:T(8,128)(2,1)S(1)}, bf16[512,896]{1,0:T(8,128)(2,1)S(1)}, u32[]{:S(2)}, u32[]{:S(2)}) %collective-permute-start.1) | collective-permute-done | bytes 917536 | tf_op jit(solution)/shard_map/ppermute | solution.py:12
  111.2 27.4 %all-gather.2.cloned.1.call-done = bf16[1024,512]{1,0:T(8,128)(2,1)} async-done(((bf16[256,512]{1,0:T(8,128)(2,1)}), bf16[1024,512]{1,0:T(8,128)(2,1)}) %all-gather.2.cloned.1.call-update) | async-done | bytes 1048592 | tf_op jit(solution)/shard_map/all_gather | solution.py:82
  138.6 3.4 %fusion.13 = bf16[1,512,896]{2,1,0:T(8,128)(2,1)} fusion(bf16[1024,512]{1,0:T(8,128)(2,1)} %all-gather.2.cloned.1.call-done, bf16[512,896]{1,0:T(8,128)(2,1)S(1)} %collective-permute-done.1, bf16[512,896]{1,0:T(8,128)(2,1)S(1)} %bitcast.15, bf16[1,512,896]{2,1,0:T(8,128)(2,1)S(1)} %copy-done.6), kind=kOutput, calls=%fused_computation.13 | convolution fusion | flops 944570368 | bytes 4718592 | tf_op jit(solution)/shard_map/dot_general | solution.py:83
  (8 shorter events, 0.0 us)
Async XLA Ops:
  6.5 100.1 %reduce-scatter.2.cloned.1.call-start = ((), (), s32[]{:S(2)}) async-start(), calls=%async_computation.3 | async-start | bytes 2621440 | tf_op jit(solution)/shard_map/reduce_scatter | solution.py:79
  6.5 1.2 copy-start
  7.7 1.2 copy-start.1
  8.9 0.7 copy-start.2
  9.6 0.7 copy-start.3
  10.2 35.2 %copy-start.4 = (bf16[1,896,512]{2,1,0:T(8,128)(2,1)S(1)}, bf16[1,896,512]{2,1,0:T(8,128)(2,1)}, u32[]{:S(2)}) copy-start(bf16[1,896,512]{2,1,0:T(8,128)(2,1)} %param.12) | copy-start | bytes 2752516
  10.2 35.2 %copy-start.5 = (bf16[1,896,512]{2,1,0:T(8,128)(2,1)S(1)}, bf16[1,896,512]{2,1,0:T(8,128)(2,1)}, u32[]{:S(2)}) copy-start(bf16[1,896,512]{2,1,0:T(8,128)(2,1)} %param.11) | copy-start | bytes 2752516
  43.0 2.5 %collective-permute-start = (bf16[512,896]{1,0:T(8,128)(2,1)S(1)}, bf16[512,896]{1,0:T(8,128)(2,1)S(1)}, u32[]{:S(2)}, u32[]{:S(2)}) collective-permute-start(bf16[512,896]{1,0:T(8,128)(2,1)S(1)} %bitcast.16), channel_id=1, source_target_pairs={{0,1},{1,0},{2,3},{3,2},{4,5},{5,4},{6,7},{7,6},{8,9},{9,8},{10,11... | collective-permute-start | bytes 2752520 | tf_op jit(solution)/shard_map/ppermute | solution.py:12
  49.2 59.5 %all-to-all-start.1 = ((bf16[8,64,896]{2,1,0:T(8,128)(2,1)}), bf16[8,64,896]{2,1,0:T(8,128)(2,1)S(1)}, u32[]{:S(2)}, u32[]{:S(2)}) async-start(bf16[8,64,896]{2,1,0:T(8,128)(2,1)} %get-tuple-element.8), calls=%async_computation.2 | async-start | bytes 1835008 | tf_op jit(solution)/shard_map/all_to_all | solution.py:74
  52.7 85.8 %copy-start.6 = (bf16[1,512,896]{2,1,0:T(8,128)(2,1)S(1)}, bf16[1,512,896]{2,1,0:T(8,128)(2,1)}, u32[]{:S(2)}) copy-start(bf16[1,512,896]{2,1,0:T(8,128)(2,1)} %param.13) | copy-start | bytes 2752516
  52.7 85.8 %all-gather.2.cloned.1.call-start = ((), (), s32[]{:S(2)}) async-start(), calls=%async_computation.4 | async-start | bytes 1310720 | tf_op jit(solution)/shard_map/all_gather | solution.py:82
  108.7 2.5 %collective-permute-start.1 = (bf16[512,896]{1,0:T(8,128)(2,1)S(1)}, bf16[512,896]{1,0:T(8,128)(2,1)S(1)}, u32[]{:S(2)}, u32[]{:S(2)}) collective-permute-start(bf16[512,896]{1,0:T(8,128)(2,1)S(1)} %bitcast.14), channel_id=1, source_target_pairs={{0,1},{1,0},{2,3},{3,2},{4,5},{5,4},{6,7},{7,6},{8,9},{9,8},{10,11... | collective-permute-start | bytes 2752520 | tf_op jit(solution)/shard_map/ppermute | solution.py:12
Sparse Core Ops, SparseCore 0:
  49.3 57.2 reduce-scatter.1
  108.8 29.7 all-gather.1

commit v2 on v1

v2 whole, which is shorter than its diff:
```python
import functools

import jax
import jax.numpy as jnp
from jax import lax
from jax.experimental import pallas as pl
from jax.experimental.pallas import tpu as pltpu
from jax.sharding import Mesh
from jax.sharding import PartitionSpec as P

KERNEL = pltpu.CompilerParams(vmem_limit_bytes=40 << 20)
SMEM = pl.BlockSpec(memory_space=pltpu.SMEM)
WHOLE = pl.BlockSpec()


def swapped(value, axis, distance=1):
    pairs = [(s, s ^ distance) for s in range(lax.axis_size(axis))]
    return lax.ppermute(value, axis, pairs)


def dispatch_kernel(nodes, side, capacity, half_ref, ids_ref, gate_ref, x_ref, c_ref, sx_ref, sy_ref):
    pairs = ids_ref.shape[1]
    width = sx_ref.shape[-1]
    half = half_ref[0]
    ids = ids_ref[...]
    row = lax.broadcasted_iota(jnp.int32, (pairs, pairs), 0)
    col = lax.broadcasted_iota(jnp.int32, (pairs, pairs), 1)
    earlier = (row < col).astype(jnp.bfloat16)
    slots = lax.broadcasted_iota(jnp.int32, (capacity, pairs), 0)
    for node in range(nodes):
        named = ids == node
        rank = jnp.dot(
            jnp.broadcast_to(jnp.where(named, 1.0, 0.0), (8, pairs)).astype(jnp.bfloat16),
            earlier,
            preferred_element_type=jnp.float32,
        )[:1].astype(jnp.int32)
        pick = jnp.where((rank == slots) & named, 1.0, 0.0)
        gate = jnp.sum(pick * gate_ref[...], axis=1, keepdims=True)
        pick = pick.astype(jnp.bfloat16)
        for hi in range(2):
            for lo in range(side):
                block = hi * side + lo
                cols = slice(block * width, (block + 1) * width)
                x_rows = jnp.dot(pick, x_ref[:, cols], preferred_element_type=jnp.float32)
                c_rows = jnp.dot(pick, c_ref[:, cols], preferred_element_type=jnp.float32)
                sx_ref[node * side + lo, half ^ hi] = x_rows.astype(jnp.bfloat16)
                sy_ref[(hi * nodes + node) * side + lo] = (gate * c_rows).astype(jnp.bfloat16)


def dispatch(half, ids, gates, tokens, cotangent, nodes, side, capacity):
    width = tokens.shape[1] // (2 * side)
    return pl.pallas_call(
        functools.partial(dispatch_kernel, nodes, side, capacity),
        out_shape=(
            jax.ShapeDtypeStruct((nodes * side, 2, capacity, width), jnp.bfloat16),
            jax.ShapeDtypeStruct((2 * nodes * side, capacity, width), jnp.bfloat16),
        ),
        in_specs=[SMEM] + [WHOLE] * 4,
        out_specs=(WHOLE, WHOLE),
        compiler_params=KERNEL,
    )(half, ids, gates, tokens, cotangent)


def row_chunk(own_ref, other_ref, index, quarter, side):
    per_core = side // 2
    count = own_ref.shape[0] // per_core
    place = index % per_core
    own = own_ref[pl.ds(place * count, count), quarter]
    other = other_ref[pl.ds(place * count, count), quarter]
    rows = jnp.where(index < per_core, own, other)
    return rows.reshape(-1, rows.shape[-1])


def first_kernel(side, lo_ref, own_ref, other_ref, gate_ref, up_ref, acc_ref):
    hidden = gate_ref.shape[-1]
    for step in range(side):
        x = row_chunk(own_ref, other_ref, lo_ref[0] ^ step, 0, side)
        acc_ref[step, :, :hidden] = jnp.dot(x, gate_ref[...], preferred_element_type=jnp.float32)
        acc_ref[step, :, hidden:] = jnp.dot(x, up_ref[...], preferred_element_type=jnp.float32)


def second_kernel(side, cuts, lo_ref, group_ref, own_ref, other_ref, acc_ref, *refs):
    parts = len(cuts) - 1
    mine_refs, theirs_refs = refs[:parts], refs[parts : 2 * parts]
    keep_ref, send_refs = refs[2 * parts], refs[2 * parts + 1 :]
    hidden = mine_refs[0].shape[-1]
    first = group_ref[0] == 0
    for step in reversed(range(side)):
        x = row_chunk(own_ref, other_ref, lo_ref[0] ^ step, 1, side)
        mine = theirs = 0.0
        for part in range(parts):
            piece = x[:, cuts[part] : cuts[part + 1]]
            mine += jnp.dot(piece, mine_refs[part][...], preferred_element_type=jnp.float32)
            theirs += jnp.dot(piece, theirs_refs[part][...], preferred_element_type=jnp.float32)
        gate = acc_ref[step, :, :hidden] + jnp.where(first, mine, theirs)
        up = acc_ref[step, :, hidden:] + jnp.where(first, theirs, mine)
        target = send_refs[step - 1] if step else keep_ref
        target[:, :hidden] = gate.astype(target.dtype)
        target[:, hidden:] = up.astype(target.dtype)


def partial_first(lo, own, other, gate, up, side):
    chunk = 2 * own.shape[0] * own.shape[2] // side
    return pl.pallas_call(
        functools.partial(first_kernel, side),
        out_shape=jax.ShapeDtypeStruct((side, chunk, 2 * gate.shape[1]), jnp.float32),
        in_specs=[SMEM] + [WHOLE] * 4,
        out_specs=WHOLE,
        compiler_params=KERNEL,
    )(lo, own, other, gate, up)


def partial_second(lo, group, own, other, acc, mine, theirs, cuts, side):
    _, chunk, width = acc.shape
    keep = jax.ShapeDtypeStruct((chunk, width), jnp.float32)
    send = jax.ShapeDtypeStruct((chunk, width), jnp.bfloat16)
    return pl.pallas_call(
        functools.partial(second_kernel, side, cuts),
        out_shape=(keep,) + (send,) * (side - 1),
        in_specs=[SMEM] * 2 + [WHOLE] * (3 + 2 * len(mine)),
        out_specs=(WHOLE,) * side,
        compiler_params=KERNEL,
    )(lo, group, own, other, acc, *mine, *theirs)


def local(tokens, cotangent, expert_ids, gate_values, w_gate, w_up, feedback):
    token_count = tokens.shape[0]
    top_count = expert_ids.shape[1]
    nodes, side = lax.axis_size("node"), lax.axis_size("lo")
    capacity = max(2, token_count * top_count // nodes)
    width = tokens.shape[1] // (2 * side)
    half, lo, group = (lax.axis_index(a).astype(jnp.int32)[None] for a in ("hi", "lo", "groups"))
    gate_own, up_own = w_gate[0], w_up[0]

    cuts = tuple(range(0, width, 256)) + (width,)
    mine, theirs = [], []
    for start, end in zip(cuts, cuts[1:]):
        piece = jnp.where(group[0] == 0, gate_own[start:end], up_own[start:end])
        mine.append(swapped(piece, "hi"))
    theirs = [swapped(piece, "groups") for piece in mine]

    if top_count > 1:
        tokens = jnp.repeat(tokens, top_count, axis=0)
        cotangent = jnp.repeat(cotangent, top_count, axis=0)
    send_x, send_y = dispatch(
        half,
        expert_ids.reshape(1, -1),
        gate_values.reshape(1, -1),
        tokens,
        cotangent,
        nodes,
        side,
        capacity,
    )
    own_x = lax.all_to_all(send_x, ("node", "lo"), 0, 0, tiled=True)
    other_x = swapped(own_x, "rep")
    acc = partial_first(lo, own_x, other_x, gate_own, up_own, side)

    send_y, _ = lax.optimization_barrier((send_y, mine[-1]))
    own_y = lax.all_to_all(send_y, ("hi", "node", "lo"), 0, 0, tiled=True)
    other_y = swapped(own_y, "rep")

    keep, *sends = partial_second(lo, group, own_x, other_x, acc, mine, theirs, cuts, side)
    pre = keep
    for step, send in enumerate(sends, 1):
        pre = pre + swapped(send, "lo", step).astype(jnp.float32)
    pre_gate, pre_up = jnp.split(pre, 2, axis=1)
    hidden = (jax.nn.silu(pre_gate) * pre_up).astype(jnp.bfloat16)
    hidden = lax.all_gather(hidden, ("hi", "lo"), axis=0, tiled=True)
    y_rows = jnp.stack([own_y.reshape(2, -1, width), other_y.reshape(2, -1, width)], axis=1)
    grad = lax.dot_general(
        hidden,
        y_rows.reshape(-1, width),
        (((0,), (0,)), ((), ())),
        preferred_element_type=jnp.float32,
    )
    return (grad + feedback[0].astype(jnp.float32)).astype(jnp.bfloat16)[None]


def solution(mesh):
    names = ("groups", "node", "hi", "lo", "rep")
    groups, nodes, locals_, reps = (mesh.shape[a] for a in ("groups", "node", "local", "rep"))
    split = Mesh(mesh.devices.reshape(groups, nodes, 2, locals_ // 2, reps), names)
    rows = P(names, None)
    weights = P("node", ("hi", "lo"), "rep")
    return jax.shard_map(
        local,
        mesh=split,
        in_specs=(rows, rows, rows, rows, weights, weights, P("node", "rep", ("hi", "lo"))),
        out_specs=P(("groups", "node"), "rep", ("hi", "lo")),
        check_vma=False,
    )
```

time: 149 us -> 146 us (0.980)
  starting transfers between devices: 3.68 us -> 18.4 us
  blocking collectives: 30.9 us -> 17.8 us
  waiting for transfers between devices: 86.1 us -> 79.3 us
  Pallas kernels: 1.91 us -> 6.21 us
  matrix products: 7.11 us -> 3.43 us
    reduce_scatter x1 -> x0, waiting for transfers between devices: 53.8 us -> none  [local(): lax.psum_scatter(partial, 'local', scatter_dimension=0, tiled=True)]
    ppermute x2 -> x11, waiting for transfers between devices: 4.93 us -> 56.3 us  [swapped(): return lax.ppermute(value, axis, pairs)]
    ppermute x2 -> x11, starting transfers between devices: 0.07 us -> 14.1 us  [swapped(): return lax.ppermute(value, axis, pairs)]
    all_to_all x1, blocking collectives: 30.9 us -> 17.8 us  [local(): own_x = lax.all_to_all(send_x, ('node', 'lo'), 0, 0, tiled=True)]
    all_gather x1, waiting for transfers between devices: 27.4 us -> 22.9 us  [local(): hidden = lax.all_gather(hidden, ('hi', 'lo'), axis=0, tiled=True)]
    pallas_call x1 -> x3, Pallas kernels: 1.91 us -> 6.21 us  [the longest x1 2.82 us: partial_second(): pl.pallas_call(functools.partial(second_kernel, side, cuts), out_shape=(k...]
    dot_general x2 -> x1, matrix products: 7.11 us -> 3.43 us  [local(): lax.dot_general(hidden, y_rows.reshape(-1, width), (((0,), (0,)), ((), ()...]
    unnamed x14 -> x16, local copies, waits for them, and re-layouts: 3.68 us -> 4.59 us
  transfers between devices with their start and end apart: 5 -> 13, of which waited for: 4 -> 7; matrix products, arithmetic and copies ran while one was open for 1% -> 2% of each run, Pallas kernels for 0% -> 4%
where the time goes in v2:
time: 146 us
  waiting for transfers between devices  79.3 us (54%)
  starting transfers between devices  18.4 us (13%)
  blocking collectives  17.8 us (12%)
  between operations  13.5 us (9%)
  Pallas kernels  6.21 us (4%)
  local copies, waits for them, and re-layouts  4.59 us (3%)
  matrix products  3.43 us (2%)
  other arithmetic  2.54 us (2%)
    ppermute x11, waiting for transfers between devices, swapped(): return lax.ppermute(value, axis, pairs)  56.3 us
    all_gather x1, waiting for transfers between devices, local(): hidden = lax.all_gather(hidden, ('hi', 'lo'), axis=0, tiled=True)  22.9 us
    all_to_all x1, blocking collectives, local(): own_x = lax.all_to_all(send_x, ('node', 'lo'), 0, 0, tiled=True)  17.8 us
    ppermute x11, starting transfers between devices, swapped(): return lax.ppermute(value, axis, pairs)  14.1 us
    unnamed x16, local copies, waits for them, and re-layouts  4.59 us
    all_to_all x1, starting transfers between devices, local(): own_y = lax.all_to_all(send_y, ('hi', 'node', 'lo'), 0, 0, tiled=True)  4.22 us
    dot_general x1, matrix products, local(): lax.dot_general(hidden, y_rows.reshape(-1, width), (((0,), (0,)), ((), ()...  3.43 us
  transfers between devices with their start and end apart: 13, of which 7 were waited for; matrix products, arithmetic and copies ran while one was open for 2% of the time, Pallas kernels for 4%

profile of v2, /device:TPU:0, one launch (start us, length us, event | category | flops | bytes accessed | tf_op | source)
XLA Modules:
  0.0 145.8 jit_solution(5865853570522230926)
XLA Ops:
  6.5 1.2 copy-done.3
  7.7 1.2 copy-done.4
  10.2 1.0 shard_map.73
  11.2 0.9 copy-done.2
  12.1 17.8 %all_to_all.10.own_ref = bf16[4,2,64,896]{3,2,1,0:T(8,128)(2,1)S(1)} all-to-all(bf16[4,2,64,896]{3,2,1,0:T(8,128)(2,1)S(1)} %get-tuple-element.10), channel_id=1, replica_groups=mesh['groups'=2,'node'=2,'hi'=2,'lo'=2,'rep'=2] {'node','lo'}, dimensions={0} | all-to-all | bytes 1835008 | tf_op jit(solution)/shard_map/all_to_all | solution.py:155
  30.0 2.7 %collective-permute-start.1 = (bf16[256,512]{1,0:T(8,128)(2,1)S(1)}, bf16[256,512]{1,0:T(8,128)(2,1)S(1)}, u32[]{:S(2)}, u32[]{:S(2)}) collective-permute-start(bf16[256,512]{1,0:T(8,128)(2,1)S(1)} %get-tuple-element.17), channel_id=1, source_target_pairs={{0,4},{4,0},{1,5},{5,1},{2,6},{6,2},{3,7},{7,3},{8,12},{12,8},{9,1... | collective-permute-start | bytes 786440 | tf_op jit(solution)/shard_map/ppermute | solution.py:18
  33.0 2.6 %collective-permute-start.3 = (bf16[256,512]{1,0:T(8,128)(2,1)S(1)}, bf16[256,512]{1,0:T(8,128)(2,1)S(1)}, u32[]{:S(2)}, u32[]{:S(2)}) collective-permute-start(bf16[256,512]{1,0:T(8,128)(2,1)S(1)} %get-tuple-element.15), channel_id=1, source_target_pairs={{0,4},{4,0},{1,5},{5,1},{2,6},{6,2},{3,7},{7,3},{8,12},{12,8},{9,1... | collective-permute-start | bytes 786440 | tf_op jit(solution)/shard_map/ppermute | solution.py:18
  36.0 23.7 %collective-permute-done.1.refs_0_ = bf16[256,512]{1,0:T(8,128)(2,1)S(1)} collective-permute-done((bf16[256,512]{1,0:T(8,128)(2,1)S(1)}, bf16[256,512]{1,0:T(8,128)(2,1)S(1)}, u32[]{:S(2)}, u32[]{:S(2)}) %collective-permute-start.1) | collective-permute-done | bytes 262176 | tf_op jit(solution)/shard_map/ppermute | solution.py:18
  59.7 1.5 %collective-permute-start.5 = (bf16[256,512]{1,0:T(8,128)(2,1)S(1)}, bf16[256,512]{1,0:T(8,128)(2,1)}, u32[]{:S(2)}, u32[]{:S(2)}) collective-permute-start(bf16[256,512]{1,0:T(8,128)(2,1)S(1)} %collective-permute-done.1.refs_0_), channel_id=1, source_target_pairs={{0,16},{16,0},{1,17},{17,1},{2,18},{18,2},{3,19},{19,3},{4,20},{20... | collective-permute-start | bytes 786440 | tf_op jit(solution)/shard_map/ppermute | solution.py:18
  61.2 4.1 %collective-permute-done.2.refs_1_ = bf16[256,512]{1,0:T(8,128)(2,1)S(1)} collective-permute-done((bf16[256,512]{1,0:T(8,128)(2,1)S(1)}, bf16[256,512]{1,0:T(8,128)(2,1)S(1)}, u32[]{:S(2)}, u32[]{:S(2)}) %collective-permute-start.2) | collective-permute-done | bytes 262176 | tf_op jit(solution)/shard_map/ppermute | solution.py:18
  65.3 1.5 %collective-permute-start.6 = (bf16[256,512]{1,0:T(8,128)(2,1)S(1)}, bf16[256,512]{1,0:T(8,128)(2,1)}, u32[]{:S(2)}, u32[]{:S(2)}) collective-permute-start(bf16[256,512]{1,0:T(8,128)(2,1)S(1)} %collective-permute-done.2.refs_1_), channel_id=1, source_target_pairs={{0,16},{16,0},{1,17},{17,1},{2,18},{18,2},{3,19},{19,3},{4,20},{20... | collective-permute-start | bytes 786440 | tf_op jit(solution)/shard_map/ppermute | solution.py:18
  66.8 4.1 %collective-permute-done.3.refs_2_ = bf16[256,512]{1,0:T(8,128)(2,1)S(1)} collective-permute-done((bf16[256,512]{1,0:T(8,128)(2,1)S(1)}, bf16[256,512]{1,0:T(8,128)(2,1)S(1)}, u32[]{:S(2)}, u32[]{:S(2)}) %collective-permute-start.3) | collective-permute-done | bytes 262176 | tf_op jit(solution)/shard_map/ppermute | solution.py:18
  70.9 1.5 %collective-permute-start.7 = (bf16[256,512]{1,0:T(8,128)(2,1)S(1)}, bf16[256,512]{1,0:T(8,128)(2,1)}, u32[]{:S(2)}, u32[]{:S(2)}) collective-permute-start(bf16[256,512]{1,0:T(8,128)(2,1)S(1)} %collective-permute-done.3.refs_2_), channel_id=1, source_target_pairs={{0,16},{16,0},{1,17},{17,1},{2,18},{18,2},{3,19},{19,3},{4,20},{20... | collective-permute-start | bytes 786440 | tf_op jit(solution)/shard_map/ppermute | solution.py:18
  72.4 1.0 collective-permute-done.4.refs_3_
  73.5 1.5 %collective-permute-start.8 = (bf16[128,512]{1,0:T(8,128)(2,1)}, bf16[128,512]{1,0:T(8,128)(2,1)}, u32[]{:S(2)}, u32[]{:S(2)}) collective-permute-start(bf16[128,512]{1,0:T(8,128)(2,1)} %collective-permute-done.4.refs_3_), channel_id=1, source_target_pairs={{0,16},{16,0},{1,17},{17,1},{2,18},{18,2},{3,19},{19,3},{4,20},{20... | collective-permute-start | bytes 393224 | tf_op jit(solution)/shard_map/ppermute | solution.py:18
  75.0 4.2 %all-to-all-start.1 = ((bf16[8,64,896]{2,1,0:T(8,128)(2,1)}), bf16[8,64,896]{2,1,0:T(8,128)(2,1)}, u32[]{:S(2)}, u32[]{:S(2)}) async-start(bf16[8,64,896]{2,1,0:T(8,128)(2,1)} %copy-done.2), calls=%async_computation.1 | async-start | bytes 1835008 | tf_op jit(solution)/shard_map/all_to_all | solution.py:160
  79.3 2.4 %shard_map.74.acc_ref = f32[2,256,1024]{2,1,0:T(8,128)S(1)} custom-call(s32[1]{0:T(128)} %bitcast.lo_ref, bf16[4,2,64,896]{3,2,1,0:T(8,128)(2,1)S(1)} %all_to_all.10.own_ref, bf16[4,2,64,896]{3,2,1,0:T(8,128)(2,1)} %collective-permute-done.other_ref, bf16[896,512]{1,0:T(8,128)(2,1)S(1)} %bitcast.29, bf16[896,512]{1,0:T(8,128)(2,1)S(1)} %bitcast.30), custom_call_target="tpu_custom_call" | custom-call | tf_op jit(solution)/shard_map/pallas_call | solution.py:104
  81.7 2.8 %shard_map.75 = (f32[256,1024]{1,0:T(8,128)S(1)}, bf16[256,1024]{1,0:T(8,128)(2,1)S(1)}) custom-call(s32[1]{0:T(128)} %bitcast.lo_ref, s32[1]{0:T(128)} %bitcast.1.group_ref, bf16[4,2,64,896]{3,2,1,0:T(8,128)(2,1)S(1)} %all_to_all.10.own_ref, bf16[4,2,64,896]{3,2,1,0:T(8,128)(2,1)} %collective-permute-done.other_ref, f32[2,256,1024]{2,1,0:T(8,128)S(1)} %shard_map.74.acc_ref, ...), custom_call_target="tpu_custom_call" | custom-call | tf_op jit(solution)/shard_map/pallas_call | solution.py:117
  84.6 2.0 %collective-permute-start.9 = (bf16[256,1024]{1,0:T(8,128)(2,1)S(1)}, bf16[256,1024]{1,0:T(8,128)(2,1)S(1)}, u32[]{:S(2)}, u32[]{:S(2)}) collective-permute-start(bf16[256,1024]{1,0:T(8,128)(2,1)S(1)} %get-tuple-element.12), channel_id=1, source_target_pairs={{0,2},{2,0},{1,3},{3,1},{4,6},{6,4},{5,7},{7,5},{8,10},{10,8},{9,1... | collective-permute-start | bytes 1572872 | tf_op jit(solution)/shard_map/ppermute | solution.py:18
  86.6 20.7 %collective-permute-done.9 = bf16[256,1024]{1,0:T(8,128)(2,1)S(1)} collective-permute-done((bf16[256,1024]{1,0:T(8,128)(2,1)S(1)}, bf16[256,1024]{1,0:T(8,128)(2,1)S(1)}, u32[]{:S(2)}, u32[]{:S(2)}) %collective-permute-start.9) | collective-permute-done | bytes 524320 | tf_op jit(solution)/shard_map/ppermute | solution.py:18
  108.4 2.7 %collective-permute-done.10 = bf16[8,64,896]{2,1,0:T(8,128)(2,1)S(1)} collective-permute-done((bf16[8,64,896]{2,1,0:T(8,128)(2,1)}, bf16[8,64,896]{2,1,0:T(8,128)(2,1)S(1)}, u32[]{:S(2)}, u32[]{:S(2)}) %collective-permute-start.10) | collective-permute-done | bytes 917536 | tf_op jit(solution)/shard_map/ppermute | solution.py:18
  111.1 1.4 pad_maximum_fusion
  112.5 22.9 %all-gather.2.cloned.1.call-done = bf16[1024,512]{1,0:T(8,128)(2,1)} async-done(((bf16[256,512]{1,0:T(8,128)(2,1)}), bf16[1024,512]{1,0:T(8,128)(2,1)}) %all-gather.2.cloned.1.call-update) | async-done | bytes 1048592 | tf_op jit(solution)/shard_map/all_gather | solution.py:169
  135.5 3.4 %fusion.1 = bf16[1,512,896]{2,1,0:T(8,128)(2,1)} fusion(bf16[1024,512]{1,0:T(8,128)(2,1)} %all-gather.2.cloned.1.call-done, bf16[1024,896]{1,0:T(8,128)(2,1)S(1)} %bitcast.33, bf16[1,512,896]{2,1,0:T(8,128)(2,1)S(1)} %copy-done.7), kind=kOutput, calls=%fused_computation.3 | convolution fusion | flops 940900352 | bytes 4718592 | tf_op jit(solution)/shard_map/dot_general | solution.py:171
  (29 shorter events, 3.3 us)
Async XLA Ops:
  6.5 1.2 copy-start.3
  7.7 1.2 copy-start.4
  8.9 0.7 copy-start.5
  9.5 0.7 copy-start.6
  10.2 19.7 %copy-start = (bf16[1,896,512]{2,1,0:T(8,128)(2,1)S(1)}, bf16[1,896,512]{2,1,0:T(8,128)(2,1)}, u32[]{:S(2)}) copy-start(bf16[1,896,512]{2,1,0:T(8,128)(2,1)} %param.11) | copy-start | bytes 2752516
  10.2 19.7 %copy-start.1 = (bf16[1,896,512]{2,1,0:T(8,128)(2,1)S(1)}, bf16[1,896,512]{2,1,0:T(8,128)(2,1)}, u32[]{:S(2)}) copy-start(bf16[1,896,512]{2,1,0:T(8,128)(2,1)} %param.12) | copy-start | bytes 2752516
  11.2 0.9 copy-start.2
  29.9 49.4 %collective-permute-start = (bf16[4,2,64,896]{3,2,1,0:T(8,128)(2,1)S(1)}, bf16[4,2,64,896]{3,2,1,0:T(8,128)(2,1)}, u32[]{:S(2)}, u32[]{:S(2)}) collective-permute-start(bf16[4,2,64,896]{3,2,1,0:T(8,128)(2,1)S(1)} %all_to_all.10.own_ref), channel_id=1, source_target_pairs={{0,1},{1,0},{2,3},{3,2},{4,5},{5,4},{6,7},{7,6},{8,9},{9,8},{10,11... | collective-permute-start | bytes 2752520 | tf_op jit(solution)/shard_map/ppermute | solution.py:18
  30.0 29.7 %collective-permute-start.1 = (bf16[256,512]{1,0:T(8,128)(2,1)S(1)}, bf16[256,512]{1,0:T(8,128)(2,1)S(1)}, u32[]{:S(2)}, u32[]{:S(2)}) collective-permute-start(bf16[256,512]{1,0:T(8,128)(2,1)S(1)} %get-tuple-element.17), channel_id=1, source_target_pairs={{0,4},{4,0},{1,5},{5,1},{2,6},{6,2},{3,7},{7,3},{8,12},{12,8},{9,1... | collective-permute-start | bytes 786440 | tf_op jit(solution)/shard_map/ppermute | solution.py:18
  32.6 32.7 %collective-permute-start.2 = (bf16[256,512]{1,0:T(8,128)(2,1)S(1)}, bf16[256,512]{1,0:T(8,128)(2,1)S(1)}, u32[]{:S(2)}, u32[]{:S(2)}) collective-permute-start(bf16[256,512]{1,0:T(8,128)(2,1)S(1)} %get-tuple-element.16), channel_id=1, source_target_pairs={{0,4},{4,0},{1,5},{5,1},{2,6},{6,2},{3,7},{7,3},{8,12},{12,8},{9,1... | collective-permute-start | bytes 786440 | tf_op jit(solution)/shard_map/ppermute | solution.py:18
  33.0 38.0 %collective-permute-start.3 = (bf16[256,512]{1,0:T(8,128)(2,1)S(1)}, bf16[256,512]{1,0:T(8,128)(2,1)S(1)}, u32[]{:S(2)}, u32[]{:S(2)}) collective-permute-start(bf16[256,512]{1,0:T(8,128)(2,1)S(1)} %get-tuple-element.15), channel_id=1, source_target_pairs={{0,4},{4,0},{1,5},{5,1},{2,6},{6,2},{3,7},{7,3},{8,12},{12,8},{9,1... | collective-permute-start | bytes 786440 | tf_op jit(solution)/shard_map/ppermute | solution.py:18
  35.6 37.9 %collective-permute-start.4 = (bf16[128,512]{1,0:T(8,128)(2,1)S(1)}, bf16[128,512]{1,0:T(8,128)(2,1)}, u32[]{:S(2)}, u32[]{:S(2)}) collective-permute-start(bf16[128,512]{1,0:T(8,128)(2,1)S(1)} %select_bitcast_fusion.3), channel_id=1, source_target_pairs={{0,4},{4,0},{1,5},{5,1},{2,6},{6,2},{3,7},{7,3},{8,12},{12,8},{9,1... | collective-permute-start | bytes 393224 | tf_op jit(solution)/shard_map/ppermute | solution.py:18
  59.7 22.0 %collective-permute-start.5 = (bf16[256,512]{1,0:T(8,128)(2,1)S(1)}, bf16[256,512]{1,0:T(8,128)(2,1)}, u32[]{:S(2)}, u32[]{:S(2)}) collective-permute-start(bf16[256,512]{1,0:T(8,128)(2,1)S(1)} %collective-permute-done.1.refs_0_), channel_id=1, source_target_pairs={{0,16},{16,0},{1,17},{17,1},{2,18},{18,2},{3,19},{19,3},{4,20},{20... | collective-permute-start | bytes 786440 | tf_op jit(solution)/shard_map/ppermute | solution.py:18
  65.3 16.4 %collective-permute-start.6 = (bf16[256,512]{1,0:T(8,128)(2,1)S(1)}, bf16[256,512]{1,0:T(8,128)(2,1)}, u32[]{:S(2)}, u32[]{:S(2)}) collective-permute-start(bf16[256,512]{1,0:T(8,128)(2,1)S(1)} %collective-permute-done.2.refs_1_), channel_id=1, source_target_pairs={{0,16},{16,0},{1,17},{17,1},{2,18},{18,2},{3,19},{19,3},{4,20},{20... | collective-permute-start | bytes 786440 | tf_op jit(solution)/shard_map/ppermute | solution.py:18
  70.9 10.8 %collective-permute-start.7 = (bf16[256,512]{1,0:T(8,128)(2,1)S(1)}, bf16[256,512]{1,0:T(8,128)(2,1)}, u32[]{:S(2)}, u32[]{:S(2)}) collective-permute-start(bf16[256,512]{1,0:T(8,128)(2,1)S(1)} %collective-permute-done.3.refs_2_), channel_id=1, source_target_pairs={{0,16},{16,0},{1,17},{17,1},{2,18},{18,2},{3,19},{19,3},{4,20},{20... | collective-permute-start | bytes 786440 | tf_op jit(solution)/shard_map/ppermute | solution.py:18
  73.5 8.2 %collective-permute-start.8 = (bf16[128,512]{1,0:T(8,128)(2,1)}, bf16[128,512]{1,0:T(8,128)(2,1)}, u32[]{:S(2)}, u32[]{:S(2)}) collective-permute-start(bf16[128,512]{1,0:T(8,128)(2,1)} %collective-permute-done.4.refs_3_), channel_id=1, source_target_pairs={{0,16},{16,0},{1,17},{17,1},{2,18},{18,2},{3,19},{19,3},{4,20},{20... | collective-permute-start | bytes 393224 | tf_op jit(solution)/shard_map/ppermute | solution.py:18
  75.0 33.4 %all-to-all-start.1 = ((bf16[8,64,896]{2,1,0:T(8,128)(2,1)}), bf16[8,64,896]{2,1,0:T(8,128)(2,1)}, u32[]{:S(2)}, u32[]{:S(2)}) async-start(bf16[8,64,896]{2,1,0:T(8,128)(2,1)} %copy-done.2), calls=%async_computation.1 | async-start | bytes 1835008 | tf_op jit(solution)/shard_map/all_to_all | solution.py:160
  79.2 56.3 %all-gather.2.cloned.1.call-start = ((), (), s32[]{:S(2)}) async-start(), calls=%async_computation.2 | async-start | bytes 1310720 | tf_op jit(solution)/shard_map/all_gather | solution.py:169
  84.6 22.7 %collective-permute-start.9 = (bf16[256,1024]{1,0:T(8,128)(2,1)S(1)}, bf16[256,1024]{1,0:T(8,128)(2,1)S(1)}, u32[]{:S(2)}, u32[]{:S(2)}) collective-permute-start(bf16[256,1024]{1,0:T(8,128)(2,1)S(1)} %get-tuple-element.12), channel_id=1, source_target_pairs={{0,2},{2,0},{1,3},{3,1},{4,6},{6,4},{5,7},{7,5},{8,10},{10,8},{9,1... | collective-permute-start | bytes 1572872 | tf_op jit(solution)/shard_map/ppermute | solution.py:18
  108.3 2.7 %collective-permute-start.10 = (bf16[8,64,896]{2,1,0:T(8,128)(2,1)}, bf16[8,64,896]{2,1,0:T(8,128)(2,1)S(1)}, u32[]{:S(2)}, u32[]{:S(2)}) collective-permute-start(bf16[8,64,896]{2,1,0:T(8,128)(2,1)} %all-to-all-done.1), channel_id=1, source_target_pairs={{0,1},{1,0},{2,3},{3,2},{4,5},{5,4},{6,7},{7,6},{8,9},{9,8},{10,11... | collective-permute-start | bytes 2752520 | tf_op jit(solution)/shard_map/ppermute | solution.py:18
  111.1 24.4 %copy-start.7 = (bf16[1,512,896]{2,1,0:T(8,128)(2,1)S(1)}, bf16[1,512,896]{2,1,0:T(8,128)(2,1)}, u32[]{:S(2)}) copy-start(bf16[1,512,896]{2,1,0:T(8,128)(2,1)} %param.13) | copy-start | bytes 2752516
Sparse Core Ops, SparseCore 0:
  108.5 26.9 all-gather.1

commit v3 on v2

v3 whole, which is shorter than its diff:
```python
import functools

import jax
import jax.numpy as jnp
from jax import lax
from jax.experimental import pallas as pl
from jax.experimental.pallas import tpu as pltpu
from jax.sharding import Mesh
from jax.sharding import PartitionSpec as P

KERNEL = pltpu.CompilerParams(vmem_limit_bytes=40 << 20)
SMEM = pl.BlockSpec(memory_space=pltpu.SMEM)
WHOLE = pl.BlockSpec()
F32 = jnp.float32
BF16 = jnp.bfloat16


def cost(flops, *arrays):
    size = sum(a.size * a.dtype.itemsize for a in arrays)
    return pl.CostEstimate(flops=flops, bytes_accessed=size, transcendentals=0)


def swapped(value, axis, distance=1):
    pairs = [(s, s ^ distance) for s in range(lax.axis_size(axis))]
    return lax.ppermute(value, axis, pairs)


def dispatch_kernel(nodes, side, capacity, half_ref, ids_ref, gate_ref, x_ref, c_ref, sx_ref, sy_ref):
    pairs = ids_ref.shape[1]
    width = sx_ref.shape[-1]
    half = half_ref[0]
    ids = ids_ref[...]
    row = lax.broadcasted_iota(jnp.int32, (pairs, pairs), 0)
    col = lax.broadcasted_iota(jnp.int32, (pairs, pairs), 1)
    earlier = (row < col).astype(BF16)
    slots = lax.broadcasted_iota(jnp.int32, (capacity, pairs), 0)
    for node in range(nodes):
        named = ids == node
        rank = jnp.dot(
            jnp.broadcast_to(jnp.where(named, 1.0, 0.0), (8, pairs)).astype(BF16),
            earlier,
            preferred_element_type=F32,
        )[:1].astype(jnp.int32)
        pick = jnp.where((rank == slots) & named, 1.0, 0.0)
        gate = jnp.sum(pick * gate_ref[...], axis=1, keepdims=True)
        pick = pick.astype(BF16)
        for hi in range(2):
            for lo in range(side):
                block = hi * side + lo
                cols = slice(block * width, (block + 1) * width)
                x_rows = jnp.dot(pick, x_ref[:, cols], preferred_element_type=F32)
                c_rows = jnp.dot(pick, c_ref[:, cols], preferred_element_type=F32)
                sx_ref[node * side + lo, half ^ hi] = x_rows.astype(BF16)
                sy_ref[(hi * nodes + node) * side + lo] = (gate * c_rows).astype(BF16)


def dispatch(half, ids, gates, tokens, cotangent, nodes, side, capacity):
    width = tokens.shape[1] // (2 * side)
    return pl.pallas_call(
        functools.partial(dispatch_kernel, nodes, side, capacity),
        out_shape=(
            jax.ShapeDtypeStruct((nodes * side, 2, capacity, width), BF16),
            jax.ShapeDtypeStruct((2 * nodes * side, capacity, width), BF16),
        ),
        in_specs=[SMEM] + [WHOLE] * 4,
        out_specs=(WHOLE, WHOLE),
        compiler_params=KERNEL,
        cost_estimate=cost(4 * nodes * capacity * tokens.size, tokens, cotangent, tokens, cotangent),
    )(half, ids, gates, tokens, cotangent)


def row_chunk(own_ref, other_ref, index, quarter, side):
    per_core = side // 2
    count = own_ref.shape[0] // per_core
    place = index % per_core
    own = own_ref[pl.ds(place * count, count), quarter]
    other = other_ref[pl.ds(place * count, count), quarter]
    rows = jnp.where(index < per_core, own, other)
    return rows.reshape(-1, rows.shape[-1])


def first_kernel(side, lo_ref, group_ref, own_ref, other_ref, gate_ref, up_ref, mine_ref, theirs_ref):
    first = group_ref[0] == 0
    for step in range(side):
        x = row_chunk(own_ref, other_ref, lo_ref[0] ^ step, 0, side)
        gate = jnp.dot(x, gate_ref[...], preferred_element_type=F32)
        up = jnp.dot(x, up_ref[...], preferred_element_type=F32)
        mine_ref[step] = jnp.where(first, gate, up)
        theirs_ref[step] = jnp.where(first, up, gate)


def second_kernel(side, steps, lo_ref, own_ref, other_ref, acc_ref, weight_ref, *out_refs):
    for step, out_ref in zip(steps, out_refs):
        x = row_chunk(own_ref, other_ref, lo_ref[0] ^ step, 1, side)
        pre = acc_ref[step] + jnp.dot(x, weight_ref[...], preferred_element_type=F32)
        out_ref[...] = pre.astype(out_ref.dtype)


def partial_first(lo, group, own, other, gate, up, side):
    chunk = 2 * own.shape[0] * own.shape[2] // side
    acc = jax.ShapeDtypeStruct((side, chunk, gate.shape[1]), F32)
    return pl.pallas_call(
        functools.partial(first_kernel, side),
        out_shape=(acc, acc),
        in_specs=[SMEM] * 2 + [WHOLE] * 4,
        out_specs=(WHOLE, WHOLE),
        compiler_params=KERNEL,
        cost_estimate=cost(4 * side * chunk * gate.size, own, other, gate, up),
    )(lo, group, own, other, gate, up)


def partial_second(lo, own, other, acc, weight, side, steps, dtype):
    _, chunk, width = acc.shape
    out = jax.ShapeDtypeStruct((chunk, width), dtype)
    return pl.pallas_call(
        functools.partial(second_kernel, side, steps),
        out_shape=(out,) * len(steps),
        in_specs=[SMEM] + [WHOLE] * 4,
        out_specs=(WHOLE,) * len(steps),
        compiler_params=KERNEL,
        cost_estimate=cost(2 * len(steps) * chunk * weight.size, own, other, weight),
    )(lo, own, other, acc, weight)


def pair_sum(lo, own, other, acc, weight, side):
    sends = partial_second(lo, own, other, acc, weight, side, range(1, side), BF16)
    came = [swapped(send, "lo", step) for step, send in enumerate(sends, 1)]
    total = partial_second(lo, own, other, acc, weight, side, (0,), F32)[0]
    for part in came:
        total = total + part.astype(F32)
    return total


def block_product(hidden_ref, y_own_ref, y_other_ref, hi, lo):
    rows = jnp.where(lo == 0, y_own_ref[hi], y_other_ref[hi])
    return lax.dot_general(
        hidden_ref[...], rows, (((0,), (0,)), ((), ())), preferred_element_type=F32
    )


def near_kernel(hi_ref, lo_ref, own_ref, beside_ref, y_own_ref, y_other_ref, feedback_ref, out_ref):
    hi, lo = hi_ref[0], lo_ref[0]
    total = block_product(own_ref, y_own_ref, y_other_ref, hi, lo)
    total += block_product(beside_ref, y_own_ref, y_other_ref, hi, 1 - lo)
    out_ref[...] = total + feedback_ref[...].astype(F32)


def far_kernel(hi_ref, lo_ref, across_ref, corner_ref, y_own_ref, y_other_ref, near_ref, out_ref):
    hi, lo = hi_ref[0], lo_ref[0]
    total = block_product(across_ref, y_own_ref, y_other_ref, 1 - hi, lo)
    total += block_product(corner_ref, y_own_ref, y_other_ref, 1 - hi, 1 - lo)
    out_ref[...] = (near_ref[...] + total).astype(BF16)


def two_blocks(kernel, hi, lo, first, second, y_own, y_other, base, dtype):
    shape = (first.shape[1], y_own.shape[2])
    return pl.pallas_call(
        kernel,
        out_shape=jax.ShapeDtypeStruct(shape, dtype),
        in_specs=[SMEM] * 2 + [WHOLE] * 5,
        out_specs=WHOLE,
        compiler_params=KERNEL,
        cost_estimate=cost(4 * first.size * y_own.shape[2], first, second, y_own, y_other, base),
    )(hi, lo, first, second, y_own, y_other, base)


def product(hi, lo, hidden, own_y, other_y, feedback, side):
    width = own_y.shape[-1]
    own_y, other_y = own_y.reshape(2, -1, width), other_y.reshape(2, -1, width)
    if side == 2:
        across = swapped(hidden, "hi")
        beside = swapped(hidden, "lo")
        corner = swapped(across, "lo")
        near = two_blocks(near_kernel, hi, lo, hidden, beside, own_y, other_y, feedback, F32)
        return two_blocks(far_kernel, hi, lo, across, corner, own_y, other_y, near, BF16)
    hidden = lax.all_gather(hidden, ("hi", "lo"), axis=0, tiled=True)
    y_rows = jnp.stack([own_y, other_y], axis=1).reshape(-1, width)
    grad = lax.dot_general(hidden, y_rows, (((0,), (0,)), ((), ())), preferred_element_type=F32)
    return (grad + feedback.astype(F32)).astype(BF16)


def local(tokens, cotangent, expert_ids, gate_values, w_gate, w_up, feedback):
    token_count = tokens.shape[0]
    top_count = expert_ids.shape[1]
    nodes, side = lax.axis_size("node"), lax.axis_size("lo")
    capacity = max(2, token_count * top_count // nodes)
    hi, lo, group = (lax.axis_index(a).astype(jnp.int32)[None] for a in ("hi", "lo", "groups"))
    gate_own, up_own = w_gate[0], w_up[0]
    first = group[0] == 0

    piece = jnp.where(first, gate_own, up_own)
    tokens, piece = lax.optimization_barrier((tokens, piece))
    mine = swapped(piece, "hi")
    theirs = swapped(mine, "groups")

    if top_count > 1:
        tokens = jnp.repeat(tokens, top_count, axis=0)
        cotangent = jnp.repeat(cotangent, top_count, axis=0)
    send_x, send_y = dispatch(
        hi,
        expert_ids.reshape(1, -1),
        gate_values.reshape(1, -1),
        tokens,
        cotangent,
        nodes,
        side,
        capacity,
    )
    own_x = lax.all_to_all(send_x, ("node", "lo"), 0, 0, tiled=True)
    other_x = swapped(own_x, "rep")
    acc_mine, acc_theirs = partial_first(lo, group, own_x, other_x, gate_own, up_own, side)

    send_y, _ = lax.optimization_barrier((send_y, mine))
    own_y = lax.all_to_all(send_y, ("hi", "node", "lo"), 0, 0, tiled=True)
    other_y = swapped(own_y, "rep")

    pre_mine = pair_sum(lo, own_x, other_x, acc_mine, mine, side)
    pre_theirs = pair_sum(lo, own_x, other_x, acc_theirs, theirs, side)
    pre_gate = jnp.where(first, pre_mine, pre_theirs)
    pre_up = jnp.where(first, pre_theirs, pre_mine)
    hidden = (jax.nn.silu(pre_gate) * pre_up).astype(BF16)
    return product(hi, lo, hidden, own_y, other_y, feedback[0], side)[None]


def solution(mesh):
    names = ("groups", "node", "hi", "lo", "rep")
    groups, nodes, locals_, reps = (mesh.shape[a] for a in ("groups", "node", "local", "rep"))
    split = Mesh(mesh.devices.reshape(groups, nodes, 2, locals_ // 2, reps), names)
    rows = P(names, None)
    weights = P("node", ("hi", "lo"), "rep")
    return jax.shard_map(
        local,
        mesh=split,
        in_specs=(rows, rows, rows, rows, weights, weights, P("node", "rep", ("hi", "lo"))),
        out_specs=P(("groups", "node"), "rep", ("hi", "lo")),
        check_vma=False,
    )
```

time: 146 us -> 117 us (0.80)
  blocking collectives: 17.8 us -> 0 us
  between operations: 13.5 us -> 0.15 us
  waiting for transfers between devices: 79.3 us -> 72.5 us
  starting transfers between devices: 18.4 us -> 23.9 us
  Pallas kernels: 6.21 us -> 9.97 us
  matrix products: 3.43 us -> 0 us
  local copies, waits for them, and re-layouts: 4.59 us -> 6.64 us
    all_gather x1 -> x0, waiting for transfers between devices: 22.9 us -> none  [local(): hidden = lax.all_gather(hidden, ('hi', 'lo'), axis=0, tiled=True)]
    all_to_all x1 -> x0, blocking collectives: 17.8 us -> none  [local(): own_x = lax.all_to_all(send_x, ('node', 'lo'), 0, 0, tiled=True)]
    ppermute x11 -> x9, waiting for transfers between devices: 56.3 us -> 72.5 us  [swapped(): return lax.ppermute(value, axis, pairs)]
    all_to_all x0 -> x1, starting transfers between devices: none -> 5.22 us  [local(): own_x = lax.all_to_all(send_x, ('node', 'lo'), 0, 0, tiled=True)]
    dot_general x1 -> x0, matrix products: 3.43 us -> none  [local(): lax.dot_general(hidden, y_rows.reshape(-1, width), (((0,), (0,)), ((), ()...]
    pallas_call x2 -> x7, Pallas kernels: 5.24 us -> 7.78 us  [the longest x4 4.09 us: partial_second(): pl.pallas_call(functools.partial(second_kernel, side, steps), out_shape=(...]
    unnamed x16 -> x28, local copies, waits for them, and re-layouts: 4.59 us -> 6.64 us
    all_to_all x1, starting transfers between devices: 4.22 us -> 5.92 us  [local(): own_y = lax.all_to_all(send_y, ('hi', 'node', 'lo'), 0, 0, tiled=True)]
  transfers between devices with their start and end apart: 13 -> 11, of which waited for: 7 -> 6; matrix products, arithmetic and copies ran while one was open for 2% -> 1% of each run, Pallas kernels for 4% -> 5%
where the time goes in v3:
time: 117 us; the launch traced here: 116 us
  waiting for transfers between devices  72.5 us (62%)
  starting transfers between devices  23.9 us (20%)
  Pallas kernels  9.97 us (9%)
  local copies, waits for them, and re-layouts  6.64 us (6%)
  other arithmetic  2.86 us (2%)
    ppermute x9, waiting for transfers between devices, swapped(): return lax.ppermute(value, axis, pairs)  72.5 us
    ppermute x9, starting transfers between devices, swapped(): return lax.ppermute(value, axis, pairs)  12.8 us
    unnamed x28, local copies, waits for them, and re-layouts  6.64 us
    all_to_all x1, starting transfers between devices, local(): own_y = lax.all_to_all(send_y, ('hi', 'node', 'lo'), 0, 0, tiled=True)  5.92 us
    all_to_all x1, starting transfers between devices, local(): own_x = lax.all_to_all(send_x, ('node', 'lo'), 0, 0, tiled=True)  5.22 us
    pallas_call x4, Pallas kernels, partial_second(): pl.pallas_call(functools.partial(second_kernel, side, steps), out_shape=(...  4.09 us
    pallas_call x2, Pallas kernels, two_blocks(): pl.pallas_call(kernel, out_shape=jax.ShapeDtypeStruct(shape, dtype), in_s...  2.44 us
  transfers between devices with their start and end apart: 11, of which 6 were waited for; matrix products, arithmetic and copies ran while one was open for 1% of the time, Pallas kernels for 5%

profile of v3, /device:TPU:0, one launch (start us, length us, event | category | flops | bytes accessed | tf_op | source)
XLA Modules:
  0.0 116.0 jit_solution(9374666982491043284)
XLA Ops:
  0.0 1.7 %broadcast_select_fusion = bf16[896,512]{1,0:T(8,128)(2,1)S(1)} fusion(pred[]{:T(512)S(6)} %eq.3, bf16[1,896,512]{2,1,0:T(8,128)(2,1)} %param.12, bf16[1,896,512]{2,1,0:T(8,128)(2,1)} %param.11), kind=kLoop, calls=%fused_computation | loop fusion | flops 458752 | bytes 2752513 | tf_op jit(solution)/shard_map/jit(_where)/select_n | solution.py:191
  2.0 2.2 %shard_map.73 = (bf16[4,2,64,896]{3,2,1,0:T(8,128)(2,1)}, bf16[8,64,896]{2,1,0:T(8,128)(2,1)}) custom-call(s32[1]{0:T(128)} %bitcast.half_ref.hi_ref, s32[1,128]{1,0:T(1,128)S(1)} %bitcast.20, f32[1,128]{1,0:T(1,128)S(1)} %bitcast.21, bf16[128,3584]{1,0:T(8,128)(2,1)S(1)} %copy-done.9, bf16[128,3584]{1,0:T(8,128)(2,1)S(1)} %copy-done.10), custom_call_target="tpu_custom_call" | custom-call | flops 234881024 | bytes 3670016 | tf_op jit(solution)/shard_map/pallas_call | solution.py:59
  4.2 5.2 %all-to-all-start = ((bf16[4,2,64,896]{3,2,1,0:T(8,128)(2,1)}), bf16[4,2,64,896]{3,2,1,0:T(8,128)(2,1)S(1)}, u32[]{:S(2)}, u32[]{:S(2)}) async-start(bf16[4,2,64,896]{3,2,1,0:T(8,128)(2,1)} %get-tuple-element.13), calls=%async_computation | async-start | bytes 1835008 | tf_op jit(solution)/shard_map/all_to_all | solution.py:209
  9.5 2.6 %collective-permute-start.1 = (bf16[896,512]{1,0:T(8,128)(2,1)S(1)}, bf16[896,512]{1,0:T(8,128)(2,1)S(1)}, u32[]{:S(2)}, u32[]{:S(2)}) collective-permute-start(bf16[896,512]{1,0:T(8,128)(2,1)S(1)} %broadcast_select_fusion), channel_id=1, source_target_pairs={{0,4},{4,0},{1,5},{5,1},{2,6},{6,2},{3,7},{7,3},{8,12},{12,8},{9,1... | collective-permute-start | bytes 2752520 | tf_op jit(solution)/shard_map/ppermute | solution.py:25
  12.1 39.9 %collective-permute-done.1.weight_ref = bf16[896,512]{1,0:T(8,128)(2,1)S(1)} collective-permute-done((bf16[896,512]{1,0:T(8,128)(2,1)S(1)}, bf16[896,512]{1,0:T(8,128)(2,1)S(1)}, u32[]{:S(2)}, u32[]{:S(2)}) %collective-permute-start.1) | collective-permute-done | bytes 917536 | tf_op jit(solution)/shard_map/ppermute | solution.py:25
  52.9 5.9 %all-to-all-start.1 = ((bf16[8,64,896]{2,1,0:T(8,128)(2,1)}), bf16[8,64,896]{2,1,0:T(8,128)(2,1)S(1)}, u32[]{:S(2)}, u32[]{:S(2)}) async-start(bf16[8,64,896]{2,1,0:T(8,128)(2,1)} %get-tuple-element.18), calls=%async_computation.1 | async-start | bytes 1835008 | tf_op jit(solution)/shard_map/all_to_all | solution.py:214
  58.8 1.6 %collective-permute-start.3 = (bf16[896,512]{1,0:T(8,128)(2,1)}, bf16[896,512]{1,0:T(8,128)(2,1)}, u32[]{:S(2)}, u32[]{:S(2)}) collective-permute-start(bf16[896,512]{1,0:T(8,128)(2,1)} %copy-done.4), channel_id=1, source_target_pairs={{0,16},{16,0},{1,17},{17,1},{2,18},{18,2},{3,19},{19,3},{4,20},{20... | collective-permute-start | bytes 2752520 | tf_op jit(solution)/shard_map/ppermute | solution.py:25
  61.3 1.2 %copy-done.7 = bf16[1,896,512]{2,1,0:T(8,128)(2,1)S(1)} copy-done((bf16[1,896,512]{2,1,0:T(8,128)(2,1)S(1)}, bf16[1,896,512]{2,1,0:T(8,128)(2,1)}, u32[]{:S(2)}) %copy-start.7) | copy-done | bytes 917528
  62.4 1.2 %copy-done.8 = bf16[1,896,512]{2,1,0:T(8,128)(2,1)S(1)} copy-done((bf16[1,896,512]{2,1,0:T(8,128)(2,1)S(1)}, bf16[1,896,512]{2,1,0:T(8,128)(2,1)}, u32[]{:S(2)}) %copy-start.8) | copy-done | bytes 917528
  63.6 1.2 %shard_map.74 = (f32[2,256,512]{2,1,0:T(8,128)S(1)}, f32[2,256,512]{2,1,0:T(8,128)S(1)}) custom-call(s32[1]{0:T(128)} %bitcast.1.lo_ref, s32[1]{0:T(128)} %bitcast.6.group_ref, bf16[4,2,64,896]{3,2,1,0:T(8,128)(2,1)S(1)} %all-to-all-done.own_ref, bf16[4,2,64,896]{3,2,1,0:T(8,128)(2,1)S(1)} %collective-permute-done.other_ref, bf16[896,512]{1,0:T(8,128)(2,1)S(1)} %bitcast.15, ...), custom_call_target="tpu_custom_call" | custom-call | flops 939524096 | bytes 3670016 | tf_op jit(solution)/shard_map/pallas_call | solution.py:102
  65.8 2.0 %collective-permute-start.2 = (bf16[256,512]{1,0:T(8,128)(2,1)S(1)}, bf16[256,512]{1,0:T(8,128)(2,1)S(1)}, u32[]{:S(2)}, u32[]{:S(2)}) collective-permute-start(bf16[256,512]{1,0:T(8,128)(2,1)S(1)} %shard_map.76), channel_id=1, source_target_pairs={{0,2},{2,0},{1,3},{3,1},{4,6},{6,4},{5,7},{7,5},{8,10},{10,8},{9,1... | collective-permute-start | bytes 786440 | tf_op jit(solution)/shard_map/ppermute | solution.py:25
  67.9 14.0 %collective-permute-done.3.weight_ref = bf16[896,512]{1,0:T(8,128)(2,1)} collective-permute-done((bf16[896,512]{1,0:T(8,128)(2,1)}, bf16[896,512]{1,0:T(8,128)(2,1)}, u32[]{:S(2)}, u32[]{:S(2)}) %collective-permute-start.3) | collective-permute-done | bytes 917536 | tf_op jit(solution)/shard_map/ppermute | solution.py:25
  81.9 1.6 %shard_map.78 = bf16[256,512]{1,0:T(8,128)(2,1)S(1)} custom-call(s32[1]{0:T(128)} %bitcast.1.lo_ref, bf16[4,2,64,896]{3,2,1,0:T(8,128)(2,1)S(1)} %all-to-all-done.own_ref, bf16[4,2,64,896]{3,2,1,0:T(8,128)(2,1)S(1)} %collective-permute-done.other_ref, f32[2,256,512]{2,1,0:T(8,128)S(1)} %get-tuple-element.16.acc_ref, ...), custom_call_target="tpu_custom_call" | custom-call | flops 234881024 | bytes 2752512 | tf_op jit(solution)/shard_map/pallas_call | solution.py:115
  83.5 2.1 %collective-permute-start.4 = (bf16[256,512]{1,0:T(8,128)(2,1)S(1)}, bf16[256,512]{1,0:T(8,128)(2,1)}, u32[]{:S(2)}, u32[]{:S(2)}) collective-permute-start(bf16[256,512]{1,0:T(8,128)(2,1)S(1)} %shard_map.78), channel_id=1, source_target_pairs={{0,2},{2,0},{1,3},{3,1},{4,6},{6,4},{5,7},{7,5},{8,10},{10,8},{9,1... | collective-permute-start | bytes 786440 | tf_op jit(solution)/shard_map/ppermute | solution.py:25
  85.6 1.3 %copy-done.3 = f32[2,256,512]{2,1,0:T(8,128)S(1)} copy-done((f32[2,256,512]{2,1,0:T(8,128)S(1)}, f32[2,256,512]{2,1,0:T(8,128)}, u32[]{:S(2)}) %copy-start.3) | copy-done | bytes 1048600
  86.9 1.2 %copy-done.6 = bf16[896,512]{1,0:T(8,128)(2,1)S(1)} copy-done((bf16[896,512]{1,0:T(8,128)(2,1)S(1)}, bf16[896,512]{1,0:T(8,128)(2,1)}, u32[]{:S(2)}) %copy-start.6) | copy-done | bytes 917528
  88.5 1.6 %shard_map.77 = f32[256,512]{1,0:T(8,128)S(1)} custom-call(s32[1]{0:T(128)} %bitcast.1.lo_ref, bf16[4,2,64,896]{3,2,1,0:T(8,128)(2,1)S(1)} %all-to-all-done.own_ref, bf16[4,2,64,896]{3,2,1,0:T(8,128)(2,1)S(1)} %collective-permute-done.other_ref, f32[2,256,512]{2,1,0:T(8,128)S(1)} %copy-done.1, bf16[896,512]{1,0:T(8,128)(2,1)} %collective-permute-done.3.weight_ref), custom_call_target="tpu_custom_call" | custom-call | flops 234881024 | bytes 2752512 | tf_op jit(solution)/shard_map/pallas_call | solution.py:115
  90.2 1.7 %collective-permute-done.4 = bf16[256,512]{1,0:T(8,128)(2,1)} collective-permute-done((bf16[256,512]{1,0:T(8,128)(2,1)S(1)}, bf16[256,512]{1,0:T(8,128)(2,1)}, u32[]{:S(2)}, u32[]{:S(2)}) %collective-permute-start.4) | collective-permute-done | bytes 262176 | tf_op jit(solution)/shard_map/ppermute | solution.py:25
  91.9 1.2 %multiply_convert_fusion.own_ref = bf16[256,512]{1,0:T(8,128)(2,1)S(1)} fusion(f32[256,512]{1,0:T(8,128)S(1)} %shard_map.77, bf16[256,512]{1,0:T(8,128)(2,1)} %collective-permute-done.4, f32[256,512]{1,0:T(8,128)S(1)} %shard_map.75, bf16[256,512]{1,0:T(8,128)(2,1)S(1)} %collective-permute-done.2, pred[]{:T(512)S(6)} %eq.3), kind=kLoop, calls=%fused_computation.1 | loop fusion | flops 1572864 | bytes 1835009 | tf_op jit(solution)/shard_map/convert_element_type | solution.py:221
  93.1 2.7 %collective-permute-start.5 = (bf16[256,512]{1,0:T(8,128)(2,1)S(1)}, bf16[256,512]{1,0:T(8,128)(2,1)S(1)}, u32[]{:S(2)}, u32[]{:S(2)}) collective-permute-start(bf16[256,512]{1,0:T(8,128)(2,1)S(1)} %multiply_convert_fusion.own_ref), channel_id=1, source_target_pairs={{0,4},{4,0},{1,5},{5,1},{2,6},{6,2},{3,7},{7,3},{8,12},{12,8},{9,1... | collective-permute-start | bytes 786440 | tf_op jit(solution)/shard_map/ppermute | solution.py:25
  95.8 1.5 %collective-permute-start.8 = (bf16[256,512]{1,0:T(8,128)(2,1)S(1)}, bf16[256,512]{1,0:T(8,128)(2,1)S(1)}, u32[]{:S(2)}, u32[]{:S(2)}) collective-permute-start(bf16[256,512]{1,0:T(8,128)(2,1)S(1)} %multiply_convert_fusion.own_ref), channel_id=1, source_target_pairs={{0,2},{2,0},{1,3},{3,1},{4,6},{6,4},{5,7},{7,5},{8,10},{10,8},{9,1... | collective-permute-start | bytes 786440 | tf_op jit(solution)/shard_map/ppermute | solution.py:25
  97.2 9.9 %collective-permute-done.5.across_ref = bf16[256,512]{1,0:T(8,128)(2,1)S(1)} collective-permute-done((bf16[256,512]{1,0:T(8,128)(2,1)S(1)}, bf16[256,512]{1,0:T(8,128)(2,1)S(1)}, u32[]{:S(2)}, u32[]{:S(2)}) %collective-permute-start.5) | collective-permute-done | bytes 262176 | tf_op jit(solution)/shard_map/ppermute | solution.py:25
  108.2 6.2 %collective-permute-done.6.corner_ref = bf16[256,512]{1,0:T(8,128)(2,1)S(1)} collective-permute-done((bf16[256,512]{1,0:T(8,128)(2,1)S(1)}, bf16[256,512]{1,0:T(8,128)(2,1)S(1)}, u32[]{:S(2)}, u32[]{:S(2)}) %collective-permute-start.6) | collective-permute-done | bytes 262176 | tf_op jit(solution)/shard_map/ppermute | solution.py:25
  114.4 1.7 %shard_map.80 = bf16[512,896]{1,0:T(8,128)(2,1)} custom-call(s32[1]{0:T(128)} %bitcast.half_ref.hi_ref, s32[1]{0:T(128)} %bitcast.1.lo_ref, bf16[256,512]{1,0:T(8,128)(2,1)S(1)} %collective-permute-done.5.across_ref, bf16[256,512]{1,0:T(8,128)(2,1)S(1)} %collective-permute-done.6.corner_ref, bf16[2,256,896]{2,1,0:T(8,128)(2,1)S(1)} %bitcast.14, ...), custom_call_target="tpu_custom_call" | custom-call | flops 469762048 | bytes 4194304 | tf_op jit(solution)/shard_map/pallas_call | solution.py:157
  (36 shorter events, 4.6 us)
Async XLA Ops:
  0.0 1.7 %copy-start.9 = (bf16[128,3584]{1,0:T(8,128)(2,1)S(1)}, bf16[128,3584]{1,0:T(8,128)(2,1)}, u32[]{:S(2)}) copy-start(bf16[128,3584]{1,0:T(8,128)(2,1)} %x_ref) | copy-start | bytes 2752516
  0.0 1.7 %copy-start.12 = (s32[128,1]{0,1:T(1,128)S(1)}, s32[128,1]{0,1:T(1,128)}, u32[]{:S(2)}) copy-start(s32[128,1]{0,1:T(1,128)} %param.9) | copy-start | bytes 1540
  0.0 1.7 %copy-start.13 = (f32[128,1]{0,1:T(1,128)S(1)}, f32[128,1]{0,1:T(1,128)}, u32[]{:S(2)}) copy-start(f32[128,1]{0,1:T(1,128)} %param.10) | copy-start | bytes 1540
  0.0 2.0 %copy-start.10 = (bf16[128,3584]{1,0:T(8,128)(2,1)S(1)}, bf16[128,3584]{1,0:T(8,128)(2,1)}, u32[]{:S(2)}) copy-start(bf16[128,3584]{1,0:T(8,128)(2,1)} %c_ref.1) | copy-start | bytes 2752516
  4.2 47.7 %all-to-all-start = ((bf16[4,2,64,896]{3,2,1,0:T(8,128)(2,1)}), bf16[4,2,64,896]{3,2,1,0:T(8,128)(2,1)S(1)}, u32[]{:S(2)}, u32[]{:S(2)}) async-start(bf16[4,2,64,896]{3,2,1,0:T(8,128)(2,1)} %get-tuple-element.13), calls=%async_computation | async-start | bytes 1835008 | tf_op jit(solution)/shard_map/all_to_all | solution.py:209
  9.5 42.5 %collective-permute-start.1 = (bf16[896,512]{1,0:T(8,128)(2,1)S(1)}, bf16[896,512]{1,0:T(8,128)(2,1)S(1)}, u32[]{:S(2)}, u32[]{:S(2)}) collective-permute-start(bf16[896,512]{1,0:T(8,128)(2,1)S(1)} %broadcast_select_fusion), channel_id=1, source_target_pairs={{0,4},{4,0},{1,5},{5,1},{2,6},{6,2},{3,7},{7,3},{8,12},{12,8},{9,1... | collective-permute-start | bytes 2752520 | tf_op jit(solution)/shard_map/ppermute | solution.py:25
  52.9 32.7 %all-to-all-start.1 = ((bf16[8,64,896]{2,1,0:T(8,128)(2,1)}), bf16[8,64,896]{2,1,0:T(8,128)(2,1)S(1)}, u32[]{:S(2)}, u32[]{:S(2)}) async-start(bf16[8,64,896]{2,1,0:T(8,128)(2,1)} %get-tuple-element.18), calls=%async_computation.1 | async-start | bytes 1835008 | tf_op jit(solution)/shard_map/all_to_all | solution.py:214
  58.8 2.5 %collective-permute-start = (bf16[4,2,64,896]{3,2,1,0:T(8,128)(2,1)S(1)}, bf16[4,2,64,896]{3,2,1,0:T(8,128)(2,1)S(1)}, u32[]{:S(2)}, u32[]{:S(2)}) collective-permute-start(bf16[4,2,64,896]{3,2,1,0:T(8,128)(2,1)S(1)} %all-to-all-done.own_ref), channel_id=1, source_target_pairs={{0,1},{1,0},{2,3},{3,2},{4,5},{5,4},{6,7},{7,6},{8,9},{9,8},{10,11... | collective-permute-start | bytes 2752520 | tf_op jit(solution)/shard_map/ppermute | solution.py:25
  58.8 23.1 %collective-permute-start.3 = (bf16[896,512]{1,0:T(8,128)(2,1)}, bf16[896,512]{1,0:T(8,128)(2,1)}, u32[]{:S(2)}, u32[]{:S(2)}) collective-permute-start(bf16[896,512]{1,0:T(8,128)(2,1)} %copy-done.4), channel_id=1, source_target_pairs={{0,16},{16,0},{1,17},{17,1},{2,18},{18,2},{3,19},{19,3},{4,20},{20... | collective-permute-start | bytes 2752520 | tf_op jit(solution)/shard_map/ppermute | solution.py:25
  61.3 1.2 %copy-start.7 = (bf16[1,896,512]{2,1,0:T(8,128)(2,1)S(1)}, bf16[1,896,512]{2,1,0:T(8,128)(2,1)}, u32[]{:S(2)}) copy-start(bf16[1,896,512]{2,1,0:T(8,128)(2,1)} %param.11) | copy-start | bytes 2752516
  62.4 1.2 %copy-start.8 = (bf16[1,896,512]{2,1,0:T(8,128)(2,1)S(1)}, bf16[1,896,512]{2,1,0:T(8,128)(2,1)}, u32[]{:S(2)}) copy-start(bf16[1,896,512]{2,1,0:T(8,128)(2,1)} %param.12) | copy-start | bytes 2752516
  63.6 1.3 %copy-start.5 = (bf16[896,512]{1,0:T(8,128)(2,1)S(1)}, bf16[896,512]{1,0:T(8,128)(2,1)}, u32[]{:S(2)}) copy-start(bf16[896,512]{1,0:T(8,128)(2,1)} %copy-done.4) | copy-start | bytes 2752516
  64.9 1.0 copy-start.2
  64.9 17.0 %copy-start = (f32[2,256,512]{2,1,0:T(8,128)}, f32[2,256,512]{2,1,0:T(8,128)S(1)}, u32[]{:S(2)}) copy-start(f32[2,256,512]{2,1,0:T(8,128)S(1)} %get-tuple-element.16.acc_ref) | copy-start | bytes 3145732
  65.8 24.3 %collective-permute-start.2 = (bf16[256,512]{1,0:T(8,128)(2,1)S(1)}, bf16[256,512]{1,0:T(8,128)(2,1)S(1)}, u32[]{:S(2)}, u32[]{:S(2)}) collective-permute-start(bf16[256,512]{1,0:T(8,128)(2,1)S(1)} %shard_map.76), channel_id=1, source_target_pairs={{0,2},{2,0},{1,3},{3,1},{4,6},{6,4},{5,7},{7,5},{8,10},{10,8},{9,1... | collective-permute-start | bytes 786440 | tf_op jit(solution)/shard_map/ppermute | solution.py:25
  83.5 8.4 %collective-permute-start.4 = (bf16[256,512]{1,0:T(8,128)(2,1)S(1)}, bf16[256,512]{1,0:T(8,128)(2,1)}, u32[]{:S(2)}, u32[]{:S(2)}) collective-permute-start(bf16[256,512]{1,0:T(8,128)(2,1)S(1)} %shard_map.78), channel_id=1, source_target_pairs={{0,2},{2,0},{1,3},{3,1},{4,6},{6,4},{5,7},{7,5},{8,10},{10,8},{9,1... | collective-permute-start | bytes 786440 | tf_op jit(solution)/shard_map/ppermute | solution.py:25
  85.6 2.9 %copy-start.1 = (f32[2,256,512]{2,1,0:T(8,128)S(1)}, f32[2,256,512]{2,1,0:T(8,128)}, u32[]{:S(2)}) copy-start(f32[2,256,512]{2,1,0:T(8,128)} %copy-done) | copy-start | bytes 3145732
  85.6 21.8 %collective-permute-start.7 = (bf16[8,64,896]{2,1,0:T(8,128)(2,1)S(1)}, bf16[8,64,896]{2,1,0:T(8,128)(2,1)S(1)}, u32[]{:S(2)}, u32[]{:S(2)}) collective-permute-start(bf16[8,64,896]{2,1,0:T(8,128)(2,1)S(1)} %all-to-all-done.1), channel_id=1, source_target_pairs={{0,1},{1,0},{2,3},{3,2},{4,5},{5,4},{6,7},{7,6},{8,9},{9,8},{10,11... | collective-permute-start | bytes 2752520 | tf_op jit(solution)/shard_map/ppermute | solution.py:25
  85.6 1.3 %copy-start.3 = (f32[2,256,512]{2,1,0:T(8,128)S(1)}, f32[2,256,512]{2,1,0:T(8,128)}, u32[]{:S(2)}) copy-start(f32[2,256,512]{2,1,0:T(8,128)} %copy-done.2) | copy-start | bytes 3145732
  86.9 1.2 %copy-start.6 = (bf16[896,512]{1,0:T(8,128)(2,1)S(1)}, bf16[896,512]{1,0:T(8,128)(2,1)}, u32[]{:S(2)}) copy-start(bf16[896,512]{1,0:T(8,128)(2,1)} %copy-done.4) | copy-start | bytes 2752516
  90.2 17.3 %copy-start.11 = (bf16[1,512,896]{2,1,0:T(8,128)(2,1)S(1)}, bf16[1,512,896]{2,1,0:T(8,128)(2,1)}, u32[]{:S(2)}) copy-start(bf16[1,512,896]{2,1,0:T(8,128)(2,1)} %param.13) | copy-start | bytes 2752516
  93.1 14.1 %collective-permute-start.5 = (bf16[256,512]{1,0:T(8,128)(2,1)S(1)}, bf16[256,512]{1,0:T(8,128)(2,1)S(1)}, u32[]{:S(2)}, u32[]{:S(2)}) collective-permute-start(bf16[256,512]{1,0:T(8,128)(2,1)S(1)} %multiply_convert_fusion.own_ref), channel_id=1, source_target_pairs={{0,4},{4,0},{1,5},{5,1},{2,6},{6,2},{3,7},{7,3},{8,12},{12,8},{9,1... | collective-permute-start | bytes 786440 | tf_op jit(solution)/shard_map/ppermute | solution.py:25
  95.8 11.7 %collective-permute-start.8 = (bf16[256,512]{1,0:T(8,128)(2,1)S(1)}, bf16[256,512]{1,0:T(8,128)(2,1)S(1)}, u32[]{:S(2)}, u32[]{:S(2)}) collective-permute-start(bf16[256,512]{1,0:T(8,128)(2,1)S(1)} %multiply_convert_fusion.own_ref), channel_id=1, source_target_pairs={{0,2},{2,0},{1,3},{3,1},{4,6},{6,4},{5,7},{7,5},{8,10},{10,8},{9,1... | collective-permute-start | bytes 786440 | tf_op jit(solution)/shard_map/ppermute | solution.py:25
  107.1 7.2 %collective-permute-start.6 = (bf16[256,512]{1,0:T(8,128)(2,1)S(1)}, bf16[256,512]{1,0:T(8,128)(2,1)S(1)}, u32[]{:S(2)}, u32[]{:S(2)}) collective-permute-start(bf16[256,512]{1,0:T(8,128)(2,1)S(1)} %collective-permute-done.5.across_ref), channel_id=1, source_target_pairs={{0,2},{2,0},{1,3},{3,1},{4,6},{6,4},{5,7},{7,5},{8,10},{10,8},{9,1... | collective-permute-start | bytes 786440 | tf_op jit(solution)/shard_map/ppermute | solution.py:25
  (1 other events, 1.0 us)

commit v4 on v1

v4 whole, which is shorter than its diff:
```python
import functools

import jax
import jax.numpy as jnp
from jax import lax
from jax.experimental import pallas as pl
from jax.experimental.pallas import tpu as pltpu
from jax.sharding import Mesh
from jax.sharding import PartitionSpec as P


CUT = 384
KERNEL = pltpu.CompilerParams(vmem_limit_bytes=40 << 20)
SMEM = pl.BlockSpec(memory_space=pltpu.SMEM)
WHOLE = pl.BlockSpec()
F32 = jnp.float32
BF16 = jnp.bfloat16


def call(kernel, flops, outs, scalars, arrays):
    size = sum(a.size * a.dtype.itemsize for a in (*arrays, *outs))
    return pl.pallas_call(
        kernel,
        out_shape=outs,
        in_specs=[SMEM] * len(scalars) + [WHOLE] * len(arrays),
        out_specs=(WHOLE,) * len(outs),
        compiler_params=KERNEL,
        cost_estimate=pl.CostEstimate(flops=flops, bytes_accessed=size, transcendentals=0),
    )(*scalars, *arrays)


def shape(dims, dtype):
    return jax.ShapeDtypeStruct(dims, dtype)


def swapped(value, axis, distance=1):
    pairs = [(s, s ^ distance) for s in range(lax.axis_size(axis))]
    return lax.ppermute(value, axis, pairs)


def dispatch_kernel(nodes, side, capacity, node_ref, hi_ref, lo_ref, ids_ref, gate_ref, x_ref, c_ref, *out_refs):
    pairs = ids_ref.shape[1]
    sx_refs, sy_refs = out_refs[:nodes], out_refs[nodes:]
    width = sx_refs[0].shape[-1]
    ids = ids_ref[...]
    row = lax.broadcasted_iota(jnp.int32, (pairs, pairs), 0)
    col = lax.broadcasted_iota(jnp.int32, (pairs, pairs), 1)
    earlier = (row < col).astype(BF16)
    slots = lax.broadcasted_iota(jnp.int32, (capacity, pairs), 0)
    for step in range(nodes):
        named = ids == (node_ref[0] ^ step)
        rank = jnp.dot(
            jnp.broadcast_to(jnp.where(named, 1.0, 0.0), (8, pairs)).astype(BF16),
            earlier,
            preferred_element_type=F32,
        )[:1].astype(jnp.int32)
        pick = jnp.where((rank == slots) & named, 1.0, 0.0)
        gate = jnp.sum(pick * gate_ref[...], axis=1, keepdims=True)
        pick = pick.astype(BF16)
        for hi in range(2):
            for lo in range(side):
                block = hi * side + lo
                cols = slice(block * width, (block + 1) * width)
                x_rows = jnp.dot(pick, x_ref[:, cols], preferred_element_type=F32)
                c_rows = jnp.dot(pick, c_ref[:, cols], preferred_element_type=F32)
                sx_refs[step][lo_ref[0] ^ lo, hi_ref[0] ^ hi] = x_rows.astype(BF16)
                sy_refs[step][hi_ref[0] ^ hi, lo_ref[0] ^ lo] = (gate * c_rows).astype(BF16)


def dispatch(node, hi, lo, ids, gates, tokens, cotangent, nodes, side, capacity):
    width = tokens.shape[1] // (2 * side)
    x = shape((side, 2, capacity, width), BF16)
    y = shape((2, side, capacity, width), BF16)
    outs = call(
        functools.partial(dispatch_kernel, nodes, side, capacity),
        4 * nodes * capacity * tokens.size,
        (x,) * nodes + (y,) * nodes,
        (node, hi, lo),
        (ids, gates, tokens, cotangent),
    )
    return outs[:nodes], outs[nodes:]


def owned_rows(own_ref, other_ref, lo, step, pick, nodes, side):
    owner = lo ^ step
    per_core = side // 2
    count = nodes // per_core
    place = (owner % per_core) * count
    rows = []
    for source in range(side):
        own = pick(own_ref, step ^ source, pl.ds(place, count))
        other = pick(other_ref, step ^ source, pl.ds(place, count))
        chosen = jnp.where(owner < per_core, own, other)
        rows.append(chosen.reshape(-1, chosen.shape[-1]))
    return jnp.concatenate(rows, axis=0)


def first_kernel(nodes, side, lo_ref, group_ref, own_ref, other_ref, gate_ref, up_ref, mine_ref, theirs_ref):
    first = group_ref[0] == 0
    half = gate_ref.shape[1] // 2
    for step in range(side):
        pick = lambda ref, source, part: ref[source, part, 0]
        x = owned_rows(own_ref, other_ref, lo_ref[0], step, pick, nodes, side)
        for place, weight_ref in enumerate((gate_ref, up_ref)):
            pre = jnp.dot(x, weight_ref[...], preferred_element_type=F32)
            cols = slice(place * half, (place + 1) * half)
            mine_ref[step, :, cols] = jnp.where(first, pre[:, :half], pre[:, half:])
            theirs_ref[step, :, cols] = jnp.where(first, pre[:, half:], pre[:, :half])


def second_kernel(nodes, side, steps, cuts, lo_ref, own_ref, other_ref, acc_ref, *refs):
    parts = len(cuts) - 1
    weight_refs, out_refs = refs[:parts], refs[parts:]
    for step, out_ref in zip(steps, out_refs):
        pick = lambda ref, source, part: ref[source, part, 1]
        x = owned_rows(own_ref, other_ref, lo_ref[0], step, pick, nodes, side)
        pre = acc_ref[step]
        for start, end, weight_ref in zip(cuts, cuts[1:], weight_refs):
            pre += jnp.dot(x[:, start:end], weight_ref[...], preferred_element_type=F32)
        out_ref[...] = pre.astype(out_ref.dtype)


def partial_first(lo, group, own, other, gate, up, nodes, side):
    chunk = 2 * nodes * own.shape[3]
    acc = shape((side, chunk, gate.shape[1]), F32)
    return call(
        functools.partial(first_kernel, nodes, side),
        4 * side * chunk * gate.size,
        (acc, acc),
        (lo, group),
        (own, other, gate, up),
    )


def partial_second(lo, own, other, acc, weights, cuts, nodes, side, steps, dtype):
    out = shape(acc.shape[1:], dtype)
    return call(
        functools.partial(second_kernel, nodes, side, steps, cuts),
        2 * len(steps) * acc.shape[1] * cuts[-1] * acc.shape[2],
        (out,) * len(steps),
        (lo,),
        (own, other, acc, *weights),
    )


def block_product(nodes, side, hidden_ref, own_ref, other_ref, lo, place):
    hi_step, lo_step = place
    pick = lambda ref, source, part: ref[hi_step, source, part]
    rows = owned_rows(own_ref, other_ref, lo, lo_step, pick, nodes, side)
    return lax.dot_general(
        hidden_ref[...], rows, (((0,), (0,)), ((), ())), preferred_element_type=F32
    )


def near_kernel(nodes, side, lo_ref, group_ref, *refs):
    blocks, (own_ref, other_ref, feedback_ref, done_ref, base_ref) = refs[:-5], refs[-5:]
    half = done_ref.shape[0]
    places = [(h, l) for h in range(2) for l in range(side)]
    sums = []
    for start, count, which in ((0, 2 * side, group_ref[0]), (2 * side, side, 1 - group_ref[0])):
        total = feedback_ref[pl.ds(pl.multiple_of(which * half, half), half), :].astype(F32)
        for block_ref, place in zip(blocks[start : start + count], places):
            total += block_product(nodes, side, block_ref, own_ref, other_ref, lo_ref[0], place)
        sums.append(total)
    done_ref[...] = sums[0].astype(BF16)
    base_ref[...] = sums[1]


def far_kernel(nodes, side, lo_ref, group_ref, *refs):
    blocks, (own_ref, other_ref, done_ref, base_ref, out_ref) = refs[:-5], refs[-5:]
    half = done_ref.shape[0]
    total = base_ref[...]
    for step, block_ref in enumerate(blocks):
        total += block_product(nodes, side, block_ref, own_ref, other_ref, lo_ref[0], (1, step))
    mine, theirs = group_ref[0], 1 - group_ref[0]
    out_ref[pl.ds(pl.multiple_of(mine * half, half), half), :] = done_ref[...]
    out_ref[pl.ds(pl.multiple_of(theirs * half, half), half), :] = total.astype(BF16)


def product(lo, group, first, second, own, other, feedback, nodes, side):
    half, width = first[0].shape[1], own.shape[-1]
    flops = 2 * first[0].size * width
    done, base = call(
        functools.partial(near_kernel, nodes, side),
        3 * side * flops,
        (shape((half, width), BF16), shape((half, width), F32)),
        (lo, group),
        (*first, *second[:side], own, other, feedback),
    )
    return call(
        functools.partial(far_kernel, nodes, side),
        side * flops,
        (shape((2 * half, width), BF16),),
        (lo, group),
        (*second[side:], own, other, done, base),
    )[0]


def local(tokens, cotangent, expert_ids, gate_values, w_gate, w_up, feedback):
    token_count = tokens.shape[0]
    top_count = expert_ids.shape[1]
    nodes, side = lax.axis_size("node"), lax.axis_size("lo")
    capacity = max(2, token_count * top_count // nodes)
    node, hi, lo, group = (
        lax.axis_index(a).astype(jnp.int32)[None] for a in ("node", "hi", "lo", "groups")
    )
    gate_own, up_own = w_gate[0], w_up[0]
    half = gate_own.shape[1] // 2
    width = gate_own.shape[0]
    cuts = (0, CUT, width) if width > CUT else (0, width)
    pieces = []
    for rows in (slice(*pair) for pair in zip(cuts, cuts[1:])):
        left = jnp.concatenate([gate_own[rows, :half], up_own[rows, :half]], axis=1)
        right = jnp.concatenate([gate_own[rows, half:], up_own[rows, half:]], axis=1)
        pieces.append(jnp.where(group[0] == 0, left, right))
    tokens, pieces = lax.optimization_barrier((tokens, pieces))
    mine = [swapped(piece, "hi") for piece in pieces]
    theirs = [swapped(piece, "groups") for piece in mine[:-1]]

    if top_count > 1:
        tokens = jnp.repeat(tokens, top_count, axis=0)
        cotangent = jnp.repeat(cotangent, top_count, axis=0)
    send_x, send_y = dispatch(
        node,
        hi,
        lo,
        expert_ids.reshape(1, -1),
        gate_values.reshape(1, -1),
        tokens,
        cotangent,
        nodes,
        side,
        capacity,
    )

    x = [send_x[0]] + [swapped(send_x[d], "node", d) for d in range(1, nodes)]
    x = [jnp.stack([part[d] for part in x]) for d in range(side)]
    x, mine[0] = lax.optimization_barrier((x, mine[0]))
    own_x = jnp.stack([x[0]] + [swapped(x[d], "lo", d) for d in range(1, side)])
    own_x, theirs = lax.optimization_barrier((own_x, theirs))
    other_x = swapped(own_x, "rep")
    acc_mine, acc_theirs = partial_first(lo, group, own_x, other_x, gate_own, up_own, nodes, side)
    mine[-1], acc_mine, acc_theirs = lax.optimization_barrier((mine[-1], acc_mine, acc_theirs))
    theirs.append(swapped(mine[-1], "groups"))

    y = [send_y[0]] + [swapped(send_y[d], "node", d) for d in range(1, nodes)]
    y = [[jnp.stack([part[h, l] for part in y]) for l in range(side)] for h in range(2)]
    y, mine[-1] = lax.optimization_barrier((y, mine[-1]))
    for h in range(2):
        for l in range(side):
            if (h, l) != (0, 0):
                pairs = [(s, s ^ (h * side + l)) for s in range(2 * side)]
                y[h][l] = lax.ppermute(y[h][l], ("hi", "lo"), pairs)
    own_y = jnp.stack([jnp.stack(row) for row in y])
    other_y = swapped(own_y, "rep")

    def spread_hidden(acc, weights):
        args = (lo, own_x, other_x, acc, weights, cuts, nodes, side)
        sends = partial_second(*args, range(1, side), BF16)
        came = [swapped(send, "lo", d) for d, send in enumerate(sends, 1)]
        pre = partial_second(*args, (0,), F32)[0]
        for part in came:
            pre = pre + part.astype(F32)
        hidden = (jax.nn.silu(pre[:, :half]) * pre[:, half:]).astype(BF16)
        across = swapped(hidden, "hi")
        beside = [swapped(hidden, "lo", d) for d in range(1, side)]
        corners = [swapped(across, "lo", d) for d in range(1, side)]
        return [hidden, *beside, across, *corners]

    first = spread_hidden(acc_mine, mine)
    first[0], theirs = lax.optimization_barrier((first[0], theirs))
    second = spread_hidden(acc_theirs, theirs)
    return product(lo, group, first, second, own_y, other_y, feedback[0], nodes, side)[None]


def solution(mesh):
    names = ("groups", "node", "hi", "lo", "rep")
    groups, nodes, locals_, reps = (mesh.shape[a] for a in ("groups", "node", "local", "rep"))
    split = Mesh(mesh.devices.reshape(groups, nodes, 2, locals_ // 2, reps), names)
    rows = P(names, None)
    weights = P("node", ("hi", "lo"), "rep")
    return jax.shard_map(
        local,
        mesh=split,
        in_specs=(rows, rows, rows, rows, weights, weights, P("node", "rep", ("hi", "lo"))),
        out_specs=P(("groups", "node"), "rep", ("hi", "lo")),
        check_vma=False,
    )
```

time: 149 us -> 109 us (0.73)
  blocking collectives: 30.9 us -> 0 us
  starting transfers between devices: 3.68 us -> 25.8 us
  waiting for transfers between devices: 86.1 us -> 70.9 us
  between operations: 13.4 us -> 0.32 us
  matrix products: 7.11 us -> 0 us
  Pallas kernels: 1.91 us -> 6.36 us
    ppermute x2 -> x20, waiting for transfers between devices: 4.93 us -> 70.9 us  [the longest x17 57.4 us: swapped(): return lax.ppermute(value, axis, pairs)]
    reduce_scatter x1 -> x0, waiting for transfers between devices: 53.8 us -> none  [local(): lax.psum_scatter(partial, 'local', scatter_dimension=0, tiled=True)]
    all_to_all x1 -> x0, blocking collectives: 30.9 us -> none  [local(): own_x = lax.all_to_all(send_x, axes, 0, 0, tiled=True).reshape(-1, width)]
    all_gather x1 -> x0, waiting for transfers between devices: 27.4 us -> none  [local(): hidden = lax.all_gather(hidden, 'local', axis=0, tiled=True)]
    ppermute x2 -> x20, starting transfers between devices: 0.07 us -> 25.8 us  [the longest x17 21.4 us: swapped(): return lax.ppermute(value, axis, pairs)]
    dot_general x2 -> x0, matrix products: 7.11 us -> none  [the longest x1 3.68 us: local(): jnp.dot(x_rows, weights, preferred_element_type=jnp.float32)]
    pallas_call x1 -> x8, Pallas kernels: 1.91 us -> 6.36 us  [call(): pl.pallas_call(kernel, out_shape=outs, in_specs=[SMEM] * len(scalars) + [...]
    all_to_all x1 -> x0, starting transfers between devices: 3.57 us -> none  [local(): own_y = lax.all_to_all(send_y, axes, 0, 0, tiled=True).reshape(-1, width)]
  transfers between devices with their start and end apart: 5 -> 20, of which waited for: 4 -> 14; matrix products, arithmetic and copies ran while one was open for 1% -> 1% of each run, Pallas kernels for 0% -> 3%
where the time goes in v4:
time: 109 us; the launch traced here: 108 us
  waiting for transfers between devices  70.9 us (65%)
  starting transfers between devices  25.8 us (24%)
  Pallas kernels  6.36 us (6%)
  local copies, waits for them, and re-layouts  4.01 us (4%)
    ppermute x17, waiting for transfers between devices, swapped(): return lax.ppermute(value, axis, pairs)  57.4 us
    ppermute x17, starting transfers between devices, swapped(): return lax.ppermute(value, axis, pairs)  21.4 us
    ppermute x3, waiting for transfers between devices, local(): y[h][l] = lax.ppermute(y[h][l], ('hi', 'lo'), pairs)  13.6 us
    pallas_call x8, Pallas kernels, call(): pl.pallas_call(kernel, out_shape=outs, in_specs=[SMEM] * len(scalars) + [...  6.36 us
    ppermute x3, starting transfers between devices, local(): y[h][l] = lax.ppermute(y[h][l], ('hi', 'lo'), pairs)  4.39 us
    slice x2, local copies, waits for them, and re-layouts, local(): gate_own[rows, half:]  2.44 us
  transfers between devices with their start and end apart: 20, of which 14 were waited for; matrix products, arithmetic and copies ran while one was open for 1% of the time, Pallas kernels for 3%

profile of v4, /device:TPU:0, one launch (start us, length us, event | category | flops | bytes accessed | tf_op | source)
XLA Modules:
  0.0 108.4 jit_solution(7142904711610009337)
XLA Ops:
  0.0 1.3 %fusion.4 = (bf16[384,256]{1,0:T(8,128)(2,1)S(1)}, bf16[384,256]{1,0:T(8,128)(2,1)S(1)}, bf16[384,256]{1,0:T(8,128)(2,1)S(1)}, bf16[384,256]{1,0:T(8,128)(2,1)S(1)}) fusion(bf16[896,512]{1,0:T(8,128)(2,1)} %bitcast.36, bf16[896,512]{1,0:T(8,128)(2,1)} %bitcast.39), kind=kLoop, calls=%fused_computation.28 | loop fusion | bytes 1572864 | tf_op jit(solution)/shard_map/slice | solution.py:214
  5.1 3.0 %collective-permute-start = (bf16[2,2,64,896]{3,2,1,0:T(8,128)(2,1)S(1)}, bf16[2,2,64,896]{3,2,1,0:T(8,128)(2,1)S(1)}, u32[]{:S(2)}, u32[]{:S(2)}) collective-permute-start(bf16[2,2,64,896]{3,2,1,0:T(8,128)(2,1)S(1)} %get-tuple-element.34), channel_id=1, source_target_pairs={{0,8},{8,0},{1,9},{9,1},{2,10},{10,2},{3,11},{11,3},{4,12},{12,4},... | collective-permute-start | bytes 1376264 | tf_op jit(solution)/shard_map/ppermute | solution.py:38
  8.1 2.6 %collective-permute-start.1 = (bf16[384,512]{1,0:T(8,128)(2,1)S(1)}, bf16[384,512]{1,0:T(8,128)(2,1)S(1)}, u32[]{:S(2)}, u32[]{:S(2)}) collective-permute-start(bf16[384,512]{1,0:T(8,128)(2,1)S(1)} %maximum_select_fusion.1), channel_id=1, source_target_pairs={{0,4},{4,0},{1,5},{5,1},{2,6},{6,2},{3,7},{7,3},{8,12},{12,8},{9,1... | collective-permute-start | bytes 1179656 | tf_op jit(solution)/shard_map/ppermute | solution.py:38
  10.8 7.9 %collective-permute-done = bf16[2,2,64,896]{3,2,1,0:T(8,128)(2,1)S(1)} collective-permute-done((bf16[2,2,64,896]{3,2,1,0:T(8,128)(2,1)S(1)}, bf16[2,2,64,896]{3,2,1,0:T(8,128)(2,1)S(1)}, u32[]{:S(2)}, u32[]{:S(2)}) %collective-permute-start) | collective-permute-done | bytes 458784 | tf_op jit(solution)/shard_map/ppermute | solution.py:38
  18.8 9.2 %collective-permute-done.1.refs_0_ = bf16[384,512]{1,0:T(8,128)(2,1)S(1)} collective-permute-done((bf16[384,512]{1,0:T(8,128)(2,1)S(1)}, bf16[384,512]{1,0:T(8,128)(2,1)S(1)}, u32[]{:S(2)}, u32[]{:S(2)}) %collective-permute-start.1) | collective-permute-done | bytes 393248 | tf_op jit(solution)/shard_map/ppermute | solution.py:38
  28.7 1.5 %collective-permute-start.3 = (bf16[384,512]{1,0:T(8,128)(2,1)S(1)}, bf16[384,512]{1,0:T(8,128)(2,1)S(1)}, u32[]{:S(2)}, u32[]{:S(2)}) collective-permute-start(bf16[384,512]{1,0:T(8,128)(2,1)S(1)} %collective-permute-done.1.refs_0_), channel_id=1, source_target_pairs={{0,16},{16,0},{1,17},{17,1},{2,18},{18,2},{3,19},{19,3},{4,20},{20... | collective-permute-start | bytes 1179656 | tf_op jit(solution)/shard_map/ppermute | solution.py:38
  30.8 3.4 %collective-permute-start.5 = (bf16[512,512]{1,0:T(8,128)(2,1)S(1)}, bf16[512,512]{1,0:T(8,128)(2,1)S(1)}, u32[]{:S(2)}, u32[]{:S(2)}) collective-permute-start(bf16[512,512]{1,0:T(8,128)(2,1)S(1)} %maximum_select_fusion), channel_id=1, source_target_pairs={{0,4},{4,0},{1,5},{5,1},{2,6},{6,2},{3,7},{7,3},{8,12},{12,8},{9,1... | collective-permute-start | bytes 1572872 | tf_op jit(solution)/shard_map/ppermute | solution.py:38
  34.1 13.4 %collective-permute-done.2 = bf16[2,2,64,896]{3,2,1,0:T(8,128)(2,1)S(1)} collective-permute-done((bf16[2,2,64,896]{3,2,1,0:T(8,128)(2,1)S(1)}, bf16[2,2,64,896]{3,2,1,0:T(8,128)(2,1)S(1)}, u32[]{:S(2)}, u32[]{:S(2)}) %collective-permute-start.2) | collective-permute-done | bytes 458784 | tf_op jit(solution)/shard_map/ppermute | solution.py:38
  48.0 2.2 %collective-permute-done.4.other_ref = bf16[2,2,2,64,896]{4,3,2,1,0:T(8,128)(2,1)S(1)} collective-permute-done((bf16[2,2,2,64,896]{4,3,2,1,0:T(8,128)(2,1)S(1)}, bf16[2,2,2,64,896]{4,3,2,1,0:T(8,128)(2,1)S(1)}, u32[]{:S(2)}, u32[]{:S(2)}) %collective-permute-start.4) | collective-permute-done | bytes 917536 | tf_op jit(solution)/shard_map/ppermute | solution.py:38
  51.4 5.3 %collective-permute-done.5.refs_1_ = bf16[512,512]{1,0:T(8,128)(2,1)S(1)} collective-permute-done((bf16[512,512]{1,0:T(8,128)(2,1)S(1)}, bf16[512,512]{1,0:T(8,128)(2,1)S(1)}, u32[]{:S(2)}, u32[]{:S(2)}) %collective-permute-start.5) | collective-permute-done | bytes 524320 | tf_op jit(solution)/shard_map/ppermute | solution.py:38
  56.7 3.0 %collective-permute-start.14 = (bf16[2,64,896]{2,1,0:T(8,128)(2,1)S(1)}, bf16[2,64,896]{2,1,0:T(8,128)(2,1)S(1)}, u32[]{:S(2)}, u32[]{:S(2)}) collective-permute-start(bf16[2,64,896]{2,1,0:T(8,128)(2,1)S(1)} %pad_maximum_fusion.7), channel_id=1, source_target_pairs={{0,6},{2,4},{4,2},{6,0},{1,7},{3,5},{5,3},{7,1},{8,14},{10,12},{12... | collective-permute-start | bytes 688136 | tf_op jit(solution)/shard_map/ppermute | solution.py:253
  59.7 1.3 %collective-permute-start.12 = (bf16[2,64,896]{2,1,0:T(8,128)(2,1)S(1)}, bf16[2,64,896]{2,1,0:T(8,128)(2,1)S(1)}, u32[]{:S(2)}, u32[]{:S(2)}) collective-permute-start(bf16[2,64,896]{2,1,0:T(8,128)(2,1)S(1)} %pad_maximum_fusion.5), channel_id=1, source_target_pairs={{0,2},{2,0},{4,6},{6,4},{1,3},{3,1},{5,7},{7,5},{8,10},{10,8},{12,... | collective-permute-start | bytes 688136 | tf_op jit(solution)/shard_map/ppermute | solution.py:253
  63.3 3.7 %collective-permute-done.14 = bf16[2,64,896]{2,1,0:T(8,128)(2,1)S(1)} collective-permute-done((bf16[2,64,896]{2,1,0:T(8,128)(2,1)S(1)}, bf16[2,64,896]{2,1,0:T(8,128)(2,1)S(1)}, u32[]{:S(2)}, u32[]{:S(2)}) %collective-permute-start.14) | collective-permute-done | bytes 229408 | tf_op jit(solution)/shard_map/ppermute | solution.py:253
  67.1 9.8 %collective-permute-done.13 = bf16[2,64,896]{2,1,0:T(8,128)(2,1)S(1)} collective-permute-done((bf16[2,64,896]{2,1,0:T(8,128)(2,1)S(1)}, bf16[2,64,896]{2,1,0:T(8,128)(2,1)S(1)}, u32[]{:S(2)}, u32[]{:S(2)}) %collective-permute-start.13) | collective-permute-done | bytes 229408 | tf_op jit(solution)/shard_map/ppermute | solution.py:253
  77.0 3.0 %collective-permute-done.7 = bf16[256,512]{1,0:T(8,128)(2,1)S(1)} collective-permute-done((bf16[256,512]{1,0:T(8,128)(2,1)S(1)}, bf16[256,512]{1,0:T(8,128)(2,1)S(1)}, u32[]{:S(2)}, u32[]{:S(2)}) %collective-permute-start.7) | collective-permute-done | bytes 262176 | tf_op jit(solution)/shard_map/ppermute | solution.py:38
  81.5 2.4 %collective-permute-start.17 = (bf16[256,256]{1,0:T(8,128)(2,1)S(1)}, bf16[256,256]{1,0:T(8,128)(2,1)S(1)}, u32[]{:S(2)}, u32[]{:S(2)}) collective-permute-start(bf16[256,256]{1,0:T(8,128)(2,1)S(1)} %fusion.1.refs_0_), channel_id=1, source_target_pairs={{0,4},{4,0},{1,5},{5,1},{2,6},{6,2},{3,7},{7,3},{8,12},{12,8},{9,1... | collective-permute-start | bytes 393224 | tf_op jit(solution)/shard_map/ppermute | solution.py:38
  84.4 6.7 %collective-permute-done.9 = bf16[256,512]{1,0:T(8,128)(2,1)S(1)} collective-permute-done((bf16[256,512]{1,0:T(8,128)(2,1)S(1)}, bf16[256,512]{1,0:T(8,128)(2,1)S(1)}, u32[]{:S(2)}, u32[]{:S(2)}) %collective-permute-start.9) | collective-permute-done | bytes 262176 | tf_op jit(solution)/shard_map/ppermute | solution.py:38
  91.7 2.5 %collective-permute-start.16 = (bf16[256,256]{1,0:T(8,128)(2,1)S(1)}, bf16[256,256]{1,0:T(8,128)(2,1)S(1)}, u32[]{:S(2)}, u32[]{:S(2)}) collective-permute-start(bf16[256,256]{1,0:T(8,128)(2,1)S(1)} %fusion.1.refs_0_), channel_id=1, source_target_pairs={{0,2},{2,0},{1,3},{3,1},{4,6},{6,4},{5,7},{7,5},{8,10},{10,8},{9,1... | collective-permute-start | bytes 393224 | tf_op jit(solution)/shard_map/ppermute | solution.py:38
  94.2 2.0 %collective-permute-start.19 = (bf16[256,256]{1,0:T(8,128)(2,1)S(1)}, bf16[256,256]{1,0:T(8,128)(2,1)S(1)}, u32[]{:S(2)}, u32[]{:S(2)}) collective-permute-start(bf16[256,256]{1,0:T(8,128)(2,1)S(1)} %fusion.refs_4_), channel_id=1, source_target_pairs={{0,2},{2,0},{1,3},{3,1},{4,6},{6,4},{5,7},{7,5},{8,10},{10,8},{9,1... | collective-permute-start | bytes 393224 | tf_op jit(solution)/shard_map/ppermute | solution.py:38
  96.2 2.2 %collective-permute-done.10.refs_0_ = bf16[256,256]{1,0:T(8,128)(2,1)S(1)} collective-permute-done((bf16[256,256]{1,0:T(8,128)(2,1)S(1)}, bf16[256,256]{1,0:T(8,128)(2,1)S(1)}, u32[]{:S(2)}, u32[]{:S(2)}) %collective-permute-start.10) | collective-permute-done | bytes 131104 | tf_op jit(solution)/shard_map/ppermute | solution.py:38
  98.5 1.6 %collective-permute-done.16.refs_1_ = bf16[256,256]{1,0:T(8,128)(2,1)S(1)} collective-permute-done((bf16[256,256]{1,0:T(8,128)(2,1)S(1)}, bf16[256,256]{1,0:T(8,128)(2,1)S(1)}, u32[]{:S(2)}, u32[]{:S(2)}) %collective-permute-start.16) | collective-permute-done | bytes 131104 | tf_op jit(solution)/shard_map/ppermute | solution.py:38
  100.1 2.8 %collective-permute-done.18.refs_3_ = bf16[256,256]{1,0:T(8,128)(2,1)S(1)} collective-permute-done((bf16[256,256]{1,0:T(8,128)(2,1)S(1)}, bf16[256,256]{1,0:T(8,128)(2,1)S(1)}, u32[]{:S(2)}, u32[]{:S(2)}) %collective-permute-start.18) | collective-permute-done | bytes 131104 | tf_op jit(solution)/shard_map/ppermute | solution.py:38
  102.9 2.7 %collective-permute-done.19.refs_5_ = bf16[256,256]{1,0:T(8,128)(2,1)S(1)} collective-permute-done((bf16[256,256]{1,0:T(8,128)(2,1)S(1)}, bf16[256,256]{1,0:T(8,128)(2,1)S(1)}, u32[]{:S(2)}, u32[]{:S(2)}) %collective-permute-start.19) | collective-permute-done | bytes 131104 | tf_op jit(solution)/shard_map/ppermute | solution.py:38
  107.0 1.4 %shard_map.80 = bf16[512,896]{1,0:T(8,128)(2,1)} custom-call(s32[1]{0:T(128)} %bitcast.lo_ref, s32[1]{0:T(128)} %bitcast.1.group_ref, bf16[256,256]{1,0:T(8,128)(2,1)S(1)} %collective-permute-done.10.refs_0_, bf16[256,256]{1,0:T(8,128)(2,1)S(1)} %collective-permute-done.11.refs_1_, bf16[2,2,2,64,896]{4,3,2,1,0:T(8,128)(2,1)S(1)} %pad_maximum_fusion.1.refs_6_.refs_2_, ...), custom_call_target="tpu_custom_call" | custom-call | flops 234881024 | bytes 4390912 | tf_op jit(solution)/shard_map/pallas_call | solution.py:22
  (60 shorter events, 13.0 us)
Async XLA Ops:
  0.0 1.5 %copy-start = (bf16[1,896,512]{2,1,0:T(8,128)(2,1)S(1)}, bf16[1,896,512]{2,1,0:T(8,128)(2,1)}, u32[]{:S(2)}) copy-start(bf16[1,896,512]{2,1,0:T(8,128)(2,1)} %param.11) | copy-start | bytes 2752516
  2.8 1.4 %copy-start.2 = (bf16[128,3584]{1,0:T(8,128)(2,1)S(1)}, bf16[128,3584]{1,0:T(8,128)(2,1)}, u32[]{:S(2)}) copy-start(bf16[128,3584]{1,0:T(8,128)(2,1)} %x_ref) | copy-start | bytes 2752516
  5.1 13.5 %collective-permute-start = (bf16[2,2,64,896]{3,2,1,0:T(8,128)(2,1)S(1)}, bf16[2,2,64,896]{3,2,1,0:T(8,128)(2,1)S(1)}, u32[]{:S(2)}, u32[]{:S(2)}) collective-permute-start(bf16[2,2,64,896]{3,2,1,0:T(8,128)(2,1)S(1)} %get-tuple-element.34), channel_id=1, source_target_pairs={{0,8},{8,0},{1,9},{9,1},{2,10},{10,2},{3,11},{11,3},{4,12},{12,4},... | collective-permute-start | bytes 1376264 | tf_op jit(solution)/shard_map/ppermute | solution.py:38
  8.1 19.9 %collective-permute-start.1 = (bf16[384,512]{1,0:T(8,128)(2,1)S(1)}, bf16[384,512]{1,0:T(8,128)(2,1)S(1)}, u32[]{:S(2)}, u32[]{:S(2)}) collective-permute-start(bf16[384,512]{1,0:T(8,128)(2,1)S(1)} %maximum_select_fusion.1), channel_id=1, source_target_pairs={{0,4},{4,0},{1,5},{5,1},{2,6},{6,2},{3,7},{7,3},{8,12},{12,8},{9,1... | collective-permute-start | bytes 1179656 | tf_op jit(solution)/shard_map/ppermute | solution.py:38
  28.0 19.5 %collective-permute-start.2 = (bf16[2,2,64,896]{3,2,1,0:T(8,128)(2,1)S(1)}, bf16[2,2,64,896]{3,2,1,0:T(8,128)(2,1)S(1)}, u32[]{:S(2)}, u32[]{:S(2)}) collective-permute-start(bf16[2,2,64,896]{3,2,1,0:T(8,128)(2,1)S(1)} %pad_maximum_fusion.3), channel_id=1, source_target_pairs={{0,2},{2,0},{1,3},{3,1},{4,6},{6,4},{5,7},{7,5},{8,10},{10,8},{9,1... | collective-permute-start | bytes 1376264 | tf_op jit(solution)/shard_map/ppermute | solution.py:38
  28.7 18.9 %collective-permute-start.3 = (bf16[384,512]{1,0:T(8,128)(2,1)S(1)}, bf16[384,512]{1,0:T(8,128)(2,1)S(1)}, u32[]{:S(2)}, u32[]{:S(2)}) collective-permute-start(bf16[384,512]{1,0:T(8,128)(2,1)S(1)} %collective-permute-done.1.refs_0_), channel_id=1, source_target_pairs={{0,16},{16,0},{1,17},{17,1},{2,18},{18,2},{3,19},{19,3},{4,20},{20... | collective-permute-start | bytes 1179656 | tf_op jit(solution)/shard_map/ppermute | solution.py:38
  30.2 17.5 %collective-permute-start.6 = (bf16[2,2,64,896]{3,2,1,0:T(8,128)(2,1)S(1)}, bf16[2,2,64,896]{3,2,1,0:T(8,128)(2,1)S(1)}, u32[]{:S(2)}, u32[]{:S(2)}) collective-permute-start(bf16[2,2,64,896]{3,2,1,0:T(8,128)(2,1)S(1)} %get-tuple-element.46), channel_id=1, source_target_pairs={{0,8},{8,0},{1,9},{9,1},{2,10},{10,2},{3,11},{11,3},{4,12},{12,4},... | collective-permute-start | bytes 1376264 | tf_op jit(solution)/shard_map/ppermute | solution.py:38
  30.8 25.9 %collective-permute-start.5 = (bf16[512,512]{1,0:T(8,128)(2,1)S(1)}, bf16[512,512]{1,0:T(8,128)(2,1)S(1)}, u32[]{:S(2)}, u32[]{:S(2)}) collective-permute-start(bf16[512,512]{1,0:T(8,128)(2,1)S(1)} %maximum_select_fusion), channel_id=1, source_target_pairs={{0,4},{4,0},{1,5},{5,1},{2,6},{6,2},{3,7},{7,3},{8,12},{12,8},{9,1... | collective-permute-start | bytes 1572872 | tf_op jit(solution)/shard_map/ppermute | solution.py:38
  47.6 2.5 %collective-permute-start.4 = (bf16[2,2,2,64,896]{4,3,2,1,0:T(8,128)(2,1)S(1)}, bf16[2,2,2,64,896]{4,3,2,1,0:T(8,128)(2,1)S(1)}, u32[]{:S(2)}, u32[]{:S(2)}) collective-permute-start(bf16[2,2,2,64,896]{4,3,2,1,0:T(8,128)(2,1)S(1)} %pad_maximum_fusion.own_ref), channel_id=1, source_target_pairs={{0,1},{1,0},{2,3},{3,2},{4,5},{5,4},{6,7},{7,6},{8,9},{9,8},{10,11... | collective-permute-start | bytes 2752520 | tf_op jit(solution)/shard_map/ppermute | solution.py:38
  47.8 2.4 %copy-start.1 = (bf16[1,896,512]{2,1,0:T(8,128)(2,1)S(1)}, bf16[1,896,512]{2,1,0:T(8,128)(2,1)}, u32[]{:S(2)}) copy-start(bf16[1,896,512]{2,1,0:T(8,128)(2,1)} %param.12) | copy-start | bytes 2752516
  56.7 10.4 %collective-permute-start.14 = (bf16[2,64,896]{2,1,0:T(8,128)(2,1)S(1)}, bf16[2,64,896]{2,1,0:T(8,128)(2,1)S(1)}, u32[]{:S(2)}, u32[]{:S(2)}) collective-permute-start(bf16[2,64,896]{2,1,0:T(8,128)(2,1)S(1)} %pad_maximum_fusion.7), channel_id=1, source_target_pairs={{0,6},{2,4},{4,2},{6,0},{1,7},{3,5},{5,3},{7,1},{8,14},{10,12},{12... | collective-permute-start | bytes 688136 | tf_op jit(solution)/shard_map/ppermute | solution.py:253
  59.7 17.2 %collective-permute-start.13 = (bf16[2,64,896]{2,1,0:T(8,128)(2,1)S(1)}, bf16[2,64,896]{2,1,0:T(8,128)(2,1)S(1)}, u32[]{:S(2)}, u32[]{:S(2)}) collective-permute-start(bf16[2,64,896]{2,1,0:T(8,128)(2,1)S(1)} %pad_maximum_fusion.6), channel_id=1, source_target_pairs={{0,4},{2,6},{4,0},{6,2},{1,5},{3,7},{5,1},{7,3},{8,12},{10,14},{12... | collective-permute-start | bytes 688136 | tf_op jit(solution)/shard_map/ppermute | solution.py:253
  59.7 17.2 %collective-permute-start.12 = (bf16[2,64,896]{2,1,0:T(8,128)(2,1)S(1)}, bf16[2,64,896]{2,1,0:T(8,128)(2,1)S(1)}, u32[]{:S(2)}, u32[]{:S(2)}) collective-permute-start(bf16[2,64,896]{2,1,0:T(8,128)(2,1)S(1)} %pad_maximum_fusion.5), channel_id=1, source_target_pairs={{0,2},{2,0},{4,6},{6,4},{1,3},{3,1},{5,7},{7,5},{8,10},{10,8},{12,... | collective-permute-start | bytes 688136 | tf_op jit(solution)/shard_map/ppermute | solution.py:253
  61.1 19.1 %collective-permute-start.8 = (bf16[512,512]{1,0:T(8,128)(2,1)S(1)}, bf16[512,512]{1,0:T(8,128)(2,1)S(1)}, u32[]{:S(2)}, u32[]{:S(2)}) collective-permute-start(bf16[512,512]{1,0:T(8,128)(2,1)S(1)} %collective-permute-done.5.refs_1_), channel_id=1, source_target_pairs={{0,16},{16,0},{1,17},{17,1},{2,18},{18,2},{3,19},{19,3},{4,20},{20... | collective-permute-start | bytes 1572872 | tf_op jit(solution)/shard_map/ppermute | solution.py:38
  62.0 18.0 %collective-permute-start.7 = (bf16[256,512]{1,0:T(8,128)(2,1)S(1)}, bf16[256,512]{1,0:T(8,128)(2,1)S(1)}, u32[]{:S(2)}, u32[]{:S(2)}) collective-permute-start(bf16[256,512]{1,0:T(8,128)(2,1)S(1)} %shard_map.76), channel_id=1, source_target_pairs={{0,2},{2,0},{1,3},{3,1},{4,6},{6,4},{5,7},{7,5},{8,10},{10,8},{9,1... | collective-permute-start | bytes 786440 | tf_op jit(solution)/shard_map/ppermute | solution.py:38
  80.6 10.5 %collective-permute-start.9 = (bf16[256,512]{1,0:T(8,128)(2,1)S(1)}, bf16[256,512]{1,0:T(8,128)(2,1)S(1)}, u32[]{:S(2)}, u32[]{:S(2)}) collective-permute-start(bf16[256,512]{1,0:T(8,128)(2,1)S(1)} %shard_map.78), channel_id=1, source_target_pairs={{0,2},{2,0},{1,3},{3,1},{4,6},{6,4},{5,7},{7,5},{8,10},{10,8},{9,1... | collective-permute-start | bytes 786440 | tf_op jit(solution)/shard_map/ppermute | solution.py:38
  81.5 24.2 %collective-permute-start.15 = (bf16[2,2,2,64,896]{4,3,2,1,0:T(8,128)(2,1)S(1)}, bf16[2,2,2,64,896]{4,3,2,1,0:T(8,128)(2,1)S(1)}, u32[]{:S(2)}, u32[]{:S(2)}) collective-permute-start(bf16[2,2,2,64,896]{4,3,2,1,0:T(8,128)(2,1)S(1)} %pad_maximum_fusion.1.refs_6_.refs_2_), channel_id=1, source_target_pairs={{0,1},{1,0},{2,3},{3,2},{4,5},{5,4},{6,7},{7,6},{8,9},{9,8},{10,11... | collective-permute-start | bytes 2752520 | tf_op jit(solution)/shard_map/ppermute | solution.py:38
  81.5 12.6 %collective-permute-start.17 = (bf16[256,256]{1,0:T(8,128)(2,1)S(1)}, bf16[256,256]{1,0:T(8,128)(2,1)S(1)}, u32[]{:S(2)}, u32[]{:S(2)}) collective-permute-start(bf16[256,256]{1,0:T(8,128)(2,1)S(1)} %fusion.1.refs_0_), channel_id=1, source_target_pairs={{0,4},{4,0},{1,5},{5,1},{2,6},{6,2},{3,7},{7,3},{8,12},{12,8},{9,1... | collective-permute-start | bytes 393224 | tf_op jit(solution)/shard_map/ppermute | solution.py:38
  84.4 21.2 %copy-start.4 = (bf16[1,512,896]{2,1,0:T(8,128)(2,1)S(1)}, bf16[1,512,896]{2,1,0:T(8,128)(2,1)}, u32[]{:S(2)}) copy-start(bf16[1,512,896]{2,1,0:T(8,128)(2,1)} %param.13) | copy-start | bytes 2752516
  91.3 7.1 %collective-permute-start.10 = (bf16[256,256]{1,0:T(8,128)(2,1)S(1)}, bf16[256,256]{1,0:T(8,128)(2,1)S(1)}, u32[]{:S(2)}, u32[]{:S(2)}) collective-permute-start(bf16[256,256]{1,0:T(8,128)(2,1)S(1)} %fusion.refs_4_), channel_id=1, source_target_pairs={{0,4},{4,0},{1,5},{5,1},{2,6},{6,2},{3,7},{7,3},{8,12},{12,8},{9,1... | collective-permute-start | bytes 393224 | tf_op jit(solution)/shard_map/ppermute | solution.py:38
  91.7 8.4 %collective-permute-start.16 = (bf16[256,256]{1,0:T(8,128)(2,1)S(1)}, bf16[256,256]{1,0:T(8,128)(2,1)S(1)}, u32[]{:S(2)}, u32[]{:S(2)}) collective-permute-start(bf16[256,256]{1,0:T(8,128)(2,1)S(1)} %fusion.1.refs_0_), channel_id=1, source_target_pairs={{0,2},{2,0},{1,3},{3,1},{4,6},{6,4},{5,7},{7,5},{8,10},{10,8},{9,1... | collective-permute-start | bytes 393224 | tf_op jit(solution)/shard_map/ppermute | solution.py:38
  94.2 8.7 %collective-permute-start.18 = (bf16[256,256]{1,0:T(8,128)(2,1)S(1)}, bf16[256,256]{1,0:T(8,128)(2,1)S(1)}, u32[]{:S(2)}, u32[]{:S(2)}) collective-permute-start(bf16[256,256]{1,0:T(8,128)(2,1)S(1)} %collective-permute-done.17.refs_2_), channel_id=1, source_target_pairs={{0,2},{2,0},{1,3},{3,1},{4,6},{6,4},{5,7},{7,5},{8,10},{10,8},{9,1... | collective-permute-start | bytes 393224 | tf_op jit(solution)/shard_map/ppermute | solution.py:38
  94.2 11.4 %collective-permute-start.19 = (bf16[256,256]{1,0:T(8,128)(2,1)S(1)}, bf16[256,256]{1,0:T(8,128)(2,1)S(1)}, u32[]{:S(2)}, u32[]{:S(2)}) collective-permute-start(bf16[256,256]{1,0:T(8,128)(2,1)S(1)} %fusion.refs_4_), channel_id=1, source_target_pairs={{0,2},{2,0},{1,3},{3,1},{4,6},{6,4},{5,7},{7,5},{8,10},{10,8},{9,1... | collective-permute-start | bytes 393224 | tf_op jit(solution)/shard_map/ppermute | solution.py:38
  98.4 8.7 %collective-permute-start.11 = (bf16[256,256]{1,0:T(8,128)(2,1)S(1)}, bf16[256,256]{1,0:T(8,128)(2,1)S(1)}, u32[]{:S(2)}, u32[]{:S(2)}) collective-permute-start(bf16[256,256]{1,0:T(8,128)(2,1)S(1)} %collective-permute-done.10.refs_0_), channel_id=1, source_target_pairs={{0,2},{2,0},{1,3},{3,1},{4,6},{6,4},{5,7},{7,5},{8,10},{10,8},{9,1... | collective-permute-start | bytes 393224 | tf_op jit(solution)/shard_map/ppermute | solution.py:38
  (3 other events, 3.6 us)

commit v5 on v4

--- a/solution.py
+++ b/solution.py
@@ -9,7 +9,7 @@
 from jax.sharding import PartitionSpec as P
 
 
-CUT = 384
+CUT = 100000
 KERNEL = pltpu.CompilerParams(vmem_limit_bytes=40 << 20)
 SMEM = pl.BlockSpec(memory_space=pltpu.SMEM)
 WHOLE = pl.BlockSpec()
@@ -233,32 +233,7 @@
         capacity,
     )
 
-    x = [send_x[0]] + [swapped(send_x[d], "node", d) for d in range(1, nodes)]
-    x = [jnp.stack([part[d] for part in x]) for d in range(side)]
-    x, mine[0] = lax.optimization_barrier((x, mine[0]))
-    own_x = jnp.stack([x[0]] + [swapped(x[d], "lo", d) for d in range(1, side)])
-    own_x, theirs = lax.optimization_barrier((own_x, theirs))
-    other_x = swapped(own_x, "rep")
-    acc_mine, acc_theirs = partial_first(lo, group, own_x, other_x, gate_own, up_own, nodes, side)
-    mine[-1], acc_mine, acc_theirs = lax.optimization_barrier((mine[-1], acc_mine, acc_theirs))
-    theirs.append(swapped(mine[-1], "groups"))
-
-    y = [send_y[0]] + [swapped(send_y[d], "node", d) for d in range(1, nodes)]
-    y = [[jnp.stack([part[h, l] for part in y]) for l in range(side)] for h in range(2)]
-    y, mine[-1] = lax.optimization_barrier((y, mine[-1]))
-    for h in range(2):
-        for l in range(side):
-            if (h, l) != (0, 0):
-                pairs = [(s, s ^ (h * side + l)) for s in range(2 * side)]
-                y[h][l] = lax.ppermute(y[h][l], ("hi", "lo"), pairs)
-    own_y = jnp.stack([jnp.stack(row) for row in y])
-    other_y = swapped(own_y, "rep")
-
-    def spread_hidden(acc, weights):
-        args = (lo, own_x, other_x, acc, weights, cuts, nodes, side)
-        sends = partial_second(*args, range(1, side), BF16)
-        came = [swapped(send, "lo", d) for d, send in enumerate(sends, 1)]
-        pre = partial_second(*args, (0,), F32)[0]
+    def spread_hidden(pre, came):
         for part in came:
             pre = pre + part.astype(F32)
         hidden = (jax.nn.silu(pre[:, :half]) * pre[:, half:]).astype(BF16)
@@ -267,9 +242,34 @@
         corners = [swapped(across, "lo", d) for d in range(1, side)]
         return [hidden, *beside, across, *corners]
 
-    first = spread_hidden(acc_mine, mine)
+    x = [send_x[0]] + [swapped(send_x[d], "node", d) for d in range(1, nodes)]
+    x = [jnp.stack([part[d] for part in x]) for d in range(side)]
+    y = [send_y[0]] + [swapped(send_y[d], "node", d) for d in range(1, nodes)]
+    y = [[jnp.stack([part[h, l] for part in y]) for l in range(side)] for h in range(2)]
+    own_x = jnp.stack([x[0]] + [swapped(x[d], "lo", d) for d in range(1, side)])
+    own_x, mine[-1] = lax.optimization_barrier((own_x, mine[-1]))
+    other_x = swapped(own_x, "rep")
+    acc_mine, acc_theirs = partial_first(lo, group, own_x, other_x, gate_own, up_own, nodes, side)
+    theirs.append(swapped(mine[-1], "groups"))
+    margs = (lo, own_x, other_x, acc_mine, mine, cuts, nodes, side)
+    sends_m = partial_second(*margs, range(1, side), BF16)
+    y, mine[-1] = lax.optimization_barrier((y, mine[-1]))
+    for h in range(2):
+        for l in range(side):
+            if (h, l) != (0, 0):
+                pairs = [(s, s ^ (h * side + l)) for s in range(2 * side)]
+                y[h][l] = lax.ppermute(y[h][l], ("hi", "lo"), pairs)
+    came_m = [swapped(send, "lo", d) for d, send in enumerate(sends_m, 1)]
+    keep_m = partial_second(*margs, (0,), F32)[0]
+    first = spread_hidden(keep_m, came_m)
+    own_y = jnp.stack([jnp.stack(row) for row in y])
+    other_y = swapped(own_y, "rep")
     first[0], theirs = lax.optimization_barrier((first[0], theirs))
-    second = spread_hidden(acc_theirs, theirs)
+    targs = (lo, own_x, other_x, acc_theirs, theirs, cuts, nodes, side)
+    sends_t = partial_second(*targs, range(1, side), BF16)
+    came_t = [swapped(send, "lo", d) for d, send in enumerate(sends_t, 1)]
+    keep_t = partial_second(*targs, (0,), F32)[0]
+    second = spread_hidden(keep_t, came_t)
     return product(lo, group, first, second, own_y, other_y, feedback[0], nodes, side)[None]
 
 

time: 109 us -> 105 us (0.963)
  waiting for transfers between devices: 70.9 us -> 67.3 us
  starting transfers between devices: 25.8 us -> 26.9 us
    ppermute x17 -> x15, waiting for transfers between devices: 57.4 us -> 53.2 us  [swapped(): return lax.ppermute(value, axis, pairs)]
    ppermute x17 -> x15, starting transfers between devices: 21.4 us -> 22.4 us  [swapped(): return lax.ppermute(value, axis, pairs)]
    slice x2 -> x1, local copies, waits for them, and re-layouts: 2.44 us -> 1.55 us  [local(): gate_own[rows, half:]]
  transfers between devices with their start and end apart: 20 -> 18, of which waited for: 14 -> 13; matrix products, arithmetic and copies ran while one was open for 1% -> 1% of each run, Pallas kernels for 3% -> 3%
where the time goes in v5:
time: 105 us
  waiting for transfers between devices  67.3 us (64%)
  starting transfers between devices  26.9 us (26%)
  Pallas kernels  6.37 us (6%)
  local copies, waits for them, and re-layouts  2.94 us (3%)
    ppermute x15, waiting for transfers between devices, swapped(): return lax.ppermute(value, axis, pairs)  53.2 us
    ppermute x15, starting transfers between devices, swapped(): return lax.ppermute(value, axis, pairs)  22.4 us
    ppermute x3, waiting for transfers between devices, local(): y[h][l] = lax.ppermute(y[h][l], ('hi', 'lo'), pairs)  14.2 us
    pallas_call x8, Pallas kernels, call(): pl.pallas_call(kernel, out_shape=outs, in_specs=[SMEM] * len(scalars) + [...  6.37 us
    ppermute x3, starting transfers between devices, local(): y[h][l] = lax.ppermute(y[h][l], ('hi', 'lo'), pairs)  4.46 us
  transfers between devices with their start and end apart: 18, of which 13 were waited for; matrix products, arithmetic and copies ran while one was open for 1% of the time, Pallas kernels for 3%

profile of v5, /device:TPU:0, one launch (start us, length us, event | category | flops | bytes accessed | tf_op | source)
XLA Modules:
  0.0 104.8 jit_solution(2996704784464546116)
XLA Ops:
  0.0 1.6 %fusion.2 = (bf16[896,256]{1,0:T(8,128)(2,1)S(1)}, bf16[896,256]{1,0:T(8,128)(2,1)S(1)}, bf16[896,256]{1,0:T(8,128)(2,1)S(1)}, bf16[896,256]{1,0:T(8,128)(2,1)S(1)}) fusion(bf16[896,512]{1,0:T(8,128)(2,1)} %bitcast.37, bf16[896,512]{1,0:T(8,128)(2,1)} %bitcast.39), kind=kLoop, calls=%fused_computation.25 | loop fusion | bytes 3670016 | tf_op jit(solution)/shard_map/slice | solution.py:214
  4.0 3.0 %collective-permute-start = (bf16[2,2,64,896]{3,2,1,0:T(8,128)(2,1)S(1)}, bf16[2,2,64,896]{3,2,1,0:T(8,128)(2,1)S(1)}, u32[]{:S(2)}, u32[]{:S(2)}) collective-permute-start(bf16[2,2,64,896]{3,2,1,0:T(8,128)(2,1)S(1)} %get-tuple-element.26), channel_id=1, source_target_pairs={{0,8},{8,0},{1,9},{9,1},{2,10},{10,2},{3,11},{11,3},{4,12},{12,4},... | collective-permute-start | bytes 1376264 | tf_op jit(solution)/shard_map/ppermute | solution.py:38
  7.0 2.6 %collective-permute-start.2 = (bf16[896,512]{1,0:T(8,128)(2,1)S(1)}, bf16[896,512]{1,0:T(8,128)(2,1)S(1)}, u32[]{:S(2)}, u32[]{:S(2)}) collective-permute-start(bf16[896,512]{1,0:T(8,128)(2,1)S(1)} %maximum_select_fusion), channel_id=1, source_target_pairs={{0,4},{4,0},{1,5},{5,1},{2,6},{6,2},{3,7},{7,3},{8,12},{12,8},{9,1... | collective-permute-start | bytes 2752520 | tf_op jit(solution)/shard_map/ppermute | solution.py:38
  9.7 7.9 %collective-permute-done = bf16[2,2,64,896]{3,2,1,0:T(8,128)(2,1)S(1)} collective-permute-done((bf16[2,2,64,896]{3,2,1,0:T(8,128)(2,1)S(1)}, bf16[2,2,64,896]{3,2,1,0:T(8,128)(2,1)S(1)}, u32[]{:S(2)}, u32[]{:S(2)}) %collective-permute-start) | collective-permute-done | bytes 458784 | tf_op jit(solution)/shard_map/ppermute | solution.py:38
  17.6 1.9 %collective-permute-start.1 = (bf16[2,2,64,896]{3,2,1,0:T(8,128)(2,1)S(1)}, bf16[2,2,64,896]{3,2,1,0:T(8,128)(2,1)S(1)}, u32[]{:S(2)}, u32[]{:S(2)}) collective-permute-start(bf16[2,2,64,896]{3,2,1,0:T(8,128)(2,1)S(1)} %pad_maximum_fusion.2), channel_id=1, source_target_pairs={{0,2},{2,0},{1,3},{3,1},{4,6},{6,4},{5,7},{7,5},{8,10},{10,8},{9,1... | collective-permute-start | bytes 1376264 | tf_op jit(solution)/shard_map/ppermute | solution.py:38
  19.5 1.5 %collective-permute-start.4 = (bf16[2,2,64,896]{3,2,1,0:T(8,128)(2,1)S(1)}, bf16[2,2,64,896]{3,2,1,0:T(8,128)(2,1)S(1)}, u32[]{:S(2)}, u32[]{:S(2)}) collective-permute-start(bf16[2,2,64,896]{3,2,1,0:T(8,128)(2,1)S(1)} %get-tuple-element.32), channel_id=1, source_target_pairs={{0,8},{8,0},{1,9},{9,1},{2,10},{10,2},{3,11},{11,3},{4,12},{12,4},... | collective-permute-start | bytes 1376264 | tf_op jit(solution)/shard_map/ppermute | solution.py:38
  21.1 17.7 %collective-permute-done.1 = bf16[2,2,64,896]{3,2,1,0:T(8,128)(2,1)S(1)} collective-permute-done((bf16[2,2,64,896]{3,2,1,0:T(8,128)(2,1)S(1)}, bf16[2,2,64,896]{3,2,1,0:T(8,128)(2,1)S(1)}, u32[]{:S(2)}, u32[]{:S(2)}) %collective-permute-start.1) | collective-permute-done | bytes 458784 | tf_op jit(solution)/shard_map/ppermute | solution.py:38
  38.9 10.5 %collective-permute-done.2.refs_0_ = bf16[896,512]{1,0:T(8,128)(2,1)S(1)} collective-permute-done((bf16[896,512]{1,0:T(8,128)(2,1)S(1)}, bf16[896,512]{1,0:T(8,128)(2,1)S(1)}, u32[]{:S(2)}, u32[]{:S(2)}) %collective-permute-start.2) | collective-permute-done | bytes 917536 | tf_op jit(solution)/shard_map/ppermute | solution.py:38
  49.7 3.6 %collective-permute-start.12 = (bf16[2,64,896]{2,1,0:T(8,128)(2,1)S(1)}, bf16[2,64,896]{2,1,0:T(8,128)(2,1)S(1)}, u32[]{:S(2)}, u32[]{:S(2)}) collective-permute-start(bf16[2,64,896]{2,1,0:T(8,128)(2,1)S(1)} %pad_maximum_fusion.6), channel_id=1, source_target_pairs={{0,6},{2,4},{4,2},{6,0},{1,7},{3,5},{5,3},{7,1},{8,14},{10,12},{12... | collective-permute-start | bytes 688136 | tf_op jit(solution)/shard_map/ppermute | solution.py:261
  53.2 1.5 %collective-permute-start.6 = (bf16[896,512]{1,0:T(8,128)(2,1)S(1)}, bf16[896,512]{1,0:T(8,128)(2,1)S(1)}, u32[]{:S(2)}, u32[]{:S(2)}) collective-permute-start(bf16[896,512]{1,0:T(8,128)(2,1)S(1)} %collective-permute-done.2.refs_0_), channel_id=1, source_target_pairs={{0,16},{16,0},{1,17},{17,1},{2,18},{18,2},{3,19},{19,3},{4,20},{20... | collective-permute-start | bytes 2752520 | tf_op jit(solution)/shard_map/ppermute | solution.py:38
  55.6 1.2 %shard_map.74 = (f32[2,256,512]{2,1,0:T(8,128)S(1)}, f32[2,256,512]{2,1,0:T(8,128)S(1)}) custom-call(s32[1]{0:T(128)} %bitcast.lo_ref, s32[1]{0:T(128)} %bitcast.1.group_ref, bf16[2,2,2,64,896]{4,3,2,1,0:T(8,128)(2,1)S(1)} %pad_maximum_fusion.own_ref, bf16[2,2,2,64,896]{4,3,2,1,0:T(8,128)(2,1)S(1)} %collective-permute-done.3.other_ref, ...), custom_call_target="tpu_custom_call" | custom-call | flops 939524096 | bytes 5767168 | tf_op jit(solution)/shard_map/pallas_call | solution.py:22
  58.5 1.5 %collective-permute-done.12 = bf16[2,64,896]{2,1,0:T(8,128)(2,1)S(1)} collective-permute-done((bf16[2,64,896]{2,1,0:T(8,128)(2,1)S(1)}, bf16[2,64,896]{2,1,0:T(8,128)(2,1)S(1)}, u32[]{:S(2)}, u32[]{:S(2)}) %collective-permute-start.12) | collective-permute-done | bytes 229408 | tf_op jit(solution)/shard_map/ppermute | solution.py:261
  60.1 12.6 %collective-permute-done.11 = bf16[2,64,896]{2,1,0:T(8,128)(2,1)S(1)} collective-permute-done((bf16[2,64,896]{2,1,0:T(8,128)(2,1)S(1)}, bf16[2,64,896]{2,1,0:T(8,128)(2,1)S(1)}, u32[]{:S(2)}, u32[]{:S(2)}) %collective-permute-start.11) | collective-permute-done | bytes 229408 | tf_op jit(solution)/shard_map/ppermute | solution.py:261
  73.3 1.8 %collective-permute-done.5 = bf16[256,512]{1,0:T(8,128)(2,1)S(1)} collective-permute-done((bf16[256,512]{1,0:T(8,128)(2,1)S(1)}, bf16[256,512]{1,0:T(8,128)(2,1)S(1)}, u32[]{:S(2)}, u32[]{:S(2)}) %collective-permute-start.5) | collective-permute-done | bytes 262176 | tf_op jit(solution)/shard_map/ppermute | solution.py:38
  76.1 1.3 %collective-permute-start.7 = (bf16[256,512]{1,0:T(8,128)(2,1)S(1)}, bf16[256,512]{1,0:T(8,128)(2,1)S(1)}, u32[]{:S(2)}, u32[]{:S(2)}) collective-permute-start(bf16[256,512]{1,0:T(8,128)(2,1)S(1)} %shard_map.78), channel_id=1, source_target_pairs={{0,2},{2,0},{1,3},{3,1},{4,6},{6,4},{5,7},{7,5},{8,10},{10,8},{9,1... | collective-permute-start | bytes 786440 | tf_op jit(solution)/shard_map/ppermute | solution.py:38
  77.6 2.4 %collective-permute-start.15 = (bf16[256,256]{1,0:T(8,128)(2,1)S(1)}, bf16[256,256]{1,0:T(8,128)(2,1)S(1)}, u32[]{:S(2)}, u32[]{:S(2)}) collective-permute-start(bf16[256,256]{1,0:T(8,128)(2,1)S(1)} %fusion.1.refs_0_), channel_id=1, source_target_pairs={{0,4},{4,0},{1,5},{5,1},{2,6},{6,2},{3,7},{7,3},{8,12},{12,8},{9,1... | collective-permute-start | bytes 393224 | tf_op jit(solution)/shard_map/ppermute | solution.py:38
  80.5 6.3 %collective-permute-done.7 = bf16[256,512]{1,0:T(8,128)(2,1)S(1)} collective-permute-done((bf16[256,512]{1,0:T(8,128)(2,1)S(1)}, bf16[256,512]{1,0:T(8,128)(2,1)S(1)}, u32[]{:S(2)}, u32[]{:S(2)}) %collective-permute-start.7) | collective-permute-done | bytes 262176 | tf_op jit(solution)/shard_map/ppermute | solution.py:38
  87.0 1.6 %collective-permute-start.8 = (bf16[256,256]{1,0:T(8,128)(2,1)S(1)}, bf16[256,256]{1,0:T(8,128)(2,1)S(1)}, u32[]{:S(2)}, u32[]{:S(2)}) collective-permute-start(bf16[256,256]{1,0:T(8,128)(2,1)S(1)} %fusion.refs_4_), channel_id=1, source_target_pairs={{0,4},{4,0},{1,5},{5,1},{2,6},{6,2},{3,7},{7,3},{8,12},{12,8},{9,1... | collective-permute-start | bytes 393224 | tf_op jit(solution)/shard_map/ppermute | solution.py:38
  88.6 2.5 %collective-permute-start.14 = (bf16[256,256]{1,0:T(8,128)(2,1)S(1)}, bf16[256,256]{1,0:T(8,128)(2,1)S(1)}, u32[]{:S(2)}, u32[]{:S(2)}) collective-permute-start(bf16[256,256]{1,0:T(8,128)(2,1)S(1)} %fusion.1.refs_0_), channel_id=1, source_target_pairs={{0,2},{2,0},{1,3},{3,1},{4,6},{6,4},{5,7},{7,5},{8,10},{10,8},{9,1... | collective-permute-start | bytes 393224 | tf_op jit(solution)/shard_map/ppermute | solution.py:38
  91.1 2.0 %collective-permute-start.17 = (bf16[256,256]{1,0:T(8,128)(2,1)S(1)}, bf16[256,256]{1,0:T(8,128)(2,1)S(1)}, u32[]{:S(2)}, u32[]{:S(2)}) collective-permute-start(bf16[256,256]{1,0:T(8,128)(2,1)S(1)} %fusion.refs_4_), channel_id=1, source_target_pairs={{0,2},{2,0},{1,3},{3,1},{4,6},{6,4},{5,7},{7,5},{8,10},{10,8},{9,1... | collective-permute-start | bytes 393224 | tf_op jit(solution)/shard_map/ppermute | solution.py:38
  93.1 1.6 %collective-permute-done.8.refs_0_ = bf16[256,256]{1,0:T(8,128)(2,1)S(1)} collective-permute-done((bf16[256,256]{1,0:T(8,128)(2,1)S(1)}, bf16[256,256]{1,0:T(8,128)(2,1)S(1)}, u32[]{:S(2)}, u32[]{:S(2)}) %collective-permute-start.8) | collective-permute-done | bytes 131104 | tf_op jit(solution)/shard_map/ppermute | solution.py:38
  96.5 2.8 %collective-permute-done.16.refs_3_ = bf16[256,256]{1,0:T(8,128)(2,1)S(1)} collective-permute-done((bf16[256,256]{1,0:T(8,128)(2,1)S(1)}, bf16[256,256]{1,0:T(8,128)(2,1)S(1)}, u32[]{:S(2)}, u32[]{:S(2)}) %collective-permute-start.16) | collective-permute-done | bytes 131104 | tf_op jit(solution)/shard_map/ppermute | solution.py:38
  99.4 2.7 %collective-permute-done.17.refs_5_ = bf16[256,256]{1,0:T(8,128)(2,1)S(1)} collective-permute-done((bf16[256,256]{1,0:T(8,128)(2,1)S(1)}, bf16[256,256]{1,0:T(8,128)(2,1)S(1)}, u32[]{:S(2)}, u32[]{:S(2)}) %collective-permute-start.17) | collective-permute-done | bytes 131104 | tf_op jit(solution)/shard_map/ppermute | solution.py:38
  103.4 1.4 %shard_map.80 = bf16[512,896]{1,0:T(8,128)(2,1)} custom-call(s32[1]{0:T(128)} %bitcast.lo_ref, s32[1]{0:T(128)} %bitcast.1.group_ref, bf16[256,256]{1,0:T(8,128)(2,1)S(1)} %collective-permute-done.8.refs_0_, bf16[256,256]{1,0:T(8,128)(2,1)S(1)} %collective-permute-done.9.refs_1_, bf16[2,2,2,64,896]{4,3,2,1,0:T(8,128)(2,1)S(1)} %pad_maximum_fusion.1.refs_6_.refs_2_, ...), custom_call_target="tpu_custom_call" | custom-call | flops 234881024 | bytes 4390912 | tf_op jit(solution)/shard_map/pallas_call | solution.py:22
  (54 shorter events, 11.0 us)
Async XLA Ops:
  1.6 1.4 %copy-start.3 = (bf16[128,3584]{1,0:T(8,128)(2,1)S(1)}, bf16[128,3584]{1,0:T(8,128)(2,1)}, u32[]{:S(2)}) copy-start(bf16[128,3584]{1,0:T(8,128)(2,1)} %c_ref.1) | copy-start | bytes 2752516
  1.6 1.4 %copy-start.5 = (s32[128,1]{0,1:T(1,128)S(1)}, s32[128,1]{0,1:T(1,128)}, u32[]{:S(2)}) copy-start(s32[128,1]{0,1:T(1,128)} %param.9) | copy-start | bytes 1540
  1.6 1.4 %copy-start.6 = (f32[128,1]{0,1:T(1,128)S(1)}, f32[128,1]{0,1:T(1,128)}, u32[]{:S(2)}) copy-start(f32[128,1]{0,1:T(1,128)} %param.10) | copy-start | bytes 1540
  4.0 13.5 %collective-permute-start = (bf16[2,2,64,896]{3,2,1,0:T(8,128)(2,1)S(1)}, bf16[2,2,64,896]{3,2,1,0:T(8,128)(2,1)S(1)}, u32[]{:S(2)}, u32[]{:S(2)}) collective-permute-start(bf16[2,2,64,896]{3,2,1,0:T(8,128)(2,1)S(1)} %get-tuple-element.26), channel_id=1, source_target_pairs={{0,8},{8,0},{1,9},{9,1},{2,10},{10,2},{3,11},{11,3},{4,12},{12,4},... | collective-permute-start | bytes 1376264 | tf_op jit(solution)/shard_map/ppermute | solution.py:38
  7.0 42.4 %collective-permute-start.2 = (bf16[896,512]{1,0:T(8,128)(2,1)S(1)}, bf16[896,512]{1,0:T(8,128)(2,1)S(1)}, u32[]{:S(2)}, u32[]{:S(2)}) collective-permute-start(bf16[896,512]{1,0:T(8,128)(2,1)S(1)} %maximum_select_fusion), channel_id=1, source_target_pairs={{0,4},{4,0},{1,5},{5,1},{2,6},{6,2},{3,7},{7,3},{8,12},{12,8},{9,1... | collective-permute-start | bytes 2752520 | tf_op jit(solution)/shard_map/ppermute | solution.py:38
  17.6 21.2 %collective-permute-start.1 = (bf16[2,2,64,896]{3,2,1,0:T(8,128)(2,1)S(1)}, bf16[2,2,64,896]{3,2,1,0:T(8,128)(2,1)S(1)}, u32[]{:S(2)}, u32[]{:S(2)}) collective-permute-start(bf16[2,2,64,896]{3,2,1,0:T(8,128)(2,1)S(1)} %pad_maximum_fusion.2), channel_id=1, source_target_pairs={{0,2},{2,0},{1,3},{3,1},{4,6},{6,4},{5,7},{7,5},{8,10},{10,8},{9,1... | collective-permute-start | bytes 1376264 | tf_op jit(solution)/shard_map/ppermute | solution.py:38
  19.5 29.9 %collective-permute-start.4 = (bf16[2,2,64,896]{3,2,1,0:T(8,128)(2,1)S(1)}, bf16[2,2,64,896]{3,2,1,0:T(8,128)(2,1)S(1)}, u32[]{:S(2)}, u32[]{:S(2)}) collective-permute-start(bf16[2,2,64,896]{3,2,1,0:T(8,128)(2,1)S(1)} %get-tuple-element.32), channel_id=1, source_target_pairs={{0,8},{8,0},{1,9},{9,1},{2,10},{10,2},{3,11},{11,3},{4,12},{12,4},... | collective-permute-start | bytes 1376264 | tf_op jit(solution)/shard_map/ppermute | solution.py:38
  49.4 6.2 %collective-permute-start.3 = (bf16[2,2,2,64,896]{4,3,2,1,0:T(8,128)(2,1)S(1)}, bf16[2,2,2,64,896]{4,3,2,1,0:T(8,128)(2,1)S(1)}, u32[]{:S(2)}, u32[]{:S(2)}) collective-permute-start(bf16[2,2,2,64,896]{4,3,2,1,0:T(8,128)(2,1)S(1)} %pad_maximum_fusion.own_ref), channel_id=1, source_target_pairs={{0,1},{1,0},{2,3},{3,2},{4,5},{5,4},{6,7},{7,6},{8,9},{9,8},{10,11... | collective-permute-start | bytes 2752520 | tf_op jit(solution)/shard_map/ppermute | solution.py:38
  49.5 6.1 %copy-start = (bf16[1,896,512]{2,1,0:T(8,128)(2,1)S(1)}, bf16[1,896,512]{2,1,0:T(8,128)(2,1)}, u32[]{:S(2)}) copy-start(bf16[1,896,512]{2,1,0:T(8,128)(2,1)} %param.11) | copy-start | bytes 2752516
  49.5 6.1 %copy-start.1 = (bf16[1,896,512]{2,1,0:T(8,128)(2,1)S(1)}, bf16[1,896,512]{2,1,0:T(8,128)(2,1)}, u32[]{:S(2)}) copy-start(bf16[1,896,512]{2,1,0:T(8,128)(2,1)} %param.12) | copy-start | bytes 2752516
  49.7 10.4 %collective-permute-start.12 = (bf16[2,64,896]{2,1,0:T(8,128)(2,1)S(1)}, bf16[2,64,896]{2,1,0:T(8,128)(2,1)S(1)}, u32[]{:S(2)}, u32[]{:S(2)}) collective-permute-start(bf16[2,64,896]{2,1,0:T(8,128)(2,1)S(1)} %pad_maximum_fusion.6), channel_id=1, source_target_pairs={{0,6},{2,4},{4,2},{6,0},{1,7},{3,5},{5,3},{7,1},{8,14},{10,12},{12... | collective-permute-start | bytes 688136 | tf_op jit(solution)/shard_map/ppermute | solution.py:261
  53.2 19.5 %collective-permute-start.11 = (bf16[2,64,896]{2,1,0:T(8,128)(2,1)S(1)}, bf16[2,64,896]{2,1,0:T(8,128)(2,1)S(1)}, u32[]{:S(2)}, u32[]{:S(2)}) collective-permute-start(bf16[2,64,896]{2,1,0:T(8,128)(2,1)S(1)} %pad_maximum_fusion.5), channel_id=1, source_target_pairs={{0,4},{2,6},{4,0},{6,2},{1,5},{3,7},{5,1},{7,3},{8,12},{10,14},{12... | collective-permute-start | bytes 688136 | tf_op jit(solution)/shard_map/ppermute | solution.py:261
  53.2 22.5 %collective-permute-start.6 = (bf16[896,512]{1,0:T(8,128)(2,1)S(1)}, bf16[896,512]{1,0:T(8,128)(2,1)S(1)}, u32[]{:S(2)}, u32[]{:S(2)}) collective-permute-start(bf16[896,512]{1,0:T(8,128)(2,1)S(1)} %collective-permute-done.2.refs_0_), channel_id=1, source_target_pairs={{0,16},{16,0},{1,17},{17,1},{2,18},{18,2},{3,19},{19,3},{4,20},{20... | collective-permute-start | bytes 2752520 | tf_op jit(solution)/shard_map/ppermute | solution.py:38
  54.7 18.0 %collective-permute-start.10 = (bf16[2,64,896]{2,1,0:T(8,128)(2,1)S(1)}, bf16[2,64,896]{2,1,0:T(8,128)(2,1)S(1)}, u32[]{:S(2)}, u32[]{:S(2)}) collective-permute-start(bf16[2,64,896]{2,1,0:T(8,128)(2,1)S(1)} %pad_maximum_fusion.4), channel_id=1, source_target_pairs={{0,2},{2,0},{4,6},{6,4},{1,3},{3,1},{5,7},{7,5},{8,10},{10,8},{12,... | collective-permute-start | bytes 688136 | tf_op jit(solution)/shard_map/ppermute | solution.py:261
  57.3 17.7 %collective-permute-start.5 = (bf16[256,512]{1,0:T(8,128)(2,1)S(1)}, bf16[256,512]{1,0:T(8,128)(2,1)S(1)}, u32[]{:S(2)}, u32[]{:S(2)}) collective-permute-start(bf16[256,512]{1,0:T(8,128)(2,1)S(1)} %shard_map.76), channel_id=1, source_target_pairs={{0,2},{2,0},{1,3},{3,1},{4,6},{6,4},{5,7},{7,5},{8,10},{10,8},{9,1... | collective-permute-start | bytes 786440 | tf_op jit(solution)/shard_map/ppermute | solution.py:38
  76.1 10.7 %collective-permute-start.7 = (bf16[256,512]{1,0:T(8,128)(2,1)S(1)}, bf16[256,512]{1,0:T(8,128)(2,1)S(1)}, u32[]{:S(2)}, u32[]{:S(2)}) collective-permute-start(bf16[256,512]{1,0:T(8,128)(2,1)S(1)} %shard_map.78), channel_id=1, source_target_pairs={{0,2},{2,0},{1,3},{3,1},{4,6},{6,4},{5,7},{7,5},{8,10},{10,8},{9,1... | collective-permute-start | bytes 786440 | tf_op jit(solution)/shard_map/ppermute | solution.py:38
  77.5 18.0 %collective-permute-start.13 = (bf16[2,2,2,64,896]{4,3,2,1,0:T(8,128)(2,1)S(1)}, bf16[2,2,2,64,896]{4,3,2,1,0:T(8,128)(2,1)S(1)}, u32[]{:S(2)}, u32[]{:S(2)}) collective-permute-start(bf16[2,2,2,64,896]{4,3,2,1,0:T(8,128)(2,1)S(1)} %pad_maximum_fusion.1.refs_6_.refs_2_), channel_id=1, source_target_pairs={{0,1},{1,0},{2,3},{3,2},{4,5},{5,4},{6,7},{7,6},{8,9},{9,8},{10,11... | collective-permute-start | bytes 2752520 | tf_op jit(solution)/shard_map/ppermute | solution.py:38
  77.6 13.5 %collective-permute-start.15 = (bf16[256,256]{1,0:T(8,128)(2,1)S(1)}, bf16[256,256]{1,0:T(8,128)(2,1)S(1)}, u32[]{:S(2)}, u32[]{:S(2)}) collective-permute-start(bf16[256,256]{1,0:T(8,128)(2,1)S(1)} %fusion.1.refs_0_), channel_id=1, source_target_pairs={{0,4},{4,0},{1,5},{5,1},{2,6},{6,2},{3,7},{7,3},{8,12},{12,8},{9,1... | collective-permute-start | bytes 393224 | tf_op jit(solution)/shard_map/ppermute | solution.py:38
  80.5 21.5 %copy-start.4 = (bf16[1,512,896]{2,1,0:T(8,128)(2,1)S(1)}, bf16[1,512,896]{2,1,0:T(8,128)(2,1)}, u32[]{:S(2)}) copy-start(bf16[1,512,896]{2,1,0:T(8,128)(2,1)} %param.13) | copy-start | bytes 2752516
  87.0 7.7 %collective-permute-start.8 = (bf16[256,256]{1,0:T(8,128)(2,1)S(1)}, bf16[256,256]{1,0:T(8,128)(2,1)S(1)}, u32[]{:S(2)}, u32[]{:S(2)}) collective-permute-start(bf16[256,256]{1,0:T(8,128)(2,1)S(1)} %fusion.refs_4_), channel_id=1, source_target_pairs={{0,4},{4,0},{1,5},{5,1},{2,6},{6,2},{3,7},{7,3},{8,12},{12,8},{9,1... | collective-permute-start | bytes 393224 | tf_op jit(solution)/shard_map/ppermute | solution.py:38
  88.6 7.9 %collective-permute-start.14 = (bf16[256,256]{1,0:T(8,128)(2,1)S(1)}, bf16[256,256]{1,0:T(8,128)(2,1)S(1)}, u32[]{:S(2)}, u32[]{:S(2)}) collective-permute-start(bf16[256,256]{1,0:T(8,128)(2,1)S(1)} %fusion.1.refs_0_), channel_id=1, source_target_pairs={{0,2},{2,0},{1,3},{3,1},{4,6},{6,4},{5,7},{7,5},{8,10},{10,8},{9,1... | collective-permute-start | bytes 393224 | tf_op jit(solution)/shard_map/ppermute | solution.py:38
  91.1 8.3 %collective-permute-start.16 = (bf16[256,256]{1,0:T(8,128)(2,1)S(1)}, bf16[256,256]{1,0:T(8,128)(2,1)S(1)}, u32[]{:S(2)}, u32[]{:S(2)}) collective-permute-start(bf16[256,256]{1,0:T(8,128)(2,1)S(1)} %collective-permute-done.15.refs_2_), channel_id=1, source_target_pairs={{0,2},{2,0},{1,3},{3,1},{4,6},{6,4},{5,7},{7,5},{8,10},{10,8},{9,1... | collective-permute-start | bytes 393224 | tf_op jit(solution)/shard_map/ppermute | solution.py:38
  91.1 10.9 %collective-permute-start.17 = (bf16[256,256]{1,0:T(8,128)(2,1)S(1)}, bf16[256,256]{1,0:T(8,128)(2,1)S(1)}, u32[]{:S(2)}, u32[]{:S(2)}) collective-permute-start(bf16[256,256]{1,0:T(8,128)(2,1)S(1)} %fusion.refs_4_), channel_id=1, source_target_pairs={{0,2},{2,0},{1,3},{3,1},{4,6},{6,4},{5,7},{7,5},{8,10},{10,8},{9,1... | collective-permute-start | bytes 393224 | tf_op jit(solution)/shard_map/ppermute | solution.py:38
  94.7 8.7 %collective-permute-start.9 = (bf16[256,256]{1,0:T(8,128)(2,1)S(1)}, bf16[256,256]{1,0:T(8,128)(2,1)S(1)}, u32[]{:S(2)}, u32[]{:S(2)}) collective-permute-start(bf16[256,256]{1,0:T(8,128)(2,1)S(1)} %collective-permute-done.8.refs_0_), channel_id=1, source_target_pairs={{0,2},{2,0},{1,3},{3,1},{4,6},{6,4},{5,7},{7,5},{8,10},{10,8},{9,1... | collective-permute-start | bytes 393224 | tf_op jit(solution)/shard_map/ppermute | solution.py:38
  (1 other events, 1.2 us)

commit v6 on v5

--- a/solution.py
+++ b/solution.py
@@ -9,7 +9,6 @@
 from jax.sharding import PartitionSpec as P
 
 
-CUT = 100000
 KERNEL = pltpu.CompilerParams(vmem_limit_bytes=40 << 20)
 SMEM = pl.BlockSpec(memory_space=pltpu.SMEM)
 WHOLE = pl.BlockSpec()
@@ -36,6 +35,46 @@
 def swapped(value, axis, distance=1):
     pairs = [(s, s ^ distance) for s in range(lax.axis_size(axis))]
     return lax.ppermute(value, axis, pairs)
+
+
+def pick_kernel(group_ref, gate_hbm, up_hbm, out_hbm, held, in_sems, out_sems):
+    half = gate_hbm.shape[1] // 2
+    count = gate_hbm.shape[0] // 2
+    cols = pl.ds(pl.multiple_of(group_ref[0] * half, half), half)
+    loads, stores = [], []
+    for part in range(2):
+        rows = pl.ds(part * count, count)
+        for place, source in enumerate((gate_hbm, up_hbm)):
+            target = held.at[rows, pl.ds(place * half, half)]
+            loads.append(
+                pltpu.make_async_copy(source.at[rows, cols], target, in_sems.at[part, place])
+            )
+        stores.append(pltpu.make_async_copy(held.at[rows], out_hbm.at[rows], out_sems.at[part]))
+    for copy in loads:
+        copy.start()
+    for part in range(2):
+        loads[2 * part].wait()
+        loads[2 * part + 1].wait()
+        stores[part].start()
+    for copy in stores:
+        copy.wait()
+
+
+def pick_weights(group, gate, up):
+    far = pl.BlockSpec(memory_space=pltpu.HBM)
+    return pl.pallas_call(
+        pick_kernel,
+        out_shape=shape(gate.shape, BF16),
+        in_specs=[SMEM, far, far],
+        out_specs=far,
+        scratch_shapes=[
+            pltpu.VMEM(gate.shape, BF16),
+            pltpu.SemaphoreType.DMA((2, 2)),
+            pltpu.SemaphoreType.DMA((2,)),
+        ],
+        compiler_params=pltpu.CompilerParams(vmem_limit_bytes=63 << 20),
+        cost_estimate=pl.CostEstimate(flops=0, bytes_accessed=4 * gate.size, transcendentals=0),
+    )(group, gate, up)
 
 
 def dispatch_kernel(nodes, side, capacity, node_ref, hi_ref, lo_ref, ids_ref, gate_ref, x_ref, c_ref, *out_refs):
@@ -207,13 +246,8 @@
     gate_own, up_own = w_gate[0], w_up[0]
     half = gate_own.shape[1] // 2
     width = gate_own.shape[0]
-    cuts = (0, CUT, width) if width > CUT else (0, width)
-    pieces = []
-    for rows in (slice(*pair) for pair in zip(cuts, cuts[1:])):
-        left = jnp.concatenate([gate_own[rows, :half], up_own[rows, :half]], axis=1)
-        right = jnp.concatenate([gate_own[rows, half:], up_own[rows, half:]], axis=1)
-        pieces.append(jnp.where(group[0] == 0, left, right))
-    tokens, pieces = lax.optimization_barrier((tokens, pieces))
+    cuts = (0, width)
+    pieces = [pick_weights(group, gate_own, up_own)]
     mine = [swapped(piece, "hi") for piece in pieces]
     theirs = [swapped(piece, "groups") for piece in mine[:-1]]
 
@@ -242,11 +276,15 @@
         corners = [swapped(across, "lo", d) for d in range(1, side)]
         return [hidden, *beside, across, *corners]
 
-    x = [send_x[0]] + [swapped(send_x[d], "node", d) for d in range(1, nodes)]
-    x = [jnp.stack([part[d] for part in x]) for d in range(side)]
     y = [send_y[0]] + [swapped(send_y[d], "node", d) for d in range(1, nodes)]
     y = [[jnp.stack([part[h, l] for part in y]) for l in range(side)] for h in range(2)]
-    own_x = jnp.stack([x[0]] + [swapped(x[d], "lo", d) for d in range(1, side)])
+    x = [[send_x[n][d] for n in range(nodes)] for d in range(side)]
+    for d in range(side):
+        for n in range(nodes):
+            if (n, d) != (0, 0):
+                pairs = [(s, s ^ (n * side + d)) for s in range(nodes * side)]
+                x[d][n] = lax.ppermute(x[d][n], ("node", "lo"), pairs)
+    own_x = jnp.stack([jnp.stack(rows) for rows in x])
     own_x, mine[-1] = lax.optimization_barrier((own_x, mine[-1]))
     other_x = swapped(own_x, "rep")
     acc_mine, acc_theirs = partial_first(lo, group, own_x, other_x, gate_own, up_own, nodes, side)

time: 105 us -> 102 us (0.971)
  waiting for transfers between devices: 67.3 us -> 62.8 us
  Pallas kernels: 6.37 us -> 8.53 us
    ppermute x15 -> x13, waiting for transfers between devices: 53.2 us -> 26.9 us  [swapped(): return lax.ppermute(value, axis, pairs)]
    ppermute x0 -> x3, waiting for transfers between devices: none -> 21.7 us  [local(): x[d][n] = lax.ppermute(x[d][n], ('node', 'lo'), pairs)]
    ppermute x0 -> x3, starting transfers between devices: none -> 3.62 us  [local(): x[d][n] = lax.ppermute(x[d][n], ('node', 'lo'), pairs)]
    ppermute x15 -> x13, starting transfers between devices: 22.4 us -> 19.4 us  [swapped(): return lax.ppermute(value, axis, pairs)]
    pallas_call x0 -> x1, Pallas kernels: none -> 2.17 us  [pick_weights(): pl.pallas_call(pick_kernel, out_shape=shape(gate.shape, BF16), in_specs=[...]
    slice x3 -> x1, local copies, waits for them, and re-layouts: 1.63 us -> 0.04 us  [local(): x = [[send_x[n][d] for n in range(nodes)] for d in range(side)]]
  transfers between devices with their start and end apart: 18 -> 19, of which waited for: 13 -> 13; matrix products, arithmetic and copies ran while one was open for 1% -> 1% of each run, Pallas kernels for 3% -> 4%
where the time goes in v6:
time: 102 us
  waiting for transfers between devices  62.8 us (62%)
  starting transfers between devices  27.5 us (27%)
  Pallas kernels  8.53 us (8%)
  local copies, waits for them, and re-layouts  2.02 us (2%)
    ppermute x13, waiting for transfers between devices, swapped(): return lax.ppermute(value, axis, pairs)  26.9 us
    ppermute x3, waiting for transfers between devices, local(): x[d][n] = lax.ppermute(x[d][n], ('node', 'lo'), pairs)  21.7 us
    ppermute x13, starting transfers between devices, swapped(): return lax.ppermute(value, axis, pairs)  19.4 us
    ppermute x3, waiting for transfers between devices, local(): y[h][l] = lax.ppermute(y[h][l], ('hi', 'lo'), pairs)  14.3 us
    pallas_call x8, Pallas kernels, call(): pl.pallas_call(kernel, out_shape=outs, in_specs=[SMEM] * len(scalars) + [...  6.36 us
    ppermute x3, starting transfers between devices, local(): y[h][l] = lax.ppermute(y[h][l], ('hi', 'lo'), pairs)  4.5 us
    ppermute x3, starting transfers between devices, local(): x[d][n] = lax.ppermute(x[d][n], ('node', 'lo'), pairs)  3.62 us
    pallas_call x1, Pallas kernels, pick_weights(): pl.pallas_call(pick_kernel, out_shape=shape(gate.shape, BF16), in_specs=[...  2.17 us
  transfers between devices with their start and end apart: 19, of which 13 were waited for; matrix products, arithmetic and copies ran while one was open for 1% of the time, Pallas kernels for 4%

profile of v6, /device:TPU:0, one launch (start us, length us, event | category | flops | bytes accessed | tf_op | source)
XLA Modules:
  0.0 101.9 jit_solution(17722579401326881861)
XLA Ops:
  0.0 2.2 %shard_map.74 = bf16[896,512]{1,0:T(8,128)(2,1)} custom-call(s32[1]{0:T(128)} %bitcast.1.group_ref, bf16[896,512]{1,0:T(8,128)(2,1)} %bitcast.47, bf16[896,512]{1,0:T(8,128)(2,1)} %bitcast.49), custom_call_target="tpu_custom_call" | custom-call | bytes 1835008 | tf_op jit(solution)/shard_map/pallas_call | solution.py:65
  2.2 4.1 %collective-permute-start.3 = (bf16[896,512]{1,0:T(8,128)(2,1)}, bf16[896,512]{1,0:T(8,128)(2,1)S(1)}, u32[]{:S(2)}, u32[]{:S(2)}) collective-permute-start(bf16[896,512]{1,0:T(8,128)(2,1)} %shard_map.74), channel_id=1, source_target_pairs={{0,4},{4,0},{1,5},{5,1},{2,6},{6,2},{3,7},{7,3},{8,12},{12,8},{9,1... | collective-permute-start | bytes 2752520 | tf_op jit(solution)/shard_map/ppermute | solution.py:37
  9.2 2.6 %collective-permute-start.2 = (bf16[2,64,896]{2,1,0:T(8,128)(2,1)S(1)}, bf16[2,64,896]{2,1,0:T(8,128)(2,1)S(1)}, u32[]{:S(2)}, u32[]{:S(2)}) collective-permute-start(bf16[2,64,896]{2,1,0:T(8,128)(2,1)S(1)} %get-tuple-element.50), channel_id=1, source_target_pairs={{0,10},{2,8},{8,2},{10,0},{1,11},{3,9},{9,3},{11,1},{4,14},{6,12},... | collective-permute-start | bytes 688136 | tf_op jit(solution)/shard_map/ppermute | solution.py:286
  12.8 1.5 %collective-permute-start.5 = (bf16[2,2,64,896]{3,2,1,0:T(8,128)(2,1)S(1)}, bf16[2,2,64,896]{3,2,1,0:T(8,128)(2,1)S(1)}, u32[]{:S(2)}, u32[]{:S(2)}) collective-permute-start(bf16[2,2,64,896]{3,2,1,0:T(8,128)(2,1)S(1)} %get-tuple-element.28), channel_id=1, source_target_pairs={{0,8},{8,0},{1,9},{9,1},{2,10},{10,2},{3,11},{11,3},{4,12},{12,4},... | collective-permute-start | bytes 1376264 | tf_op jit(solution)/shard_map/ppermute | solution.py:37
  14.3 17.9 %collective-permute-done.2 = bf16[2,64,896]{2,1,0:T(8,128)(2,1)S(1)} collective-permute-done((bf16[2,64,896]{2,1,0:T(8,128)(2,1)S(1)}, bf16[2,64,896]{2,1,0:T(8,128)(2,1)S(1)}, u32[]{:S(2)}, u32[]{:S(2)}) %collective-permute-start.2) | collective-permute-done | bytes 229408 | tf_op jit(solution)/shard_map/ppermute | solution.py:286
  32.2 3.8 %collective-permute-done.1 = bf16[2,64,896]{2,1,0:T(8,128)(2,1)S(1)} collective-permute-done((bf16[2,64,896]{2,1,0:T(8,128)(2,1)S(1)}, bf16[2,64,896]{2,1,0:T(8,128)(2,1)S(1)}, u32[]{:S(2)}, u32[]{:S(2)}) %collective-permute-start.1) | collective-permute-done | bytes 229408 | tf_op jit(solution)/shard_map/ppermute | solution.py:286
  36.2 10.3 %collective-permute-done.3.refs_0_ = bf16[896,512]{1,0:T(8,128)(2,1)S(1)} collective-permute-done((bf16[896,512]{1,0:T(8,128)(2,1)}, bf16[896,512]{1,0:T(8,128)(2,1)S(1)}, u32[]{:S(2)}, u32[]{:S(2)}) %collective-permute-start.3) | collective-permute-done | bytes 917536 | tf_op jit(solution)/shard_map/ppermute | solution.py:37
  46.7 3.6 %collective-permute-start.13 = (bf16[2,64,896]{2,1,0:T(8,128)(2,1)S(1)}, bf16[2,64,896]{2,1,0:T(8,128)(2,1)S(1)}, u32[]{:S(2)}, u32[]{:S(2)}) collective-permute-start(bf16[2,64,896]{2,1,0:T(8,128)(2,1)S(1)} %get-tuple-element.35), channel_id=1, source_target_pairs={{0,6},{2,4},{4,2},{6,0},{1,7},{3,5},{5,3},{7,1},{8,14},{10,12},{12... | collective-permute-start | bytes 688136 | tf_op jit(solution)/shard_map/ppermute | solution.py:299
  50.4 1.5 %collective-permute-start.7 = (bf16[896,512]{1,0:T(8,128)(2,1)S(1)}, bf16[896,512]{1,0:T(8,128)(2,1)S(1)}, u32[]{:S(2)}, u32[]{:S(2)}) collective-permute-start(bf16[896,512]{1,0:T(8,128)(2,1)S(1)} %collective-permute-done.3.refs_0_), channel_id=1, source_target_pairs={{0,16},{16,0},{1,17},{17,1},{2,18},{18,2},{3,19},{19,3},{4,20},{20... | collective-permute-start | bytes 2752520 | tf_op jit(solution)/shard_map/ppermute | solution.py:37
  52.8 1.2 %shard_map.75 = (f32[2,256,512]{2,1,0:T(8,128)S(1)}, f32[2,256,512]{2,1,0:T(8,128)S(1)}) custom-call(s32[1]{0:T(128)} %bitcast.lo_ref, s32[1]{0:T(128)} %bitcast.1.group_ref, bf16[2,2,2,64,896]{4,3,2,1,0:T(8,128)(2,1)S(1)} %pad_maximum_fusion.own_ref, bf16[2,2,2,64,896]{4,3,2,1,0:T(8,128)(2,1)S(1)} %collective-permute-done.4.other_ref, ...), custom_call_target="tpu_custom_call" | custom-call | flops 939524096 | bytes 5767168 | tf_op jit(solution)/shard_map/pallas_call | solution.py:21
  54.5 1.2 %collective-permute-start.6 = (bf16[256,512]{1,0:T(8,128)(2,1)S(1)}, bf16[256,512]{1,0:T(8,128)(2,1)S(1)}, u32[]{:S(2)}, u32[]{:S(2)}) collective-permute-start(bf16[256,512]{1,0:T(8,128)(2,1)S(1)} %shard_map.77), channel_id=1, source_target_pairs={{0,2},{2,0},{1,3},{3,1},{4,6},{6,4},{5,7},{7,5},{8,10},{10,8},{9,1... | collective-permute-start | bytes 786440 | tf_op jit(solution)/shard_map/ppermute | solution.py:37
  55.7 1.5 %collective-permute-done.13 = bf16[2,64,896]{2,1,0:T(8,128)(2,1)S(1)} collective-permute-done((bf16[2,64,896]{2,1,0:T(8,128)(2,1)S(1)}, bf16[2,64,896]{2,1,0:T(8,128)(2,1)S(1)}, u32[]{:S(2)}, u32[]{:S(2)}) %collective-permute-start.13) | collective-permute-done | bytes 229408 | tf_op jit(solution)/shard_map/ppermute | solution.py:299
  57.2 12.8 %collective-permute-done.12 = bf16[2,64,896]{2,1,0:T(8,128)(2,1)S(1)} collective-permute-done((bf16[2,64,896]{2,1,0:T(8,128)(2,1)S(1)}, bf16[2,64,896]{2,1,0:T(8,128)(2,1)S(1)}, u32[]{:S(2)}, u32[]{:S(2)}) %collective-permute-start.12) | collective-permute-done | bytes 229408 | tf_op jit(solution)/shard_map/ppermute | solution.py:299
  70.5 1.7 %collective-permute-done.6 = bf16[256,512]{1,0:T(8,128)(2,1)S(1)} collective-permute-done((bf16[256,512]{1,0:T(8,128)(2,1)S(1)}, bf16[256,512]{1,0:T(8,128)(2,1)S(1)}, u32[]{:S(2)}, u32[]{:S(2)}) %collective-permute-start.6) | collective-permute-done | bytes 262176 | tf_op jit(solution)/shard_map/ppermute | solution.py:37
  73.3 1.3 %collective-permute-start.8 = (bf16[256,512]{1,0:T(8,128)(2,1)S(1)}, bf16[256,512]{1,0:T(8,128)(2,1)S(1)}, u32[]{:S(2)}, u32[]{:S(2)}) collective-permute-start(bf16[256,512]{1,0:T(8,128)(2,1)S(1)} %shard_map.79), channel_id=1, source_target_pairs={{0,2},{2,0},{1,3},{3,1},{4,6},{6,4},{5,7},{7,5},{8,10},{10,8},{9,1... | collective-permute-start | bytes 786440 | tf_op jit(solution)/shard_map/ppermute | solution.py:37
  74.8 2.4 %collective-permute-start.16 = (bf16[256,256]{1,0:T(8,128)(2,1)S(1)}, bf16[256,256]{1,0:T(8,128)(2,1)S(1)}, u32[]{:S(2)}, u32[]{:S(2)}) collective-permute-start(bf16[256,256]{1,0:T(8,128)(2,1)S(1)} %fusion.1.refs_0_), channel_id=1, source_target_pairs={{0,4},{4,0},{1,5},{5,1},{2,6},{6,2},{3,7},{7,3},{8,12},{12,8},{9,1... | collective-permute-start | bytes 393224 | tf_op jit(solution)/shard_map/ppermute | solution.py:37
  77.7 6.2 %collective-permute-done.8 = bf16[256,512]{1,0:T(8,128)(2,1)S(1)} collective-permute-done((bf16[256,512]{1,0:T(8,128)(2,1)S(1)}, bf16[256,512]{1,0:T(8,128)(2,1)S(1)}, u32[]{:S(2)}, u32[]{:S(2)}) %collective-permute-start.8) | collective-permute-done | bytes 262176 | tf_op jit(solution)/shard_map/ppermute | solution.py:37
  84.1 1.7 %collective-permute-start.9 = (bf16[256,256]{1,0:T(8,128)(2,1)S(1)}, bf16[256,256]{1,0:T(8,128)(2,1)S(1)}, u32[]{:S(2)}, u32[]{:S(2)}) collective-permute-start(bf16[256,256]{1,0:T(8,128)(2,1)S(1)} %fusion.refs_4_), channel_id=1, source_target_pairs={{0,4},{4,0},{1,5},{5,1},{2,6},{6,2},{3,7},{7,3},{8,12},{12,8},{9,1... | collective-permute-start | bytes 393224 | tf_op jit(solution)/shard_map/ppermute | solution.py:37
  85.7 2.5 %collective-permute-start.15 = (bf16[256,256]{1,0:T(8,128)(2,1)S(1)}, bf16[256,256]{1,0:T(8,128)(2,1)S(1)}, u32[]{:S(2)}, u32[]{:S(2)}) collective-permute-start(bf16[256,256]{1,0:T(8,128)(2,1)S(1)} %fusion.1.refs_0_), channel_id=1, source_target_pairs={{0,2},{2,0},{1,3},{3,1},{4,6},{6,4},{5,7},{7,5},{8,10},{10,8},{9,1... | collective-permute-start | bytes 393224 | tf_op jit(solution)/shard_map/ppermute | solution.py:37
  88.3 2.0 %collective-permute-start.18 = (bf16[256,256]{1,0:T(8,128)(2,1)S(1)}, bf16[256,256]{1,0:T(8,128)(2,1)S(1)}, u32[]{:S(2)}, u32[]{:S(2)}) collective-permute-start(bf16[256,256]{1,0:T(8,128)(2,1)S(1)} %fusion.refs_4_), channel_id=1, source_target_pairs={{0,2},{2,0},{1,3},{3,1},{4,6},{6,4},{5,7},{7,5},{8,10},{10,8},{9,1... | collective-permute-start | bytes 393224 | tf_op jit(solution)/shard_map/ppermute | solution.py:37
  90.3 1.3 %collective-permute-done.9.refs_0_ = bf16[256,256]{1,0:T(8,128)(2,1)S(1)} collective-permute-done((bf16[256,256]{1,0:T(8,128)(2,1)S(1)}, bf16[256,256]{1,0:T(8,128)(2,1)S(1)}, u32[]{:S(2)}, u32[]{:S(2)}) %collective-permute-start.9) | collective-permute-done | bytes 131104 | tf_op jit(solution)/shard_map/ppermute | solution.py:37
  93.6 2.8 %collective-permute-done.17.refs_3_ = bf16[256,256]{1,0:T(8,128)(2,1)S(1)} collective-permute-done((bf16[256,256]{1,0:T(8,128)(2,1)S(1)}, bf16[256,256]{1,0:T(8,128)(2,1)S(1)}, u32[]{:S(2)}, u32[]{:S(2)}) %collective-permute-start.17) | collective-permute-done | bytes 131104 | tf_op jit(solution)/shard_map/ppermute | solution.py:37
  96.4 2.8 %collective-permute-done.18.refs_5_ = bf16[256,256]{1,0:T(8,128)(2,1)S(1)} collective-permute-done((bf16[256,256]{1,0:T(8,128)(2,1)S(1)}, bf16[256,256]{1,0:T(8,128)(2,1)S(1)}, u32[]{:S(2)}, u32[]{:S(2)}) %collective-permute-start.18) | collective-permute-done | bytes 131104 | tf_op jit(solution)/shard_map/ppermute | solution.py:37
  100.5 1.4 %shard_map.81 = bf16[512,896]{1,0:T(8,128)(2,1)} custom-call(s32[1]{0:T(128)} %bitcast.lo_ref, s32[1]{0:T(128)} %bitcast.1.group_ref, bf16[256,256]{1,0:T(8,128)(2,1)S(1)} %collective-permute-done.9.refs_0_, bf16[256,256]{1,0:T(8,128)(2,1)S(1)} %collective-permute-done.10.refs_1_, bf16[2,2,2,64,896]{4,3,2,1,0:T(8,128)(2,1)S(1)} %pad_maximum_fusion.1.refs_6_.refs_2_, ...), custom_call_target="tpu_custom_call" | custom-call | flops 234881024 | bytes 4390912 | tf_op jit(solution)/shard_map/pallas_call | solution.py:21
  (53 shorter events, 11.4 us)
Async XLA Ops:
  0.0 6.3 %copy-start.2 = (bf16[128,3584]{1,0:T(8,128)(2,1)S(1)}, bf16[128,3584]{1,0:T(8,128)(2,1)}, u32[]{:S(2)}) copy-start(bf16[128,3584]{1,0:T(8,128)(2,1)} %x_ref.1) | copy-start | bytes 2752516
  2.2 44.3 %collective-permute-start.3 = (bf16[896,512]{1,0:T(8,128)(2,1)}, bf16[896,512]{1,0:T(8,128)(2,1)S(1)}, u32[]{:S(2)}, u32[]{:S(2)}) collective-permute-start(bf16[896,512]{1,0:T(8,128)(2,1)} %shard_map.74), channel_id=1, source_target_pairs={{0,4},{4,0},{1,5},{5,1},{2,6},{6,2},{3,7},{7,3},{8,12},{12,8},{9,1... | collective-permute-start | bytes 2752520 | tf_op jit(solution)/shard_map/ppermute | solution.py:37
  7.0 1.2 %copy-start.3 = (bf16[128,3584]{1,0:T(8,128)(2,1)S(1)}, bf16[128,3584]{1,0:T(8,128)(2,1)}, u32[]{:S(2)}) copy-start(bf16[128,3584]{1,0:T(8,128)(2,1)} %c_ref.1) | copy-start | bytes 2752516
  9.2 23.1 %collective-permute-start.2 = (bf16[2,64,896]{2,1,0:T(8,128)(2,1)S(1)}, bf16[2,64,896]{2,1,0:T(8,128)(2,1)S(1)}, u32[]{:S(2)}, u32[]{:S(2)}) collective-permute-start(bf16[2,64,896]{2,1,0:T(8,128)(2,1)S(1)} %get-tuple-element.50), channel_id=1, source_target_pairs={{0,10},{2,8},{8,2},{10,0},{1,11},{3,9},{9,3},{11,1},{4,14},{6,12},... | collective-permute-start | bytes 688136 | tf_op jit(solution)/shard_map/ppermute | solution.py:286
  11.8 24.2 %collective-permute-start.1 = (bf16[2,64,896]{2,1,0:T(8,128)(2,1)S(1)}, bf16[2,64,896]{2,1,0:T(8,128)(2,1)S(1)}, u32[]{:S(2)}, u32[]{:S(2)}) collective-permute-start(bf16[2,64,896]{2,1,0:T(8,128)(2,1)S(1)} %get-tuple-element.48), channel_id=1, source_target_pairs={{0,2},{2,0},{8,10},{10,8},{1,3},{3,1},{9,11},{11,9},{4,6},{6,4},{1... | collective-permute-start | bytes 688136 | tf_op jit(solution)/shard_map/ppermute | solution.py:286
  12.3 23.8 %collective-permute-start = (bf16[2,64,896]{2,1,0:T(8,128)(2,1)S(1)}, bf16[2,64,896]{2,1,0:T(8,128)(2,1)S(1)}, u32[]{:S(2)}, u32[]{:S(2)}) collective-permute-start(bf16[2,64,896]{2,1,0:T(8,128)(2,1)S(1)} %get-tuple-element.49), channel_id=1, source_target_pairs={{0,8},{2,10},{8,0},{10,2},{1,9},{3,11},{9,1},{11,3},{4,12},{6,14},... | collective-permute-start | bytes 688136 | tf_op jit(solution)/shard_map/ppermute | solution.py:286
  12.8 33.7 %collective-permute-start.5 = (bf16[2,2,64,896]{3,2,1,0:T(8,128)(2,1)S(1)}, bf16[2,2,64,896]{3,2,1,0:T(8,128)(2,1)S(1)}, u32[]{:S(2)}, u32[]{:S(2)}) collective-permute-start(bf16[2,2,64,896]{3,2,1,0:T(8,128)(2,1)S(1)} %get-tuple-element.28), channel_id=1, source_target_pairs={{0,8},{8,0},{1,9},{9,1},{2,10},{10,2},{3,11},{11,3},{4,12},{12,4},... | collective-permute-start | bytes 1376264 | tf_op jit(solution)/shard_map/ppermute | solution.py:37
  46.5 6.3 %collective-permute-start.4 = (bf16[2,2,2,64,896]{4,3,2,1,0:T(8,128)(2,1)S(1)}, bf16[2,2,2,64,896]{4,3,2,1,0:T(8,128)(2,1)S(1)}, u32[]{:S(2)}, u32[]{:S(2)}) collective-permute-start(bf16[2,2,2,64,896]{4,3,2,1,0:T(8,128)(2,1)S(1)} %pad_maximum_fusion.own_ref), channel_id=1, source_target_pairs={{0,1},{1,0},{2,3},{3,2},{4,5},{5,4},{6,7},{7,6},{8,9},{9,8},{10,11... | collective-permute-start | bytes 2752520 | tf_op jit(solution)/shard_map/ppermute | solution.py:37
  46.6 6.2 %copy-start = (bf16[1,896,512]{2,1,0:T(8,128)(2,1)S(1)}, bf16[1,896,512]{2,1,0:T(8,128)(2,1)}, u32[]{:S(2)}) copy-start(bf16[1,896,512]{2,1,0:T(8,128)(2,1)} %param.11) | copy-start | bytes 2752516
  46.6 6.2 %copy-start.1 = (bf16[1,896,512]{2,1,0:T(8,128)(2,1)S(1)}, bf16[1,896,512]{2,1,0:T(8,128)(2,1)}, u32[]{:S(2)}) copy-start(bf16[1,896,512]{2,1,0:T(8,128)(2,1)} %param.12) | copy-start | bytes 2752516
  46.7 10.4 %collective-permute-start.13 = (bf16[2,64,896]{2,1,0:T(8,128)(2,1)S(1)}, bf16[2,64,896]{2,1,0:T(8,128)(2,1)S(1)}, u32[]{:S(2)}, u32[]{:S(2)}) collective-permute-start(bf16[2,64,896]{2,1,0:T(8,128)(2,1)S(1)} %get-tuple-element.35), channel_id=1, source_target_pairs={{0,6},{2,4},{4,2},{6,0},{1,7},{3,5},{5,3},{7,1},{8,14},{10,12},{12... | collective-permute-start | bytes 688136 | tf_op jit(solution)/shard_map/ppermute | solution.py:299
  50.4 19.6 %collective-permute-start.12 = (bf16[2,64,896]{2,1,0:T(8,128)(2,1)S(1)}, bf16[2,64,896]{2,1,0:T(8,128)(2,1)S(1)}, u32[]{:S(2)}, u32[]{:S(2)}) collective-permute-start(bf16[2,64,896]{2,1,0:T(8,128)(2,1)S(1)} %get-tuple-element.34), channel_id=1, source_target_pairs={{0,4},{2,6},{4,0},{6,2},{1,5},{3,7},{5,1},{7,3},{8,12},{10,14},{12... | collective-permute-start | bytes 688136 | tf_op jit(solution)/shard_map/ppermute | solution.py:299
  50.4 22.5 %collective-permute-start.7 = (bf16[896,512]{1,0:T(8,128)(2,1)S(1)}, bf16[896,512]{1,0:T(8,128)(2,1)S(1)}, u32[]{:S(2)}, u32[]{:S(2)}) collective-permute-start(bf16[896,512]{1,0:T(8,128)(2,1)S(1)} %collective-permute-done.3.refs_0_), channel_id=1, source_target_pairs={{0,16},{16,0},{1,17},{17,1},{2,18},{18,2},{3,19},{19,3},{4,20},{20... | collective-permute-start | bytes 2752520 | tf_op jit(solution)/shard_map/ppermute | solution.py:37
  51.9 18.1 %collective-permute-start.11 = (bf16[2,64,896]{2,1,0:T(8,128)(2,1)S(1)}, bf16[2,64,896]{2,1,0:T(8,128)(2,1)S(1)}, u32[]{:S(2)}, u32[]{:S(2)}) collective-permute-start(bf16[2,64,896]{2,1,0:T(8,128)(2,1)S(1)} %get-tuple-element.33), channel_id=1, source_target_pairs={{0,2},{2,0},{4,6},{6,4},{1,3},{3,1},{5,7},{7,5},{8,10},{10,8},{12,... | collective-permute-start | bytes 688136 | tf_op jit(solution)/shard_map/ppermute | solution.py:299
  54.5 17.7 %collective-permute-start.6 = (bf16[256,512]{1,0:T(8,128)(2,1)S(1)}, bf16[256,512]{1,0:T(8,128)(2,1)S(1)}, u32[]{:S(2)}, u32[]{:S(2)}) collective-permute-start(bf16[256,512]{1,0:T(8,128)(2,1)S(1)} %shard_map.77), channel_id=1, source_target_pairs={{0,2},{2,0},{1,3},{3,1},{4,6},{6,4},{5,7},{7,5},{8,10},{10,8},{9,1... | collective-permute-start | bytes 786440 | tf_op jit(solution)/shard_map/ppermute | solution.py:37
  73.3 10.6 %collective-permute-start.8 = (bf16[256,512]{1,0:T(8,128)(2,1)S(1)}, bf16[256,512]{1,0:T(8,128)(2,1)S(1)}, u32[]{:S(2)}, u32[]{:S(2)}) collective-permute-start(bf16[256,512]{1,0:T(8,128)(2,1)S(1)} %shard_map.79), channel_id=1, source_target_pairs={{0,2},{2,0},{1,3},{3,1},{4,6},{6,4},{5,7},{7,5},{8,10},{10,8},{9,1... | collective-permute-start | bytes 786440 | tf_op jit(solution)/shard_map/ppermute | solution.py:37
  74.7 18.0 %collective-permute-start.14 = (bf16[2,2,2,64,896]{4,3,2,1,0:T(8,128)(2,1)S(1)}, bf16[2,2,2,64,896]{4,3,2,1,0:T(8,128)(2,1)S(1)}, u32[]{:S(2)}, u32[]{:S(2)}) collective-permute-start(bf16[2,2,2,64,896]{4,3,2,1,0:T(8,128)(2,1)S(1)} %pad_maximum_fusion.1.refs_6_.refs_2_), channel_id=1, source_target_pairs={{0,1},{1,0},{2,3},{3,2},{4,5},{5,4},{6,7},{7,6},{8,9},{9,8},{10,11... | collective-permute-start | bytes 2752520 | tf_op jit(solution)/shard_map/ppermute | solution.py:37
  74.8 13.5 %collective-permute-start.16 = (bf16[256,256]{1,0:T(8,128)(2,1)S(1)}, bf16[256,256]{1,0:T(8,128)(2,1)S(1)}, u32[]{:S(2)}, u32[]{:S(2)}) collective-permute-start(bf16[256,256]{1,0:T(8,128)(2,1)S(1)} %fusion.1.refs_0_), channel_id=1, source_target_pairs={{0,4},{4,0},{1,5},{5,1},{2,6},{6,2},{3,7},{7,3},{8,12},{12,8},{9,1... | collective-permute-start | bytes 393224 | tf_op jit(solution)/shard_map/ppermute | solution.py:37
  77.6 21.5 %copy-start.4 = (bf16[1,512,896]{2,1,0:T(8,128)(2,1)S(1)}, bf16[1,512,896]{2,1,0:T(8,128)(2,1)}, u32[]{:S(2)}) copy-start(bf16[1,512,896]{2,1,0:T(8,128)(2,1)} %param.13) | copy-start | bytes 2752516
  84.1 7.6 %collective-permute-start.9 = (bf16[256,256]{1,0:T(8,128)(2,1)S(1)}, bf16[256,256]{1,0:T(8,128)(2,1)S(1)}, u32[]{:S(2)}, u32[]{:S(2)}) collective-permute-start(bf16[256,256]{1,0:T(8,128)(2,1)S(1)} %fusion.refs_4_), channel_id=1, source_target_pairs={{0,4},{4,0},{1,5},{5,1},{2,6},{6,2},{3,7},{7,3},{8,12},{12,8},{9,1... | collective-permute-start | bytes 393224 | tf_op jit(solution)/shard_map/ppermute | solution.py:37
  85.7 7.8 %collective-permute-start.15 = (bf16[256,256]{1,0:T(8,128)(2,1)S(1)}, bf16[256,256]{1,0:T(8,128)(2,1)S(1)}, u32[]{:S(2)}, u32[]{:S(2)}) collective-permute-start(bf16[256,256]{1,0:T(8,128)(2,1)S(1)} %fusion.1.refs_0_), channel_id=1, source_target_pairs={{0,2},{2,0},{1,3},{3,1},{4,6},{6,4},{5,7},{7,5},{8,10},{10,8},{9,1... | collective-permute-start | bytes 393224 | tf_op jit(solution)/shard_map/ppermute | solution.py:37
  88.2 8.1 %collective-permute-start.17 = (bf16[256,256]{1,0:T(8,128)(2,1)S(1)}, bf16[256,256]{1,0:T(8,128)(2,1)S(1)}, u32[]{:S(2)}, u32[]{:S(2)}) collective-permute-start(bf16[256,256]{1,0:T(8,128)(2,1)S(1)} %collective-permute-done.16.refs_2_), channel_id=1, source_target_pairs={{0,2},{2,0},{1,3},{3,1},{4,6},{6,4},{5,7},{7,5},{8,10},{10,8},{9,1... | collective-permute-start | bytes 393224 | tf_op jit(solution)/shard_map/ppermute | solution.py:37
  88.3 10.9 %collective-permute-start.18 = (bf16[256,256]{1,0:T(8,128)(2,1)S(1)}, bf16[256,256]{1,0:T(8,128)(2,1)S(1)}, u32[]{:S(2)}, u32[]{:S(2)}) collective-permute-start(bf16[256,256]{1,0:T(8,128)(2,1)S(1)} %fusion.refs_4_), channel_id=1, source_target_pairs={{0,2},{2,0},{1,3},{3,1},{4,6},{6,4},{5,7},{7,5},{8,10},{10,8},{9,1... | collective-permute-start | bytes 393224 | tf_op jit(solution)/shard_map/ppermute | solution.py:37
  91.6 8.9 %collective-permute-start.10 = (bf16[256,256]{1,0:T(8,128)(2,1)S(1)}, bf16[256,256]{1,0:T(8,128)(2,1)S(1)}, u32[]{:S(2)}, u32[]{:S(2)}) collective-permute-start(bf16[256,256]{1,0:T(8,128)(2,1)S(1)} %collective-permute-done.9.refs_0_), channel_id=1, source_target_pairs={{0,2},{2,0},{1,3},{3,1},{4,6},{6,4},{5,7},{7,5},{8,10},{10,8},{9,1... | collective-permute-start | bytes 393224 | tf_op jit(solution)/shard_map/ppermute | solution.py:37
  (2 other events, 1.3 us)

commit v7 on v6

--- a/solution.py
+++ b/solution.py
@@ -192,47 +192,64 @@
 
 
 def near_kernel(nodes, side, lo_ref, group_ref, *refs):
-    blocks, (own_ref, other_ref, feedback_ref, done_ref, base_ref) = refs[:-5], refs[-5:]
-    half = done_ref.shape[0]
+    blocks, (own_ref, other_ref, feedback_ref, out_hbm, base_ref, done, sem) = refs[:-7], refs[-7:]
+    half = done.shape[0]
     places = [(h, l) for h in range(2) for l in range(side)]
-    sums = []
     for start, count, which in ((0, 2 * side, group_ref[0]), (2 * side, side, 1 - group_ref[0])):
-        total = feedback_ref[pl.ds(pl.multiple_of(which * half, half), half), :].astype(F32)
+        rows = pl.ds(pl.multiple_of(which * half, half), half)
+        total = feedback_ref[rows, :].astype(F32)
         for block_ref, place in zip(blocks[start : start + count], places):
             total += block_product(nodes, side, block_ref, own_ref, other_ref, lo_ref[0], place)
-        sums.append(total)
-    done_ref[...] = sums[0].astype(BF16)
-    base_ref[...] = sums[1]
+        if start == 0:
+            done[...] = total.astype(BF16)
+            copy = pltpu.make_async_copy(done, out_hbm.at[rows], sem)
+            copy.start()
+        else:
+            base_ref[...] = total
+    copy.wait()
 
 
 def far_kernel(nodes, side, lo_ref, group_ref, *refs):
-    blocks, (own_ref, other_ref, done_ref, base_ref, out_ref) = refs[:-5], refs[-5:]
-    half = done_ref.shape[0]
+    blocks, (own_ref, other_ref, base_ref, _, out_hbm, done, sem) = refs[:-7], refs[-7:]
+    half = done.shape[0]
     total = base_ref[...]
     for step, block_ref in enumerate(blocks):
         total += block_product(nodes, side, block_ref, own_ref, other_ref, lo_ref[0], (1, step))
-    mine, theirs = group_ref[0], 1 - group_ref[0]
-    out_ref[pl.ds(pl.multiple_of(mine * half, half), half), :] = done_ref[...]
-    out_ref[pl.ds(pl.multiple_of(theirs * half, half), half), :] = total.astype(BF16)
+    done[...] = total.astype(BF16)
+    start = pl.multiple_of((1 - group_ref[0]) * half, half)
+    copy = pltpu.make_async_copy(done, out_hbm.at[pl.ds(start, half)], sem)
+    copy.start()
+    copy.wait()
 
 
 def product(lo, group, first, second, own, other, feedback, nodes, side):
     half, width = first[0].shape[1], own.shape[-1]
     flops = 2 * first[0].size * width
-    done, base = call(
+    out = shape((2 * half, width), BF16)
+    far = pl.BlockSpec(memory_space=pltpu.HBM)
+    scratch = [pltpu.VMEM((half, width), BF16), pltpu.SemaphoreType.DMA]
+    estimate = lambda count: pl.CostEstimate(
+        flops=count * flops, bytes_accessed=2 * own.size * 2, transcendentals=0
+    )
+    out, base = pl.pallas_call(
         functools.partial(near_kernel, nodes, side),
-        3 * side * flops,
-        (shape((half, width), BF16), shape((half, width), F32)),
-        (lo, group),
-        (*first, *second[:side], own, other, feedback),
-    )
-    return call(
+        out_shape=(out, shape((half, width), F32)),
+        in_specs=[SMEM] * 2 + [WHOLE] * (3 * side + 3),
+        out_specs=(far, WHOLE),
+        scratch_shapes=scratch,
+        compiler_params=KERNEL,
+        cost_estimate=estimate(3 * side),
+    )(lo, group, *first, *second[:side], own, other, feedback)
+    return pl.pallas_call(
         functools.partial(far_kernel, nodes, side),
-        side * flops,
-        (shape((2 * half, width), BF16),),
-        (lo, group),
-        (*second[side:], own, other, done, base),
-    )[0]
+        out_shape=shape((2 * half, width), BF16),
+        in_specs=[SMEM] * 2 + [WHOLE] * (side + 3) + [far],
+        out_specs=far,
+        scratch_shapes=scratch,
+        input_output_aliases={side + 5: 0},
+        compiler_params=KERNEL,
+        cost_estimate=estimate(side),
+    )(lo, group, *second[side:], own, other, base, out)
 
 
 def local(tokens, cotangent, expert_ids, gate_values, w_gate, w_up, feedback):
@@ -273,7 +290,10 @@
         hidden = (jax.nn.silu(pre[:, :half]) * pre[:, half:]).astype(BF16)
         across = swapped(hidden, "hi")
         beside = [swapped(hidden, "lo", d) for d in range(1, side)]
-        corners = [swapped(across, "lo", d) for d in range(1, side)]
+        corners = [
+            lax.ppermute(hidden, ("hi", "lo"), [(s, s ^ (side + d)) for s in range(2 * side)])
+            for d in range(1, side)
+        ]
         return [hidden, *beside, across, *corners]
 
     y = [send_y[0]] + [swapped(send_y[d], "node", d) for d in range(1, nodes)]
@@ -300,11 +320,11 @@
     came_m = [swapped(send, "lo", d) for d, send in enumerate(sends_m, 1)]
     keep_m = partial_second(*margs, (0,), F32)[0]
     first = spread_hidden(keep_m, came_m)
+    targs = (lo, own_x, other_x, acc_theirs, theirs, cuts, nodes, side)
+    sends_t = partial_second(*targs, range(1, side), BF16)
+    y, sends_t = lax.optimization_barrier((y, sends_t))
     own_y = jnp.stack([jnp.stack(row) for row in y])
     other_y = swapped(own_y, "rep")
-    first[0], theirs = lax.optimization_barrier((first[0], theirs))
-    targs = (lo, own_x, other_x, acc_theirs, theirs, cuts, nodes, side)
-    sends_t = partial_second(*targs, range(1, side), BF16)
     came_t = [swapped(send, "lo", d) for d, send in enumerate(sends_t, 1)]
     keep_t = partial_second(*targs, (0,), F32)[0]
     second = spread_hidden(keep_t, came_t)

time: 102 us -> 102 us (level)
    ppermute x3, waiting for transfers between devices: 14.3 us -> 0.01 us  [local(): y[h][l] = lax.ppermute(y[h][l], ('hi', 'lo'), pairs)]
    ppermute x13 -> x11, waiting for transfers between devices: 26.9 us -> 38.2 us  [swapped(): return lax.ppermute(value, axis, pairs)]
    ppermute x13 -> x11, starting transfers between devices: 19.4 us -> 15.2 us  [swapped(): return lax.ppermute(value, axis, pairs)]
    ppermute x0 -> x2, starting transfers between devices: none -> 3.21 us  [spread_hidden(): lax.ppermute(hidden, ('hi', 'lo'), [(s, s ^ side + d) for s in range(2 *...]
    ppermute x0 -> x2, waiting for transfers between devices: none -> 2.99 us  [spread_hidden(): lax.ppermute(hidden, ('hi', 'lo'), [(s, s ^ side + d) for s in range(2 *...]
    pallas_call x0 -> x2, Pallas kernels: none -> 2.77 us  [the longest x1 1.53 us: product(): pl.pallas_call(functools.partial(near_kernel, nodes, side), out_shape=(ou...]
    pallas_call x8 -> x6, Pallas kernels: 6.36 us -> 3.96 us  [call(): pl.pallas_call(kernel, out_shape=outs, in_specs=[SMEM] * len(scalars) + [...]
  transfers between devices with their start and end apart: 19 -> 19, of which waited for: 13 -> 10; matrix products, arithmetic and copies ran while one was open for 1% -> 1% of each run, Pallas kernels for 4% -> 5%
where the time goes in v7:
time: 102 us; the launch traced here: 101 us
  waiting for transfers between devices  62.8 us (62%)
  starting transfers between devices  26.5 us (26%)
  Pallas kernels  8.89 us (9%)
  local copies, waits for them, and re-layouts  2.02 us (2%)
    ppermute x11, waiting for transfers between devices, swapped(): return lax.ppermute(value, axis, pairs)  38.2 us
    ppermute x3, waiting for transfers between devices, local(): x[d][n] = lax.ppermute(x[d][n], ('node', 'lo'), pairs)  21.6 us
    ppermute x11, starting transfers between devices, swapped(): return lax.ppermute(value, axis, pairs)  15.2 us
    ppermute x3, starting transfers between devices, local(): y[h][l] = lax.ppermute(y[h][l], ('hi', 'lo'), pairs)  4.45 us
    pallas_call x6, Pallas kernels, call(): pl.pallas_call(kernel, out_shape=outs, in_specs=[SMEM] * len(scalars) + [...  3.96 us
    ppermute x3, starting transfers between devices, local(): x[d][n] = lax.ppermute(x[d][n], ('node', 'lo'), pairs)  3.62 us
    ppermute x2, starting transfers between devices, spread_hidden(): lax.ppermute(hidden, ('hi', 'lo'), [(s, s ^ side + d) for s in range(2 *...  3.21 us
    ppermute x2, waiting for transfers between devices, spread_hidden(): lax.ppermute(hidden, ('hi', 'lo'), [(s, s ^ side + d) for s in range(2 *...  2.99 us
  transfers between devices with their start and end apart: 19, of which 10 were waited for; matrix products, arithmetic and copies ran while one was open for 1% of the time, Pallas kernels for 5%

profile of v7, /device:TPU:0, one launch (start us, length us, event | category | flops | bytes accessed | tf_op | source)
XLA Modules:
  0.0 101.2 jit_solution(7844417845590494249)
XLA Ops:
  0.0 2.2 %shard_map.74 = bf16[896,512]{1,0:T(8,128)(2,1)} custom-call(s32[1]{0:T(128)} %bitcast.1.group_ref, bf16[896,512]{1,0:T(8,128)(2,1)} %bitcast.47, bf16[896,512]{1,0:T(8,128)(2,1)} %bitcast.49), custom_call_target="tpu_custom_call" | custom-call | bytes 1835008 | tf_op jit(solution)/shard_map/pallas_call | solution.py:65
  2.2 4.1 %collective-permute-start.3 = (bf16[896,512]{1,0:T(8,128)(2,1)}, bf16[896,512]{1,0:T(8,128)(2,1)S(1)}, u32[]{:S(2)}, u32[]{:S(2)}) collective-permute-start(bf16[896,512]{1,0:T(8,128)(2,1)} %shard_map.74), channel_id=1, source_target_pairs={{0,4},{4,0},{1,5},{5,1},{2,6},{6,2},{3,7},{7,3},{8,12},{12,8},{9,1... | collective-permute-start | bytes 2752520 | tf_op jit(solution)/shard_map/ppermute | solution.py:37
  9.2 1.6 %collective-permute-start = (bf16[2,64,896]{2,1,0:T(8,128)(2,1)S(1)}, bf16[2,64,896]{2,1,0:T(8,128)(2,1)S(1)}, u32[]{:S(2)}, u32[]{:S(2)}) collective-permute-start(bf16[2,64,896]{2,1,0:T(8,128)(2,1)S(1)} %get-tuple-element.55), channel_id=1, source_target_pairs={{0,8},{2,10},{8,0},{10,2},{1,9},{3,11},{9,1},{11,3},{4,12},{6,14},... | collective-permute-start | bytes 688136 | tf_op jit(solution)/shard_map/ppermute | solution.py:306
  10.8 1.6 %collective-permute-start.1 = (bf16[2,64,896]{2,1,0:T(8,128)(2,1)S(1)}, bf16[2,64,896]{2,1,0:T(8,128)(2,1)S(1)}, u32[]{:S(2)}, u32[]{:S(2)}) collective-permute-start(bf16[2,64,896]{2,1,0:T(8,128)(2,1)S(1)} %get-tuple-element.54), channel_id=1, source_target_pairs={{0,2},{2,0},{8,10},{10,8},{1,3},{3,1},{9,11},{11,9},{4,6},{6,4},{1... | collective-permute-start | bytes 688136 | tf_op jit(solution)/shard_map/ppermute | solution.py:306
  12.8 1.5 %collective-permute-start.6 = (bf16[2,2,64,896]{3,2,1,0:T(8,128)(2,1)S(1)}, bf16[2,2,64,896]{3,2,1,0:T(8,128)(2,1)S(1)}, u32[]{:S(2)}, u32[]{:S(2)}) collective-permute-start(bf16[2,2,64,896]{3,2,1,0:T(8,128)(2,1)S(1)} %get-tuple-element.31), channel_id=1, source_target_pairs={{0,8},{8,0},{1,9},{9,1},{2,10},{10,2},{3,11},{11,3},{4,12},{12,4},... | collective-permute-start | bytes 1376264 | tf_op jit(solution)/shard_map/ppermute | solution.py:37
  14.3 8.4 %collective-permute-done = bf16[2,64,896]{2,1,0:T(8,128)(2,1)S(1)} collective-permute-done((bf16[2,64,896]{2,1,0:T(8,128)(2,1)S(1)}, bf16[2,64,896]{2,1,0:T(8,128)(2,1)S(1)}, u32[]{:S(2)}, u32[]{:S(2)}) %collective-permute-start) | collective-permute-done | bytes 229408 | tf_op jit(solution)/shard_map/ppermute | solution.py:306
  22.7 9.5 %collective-permute-done.1 = bf16[2,64,896]{2,1,0:T(8,128)(2,1)S(1)} collective-permute-done((bf16[2,64,896]{2,1,0:T(8,128)(2,1)S(1)}, bf16[2,64,896]{2,1,0:T(8,128)(2,1)S(1)}, u32[]{:S(2)}, u32[]{:S(2)}) %collective-permute-start.1) | collective-permute-done | bytes 229408 | tf_op jit(solution)/shard_map/ppermute | solution.py:306
  32.2 3.8 %collective-permute-done.2 = bf16[2,64,896]{2,1,0:T(8,128)(2,1)S(1)} collective-permute-done((bf16[2,64,896]{2,1,0:T(8,128)(2,1)S(1)}, bf16[2,64,896]{2,1,0:T(8,128)(2,1)S(1)}, u32[]{:S(2)}, u32[]{:S(2)}) %collective-permute-start.2) | collective-permute-done | bytes 229408 | tf_op jit(solution)/shard_map/ppermute | solution.py:306
  36.1 10.4 %collective-permute-done.3.refs_0_ = bf16[896,512]{1,0:T(8,128)(2,1)S(1)} collective-permute-done((bf16[896,512]{1,0:T(8,128)(2,1)}, bf16[896,512]{1,0:T(8,128)(2,1)S(1)}, u32[]{:S(2)}, u32[]{:S(2)}) %collective-permute-start.3) | collective-permute-done | bytes 917536 | tf_op jit(solution)/shard_map/ppermute | solution.py:37
  46.5 1.6 %collective-permute-start.5 = (bf16[896,512]{1,0:T(8,128)(2,1)S(1)}, bf16[896,512]{1,0:T(8,128)(2,1)S(1)}, u32[]{:S(2)}, u32[]{:S(2)}) collective-permute-start(bf16[896,512]{1,0:T(8,128)(2,1)S(1)} %collective-permute-done.3.refs_0_), channel_id=1, source_target_pairs={{0,16},{16,0},{1,17},{17,1},{2,18},{18,2},{3,19},{19,3},{4,20},{20... | collective-permute-start | bytes 2752520 | tf_op jit(solution)/shard_map/ppermute | solution.py:37
  49.2 3.3 %collective-permute-start.8 = (bf16[2,64,896]{2,1,0:T(8,128)(2,1)S(1)}, bf16[2,64,896]{2,1,0:T(8,128)(2,1)S(1)}, u32[]{:S(2)}, u32[]{:S(2)}) collective-permute-start(bf16[2,64,896]{2,1,0:T(8,128)(2,1)S(1)} %get-tuple-element.34), channel_id=1, source_target_pairs={{0,4},{2,6},{4,0},{6,2},{1,5},{3,7},{5,1},{7,3},{8,12},{10,14},{12... | collective-permute-start | bytes 688136 | tf_op jit(solution)/shard_map/ppermute | solution.py:319
  52.8 1.2 %shard_map.75 = (f32[2,256,512]{2,1,0:T(8,128)S(1)}, f32[2,256,512]{2,1,0:T(8,128)S(1)}) custom-call(s32[1]{0:T(128)} %bitcast.lo_ref, s32[1]{0:T(128)} %bitcast.1.group_ref, bf16[2,2,2,64,896]{4,3,2,1,0:T(8,128)(2,1)S(1)} %pad_maximum_fusion.own_ref, bf16[2,2,2,64,896]{4,3,2,1,0:T(8,128)(2,1)S(1)} %collective-permute-done.4.other_ref, ...), custom_call_target="tpu_custom_call" | custom-call | flops 939524096 | bytes 5767168 | tf_op jit(solution)/shard_map/pallas_call | solution.py:21
  54.8 14.5 %collective-permute-done.5.refs_0_ = bf16[896,512]{1,0:T(8,128)(2,1)S(1)} collective-permute-done((bf16[896,512]{1,0:T(8,128)(2,1)S(1)}, bf16[896,512]{1,0:T(8,128)(2,1)S(1)}, u32[]{:S(2)}, u32[]{:S(2)}) %collective-permute-start.5) | collective-permute-done | bytes 917536 | tf_op jit(solution)/shard_map/ppermute | solution.py:37
  70.0 3.9 %collective-permute-start.10 = (bf16[256,512]{1,0:T(8,128)(2,1)S(1)}, bf16[256,512]{1,0:T(8,128)(2,1)S(1)}, u32[]{:S(2)}, u32[]{:S(2)}) collective-permute-start(bf16[256,512]{1,0:T(8,128)(2,1)S(1)} %shard_map.77), channel_id=1, source_target_pairs={{0,2},{2,0},{1,3},{3,1},{4,6},{6,4},{5,7},{7,5},{8,10},{10,8},{9,1... | collective-permute-start | bytes 786440 | tf_op jit(solution)/shard_map/ppermute | solution.py:37
  75.1 3.0 %collective-permute-start.16 = (bf16[256,256]{1,0:T(8,128)(2,1)S(1)}, bf16[256,256]{1,0:T(8,128)(2,1)S(1)}, u32[]{:S(2)}, u32[]{:S(2)}) collective-permute-start(bf16[256,256]{1,0:T(8,128)(2,1)S(1)} %fusion.refs_0_), channel_id=1, source_target_pairs={{0,4},{4,0},{1,5},{5,1},{2,6},{6,2},{3,7},{7,3},{8,12},{12,8},{9,1... | collective-permute-start | bytes 393224 | tf_op jit(solution)/shard_map/ppermute | solution.py:37
  78.0 1.4 %collective-permute-start.17 = (bf16[256,256]{1,0:T(8,128)(2,1)S(1)}, bf16[256,256]{1,0:T(8,128)(2,1)S(1)}, u32[]{:S(2)}, u32[]{:S(2)}) collective-permute-start(bf16[256,256]{1,0:T(8,128)(2,1)S(1)} %fusion.refs_0_), channel_id=1, source_target_pairs={{0,6},{2,4},{4,2},{6,0},{1,7},{3,5},{5,3},{7,1},{8,14},{10,12},{12... | collective-permute-start | bytes 393224 | tf_op jit(solution)/shard_map/ppermute | solution.py:294
  79.4 4.4 %collective-permute-done.10 = bf16[256,512]{1,0:T(8,128)(2,1)S(1)} collective-permute-done((bf16[256,512]{1,0:T(8,128)(2,1)S(1)}, bf16[256,512]{1,0:T(8,128)(2,1)S(1)}, u32[]{:S(2)}, u32[]{:S(2)}) %collective-permute-start.10) | collective-permute-done | bytes 262176 | tf_op jit(solution)/shard_map/ppermute | solution.py:37
  84.1 2.4 %collective-permute-done.15.refs_1_ = bf16[256,256]{1,0:T(8,128)(2,1)S(1)} collective-permute-done((bf16[256,256]{1,0:T(8,128)(2,1)S(1)}, bf16[256,256]{1,0:T(8,128)(2,1)S(1)}, u32[]{:S(2)}, u32[]{:S(2)}) %collective-permute-start.15) | collective-permute-done | bytes 131104 | tf_op jit(solution)/shard_map/ppermute | solution.py:37
  87.1 1.8 %collective-permute-start.12 = (bf16[256,256]{1,0:T(8,128)(2,1)S(1)}, bf16[256,256]{1,0:T(8,128)(2,1)S(1)}, u32[]{:S(2)}, u32[]{:S(2)}) collective-permute-start(bf16[256,256]{1,0:T(8,128)(2,1)S(1)} %fusion.1.refs_4_), channel_id=1, source_target_pairs={{0,6},{2,4},{4,2},{6,0},{1,7},{3,5},{5,3},{7,1},{8,14},{10,12},{12... | collective-permute-start | bytes 393224 | tf_op jit(solution)/shard_map/ppermute | solution.py:294
  88.9 3.0 %collective-permute-done.17.refs_3_ = bf16[256,256]{1,0:T(8,128)(2,1)S(1)} collective-permute-done((bf16[256,256]{1,0:T(8,128)(2,1)S(1)}, bf16[256,256]{1,0:T(8,128)(2,1)S(1)}, u32[]{:S(2)}, u32[]{:S(2)}) %collective-permute-start.17) | collective-permute-done | bytes 131104 | tf_op jit(solution)/shard_map/ppermute | solution.py:294
  91.9 2.9 %collective-permute-done.18.refs_5_ = bf16[256,256]{1,0:T(8,128)(2,1)S(1)} collective-permute-done((bf16[256,256]{1,0:T(8,128)(2,1)S(1)}, bf16[256,256]{1,0:T(8,128)(2,1)S(1)}, u32[]{:S(2)}, u32[]{:S(2)}) %collective-permute-start.18) | collective-permute-done | bytes 131104 | tf_op jit(solution)/shard_map/ppermute | solution.py:37
  94.8 1.5 %shard_map.80 = (bf16[512,896]{1,0:T(8,128)(2,1)}, f32[256,896]{1,0:T(8,128)S(1)}) custom-call(s32[1]{0:T(128)} %bitcast.lo_ref, s32[1]{0:T(128)} %bitcast.1.group_ref, bf16[256,256]{1,0:T(8,128)(2,1)S(1)} %fusion.refs_0_, bf16[256,256]{1,0:T(8,128)(2,1)S(1)} %collective-permute-done.15.refs_1_, bf16[256,256]{1,0:T(8,128)(2,1)S(1)} %collective-permute-done.16.refs_2_, ...), custom_call_target="tpu_custom_call" | custom-call | flops 704643072 | bytes 1835008 | tf_op jit(solution)/shard_map/pallas_call | solution.py:234
  96.4 3.6 %collective-permute-done.11.refs_0_ = bf16[256,256]{1,0:T(8,128)(2,1)S(1)} collective-permute-done((bf16[256,256]{1,0:T(8,128)(2,1)S(1)}, bf16[256,256]{1,0:T(8,128)(2,1)S(1)}, u32[]{:S(2)}, u32[]{:S(2)}) %collective-permute-start.11) | collective-permute-done | bytes 131104 | tf_op jit(solution)/shard_map/ppermute | solution.py:37
  100.0 1.2 %shard_map.81 = bf16[512,896]{1,0:T(8,128)(2,1)} custom-call(s32[1]{0:T(128)} %bitcast.lo_ref, s32[1]{0:T(128)} %bitcast.1.group_ref, bf16[256,256]{1,0:T(8,128)(2,1)S(1)} %collective-permute-done.11.refs_0_, bf16[256,256]{1,0:T(8,128)(2,1)S(1)} %collective-permute-done.12.refs_1_, ...), custom_call_target="tpu_custom_call", output_to_operand_aliasing={{}: (7, {})} | custom-call | flops 234881024 | bytes 1835008 | tf_op jit(solution)/shard_map/pallas_call | solution.py:243
  (53 shorter events, 8.3 us)
Async XLA Ops:
  0.0 6.3 %copy-start.2 = (bf16[128,3584]{1,0:T(8,128)(2,1)S(1)}, bf16[128,3584]{1,0:T(8,128)(2,1)}, u32[]{:S(2)}) copy-start(bf16[128,3584]{1,0:T(8,128)(2,1)} %x_ref.1) | copy-start | bytes 2752516
  2.2 44.3 %collective-permute-start.3 = (bf16[896,512]{1,0:T(8,128)(2,1)}, bf16[896,512]{1,0:T(8,128)(2,1)S(1)}, u32[]{:S(2)}, u32[]{:S(2)}) collective-permute-start(bf16[896,512]{1,0:T(8,128)(2,1)} %shard_map.74), channel_id=1, source_target_pairs={{0,4},{4,0},{1,5},{5,1},{2,6},{6,2},{3,7},{7,3},{8,12},{12,8},{9,1... | collective-permute-start | bytes 2752520 | tf_op jit(solution)/shard_map/ppermute | solution.py:37
  7.0 1.2 %copy-start.3 = (bf16[128,3584]{1,0:T(8,128)(2,1)S(1)}, bf16[128,3584]{1,0:T(8,128)(2,1)}, u32[]{:S(2)}) copy-start(bf16[128,3584]{1,0:T(8,128)(2,1)} %c_ref.1) | copy-start | bytes 2752516
  9.2 13.5 %collective-permute-start = (bf16[2,64,896]{2,1,0:T(8,128)(2,1)S(1)}, bf16[2,64,896]{2,1,0:T(8,128)(2,1)S(1)}, u32[]{:S(2)}, u32[]{:S(2)}) collective-permute-start(bf16[2,64,896]{2,1,0:T(8,128)(2,1)S(1)} %get-tuple-element.55), channel_id=1, source_target_pairs={{0,8},{2,10},{8,0},{10,2},{1,9},{3,11},{9,1},{11,3},{4,12},{6,14},... | collective-permute-start | bytes 688136 | tf_op jit(solution)/shard_map/ppermute | solution.py:306
  10.8 21.4 %collective-permute-start.1 = (bf16[2,64,896]{2,1,0:T(8,128)(2,1)S(1)}, bf16[2,64,896]{2,1,0:T(8,128)(2,1)S(1)}, u32[]{:S(2)}, u32[]{:S(2)}) collective-permute-start(bf16[2,64,896]{2,1,0:T(8,128)(2,1)S(1)} %get-tuple-element.54), channel_id=1, source_target_pairs={{0,2},{2,0},{8,10},{10,8},{1,3},{3,1},{9,11},{11,9},{4,6},{6,4},{1... | collective-permute-start | bytes 688136 | tf_op jit(solution)/shard_map/ppermute | solution.py:306
  12.4 23.6 %collective-permute-start.2 = (bf16[2,64,896]{2,1,0:T(8,128)(2,1)S(1)}, bf16[2,64,896]{2,1,0:T(8,128)(2,1)S(1)}, u32[]{:S(2)}, u32[]{:S(2)}) collective-permute-start(bf16[2,64,896]{2,1,0:T(8,128)(2,1)S(1)} %get-tuple-element.56), channel_id=1, source_target_pairs={{0,10},{2,8},{8,2},{10,0},{1,11},{3,9},{9,3},{11,1},{4,14},{6,12},... | collective-permute-start | bytes 688136 | tf_op jit(solution)/shard_map/ppermute | solution.py:306
  12.8 35.3 %collective-permute-start.6 = (bf16[2,2,64,896]{3,2,1,0:T(8,128)(2,1)S(1)}, bf16[2,2,64,896]{3,2,1,0:T(8,128)(2,1)S(1)}, u32[]{:S(2)}, u32[]{:S(2)}) collective-permute-start(bf16[2,2,64,896]{3,2,1,0:T(8,128)(2,1)S(1)} %get-tuple-element.31), channel_id=1, source_target_pairs={{0,8},{8,0},{1,9},{9,1},{2,10},{10,2},{3,11},{11,3},{4,12},{12,4},... | collective-permute-start | bytes 1376264 | tf_op jit(solution)/shard_map/ppermute | solution.py:37
  46.5 6.3 %collective-permute-start.4 = (bf16[2,2,2,64,896]{4,3,2,1,0:T(8,128)(2,1)S(1)}, bf16[2,2,2,64,896]{4,3,2,1,0:T(8,128)(2,1)S(1)}, u32[]{:S(2)}, u32[]{:S(2)}) collective-permute-start(bf16[2,2,2,64,896]{4,3,2,1,0:T(8,128)(2,1)S(1)} %pad_maximum_fusion.own_ref), channel_id=1, source_target_pairs={{0,1},{1,0},{2,3},{3,2},{4,5},{5,4},{6,7},{7,6},{8,9},{9,8},{10,11... | collective-permute-start | bytes 2752520 | tf_op jit(solution)/shard_map/ppermute | solution.py:37
  46.5 22.8 %collective-permute-start.5 = (bf16[896,512]{1,0:T(8,128)(2,1)S(1)}, bf16[896,512]{1,0:T(8,128)(2,1)S(1)}, u32[]{:S(2)}, u32[]{:S(2)}) collective-permute-start(bf16[896,512]{1,0:T(8,128)(2,1)S(1)} %collective-permute-done.3.refs_0_), channel_id=1, source_target_pairs={{0,16},{16,0},{1,17},{17,1},{2,18},{18,2},{3,19},{19,3},{4,20},{20... | collective-permute-start | bytes 2752520 | tf_op jit(solution)/shard_map/ppermute | solution.py:37
  48.2 4.6 %copy-start = (bf16[1,896,512]{2,1,0:T(8,128)(2,1)S(1)}, bf16[1,896,512]{2,1,0:T(8,128)(2,1)}, u32[]{:S(2)}) copy-start(bf16[1,896,512]{2,1,0:T(8,128)(2,1)} %param.11) | copy-start | bytes 2752516
  48.2 4.6 %copy-start.1 = (bf16[1,896,512]{2,1,0:T(8,128)(2,1)S(1)}, bf16[1,896,512]{2,1,0:T(8,128)(2,1)}, u32[]{:S(2)}) copy-start(bf16[1,896,512]{2,1,0:T(8,128)(2,1)} %param.12) | copy-start | bytes 2752516
  48.3 21.4 %collective-permute-start.7 = (bf16[2,64,896]{2,1,0:T(8,128)(2,1)S(1)}, bf16[2,64,896]{2,1,0:T(8,128)(2,1)S(1)}, u32[]{:S(2)}, u32[]{:S(2)}) collective-permute-start(bf16[2,64,896]{2,1,0:T(8,128)(2,1)S(1)} %get-tuple-element.33), channel_id=1, source_target_pairs={{0,2},{2,0},{4,6},{6,4},{1,3},{3,1},{5,7},{7,5},{8,10},{10,8},{12,... | collective-permute-start | bytes 688136 | tf_op jit(solution)/shard_map/ppermute | solution.py:319
  49.2 20.5 %collective-permute-start.8 = (bf16[2,64,896]{2,1,0:T(8,128)(2,1)S(1)}, bf16[2,64,896]{2,1,0:T(8,128)(2,1)S(1)}, u32[]{:S(2)}, u32[]{:S(2)}) collective-permute-start(bf16[2,64,896]{2,1,0:T(8,128)(2,1)S(1)} %get-tuple-element.34), channel_id=1, source_target_pairs={{0,4},{2,6},{4,0},{6,2},{1,5},{3,7},{5,1},{7,3},{8,12},{10,14},{12... | collective-permute-start | bytes 688136 | tf_op jit(solution)/shard_map/ppermute | solution.py:319
  52.4 17.3 %collective-permute-start.9 = (bf16[2,64,896]{2,1,0:T(8,128)(2,1)S(1)}, bf16[2,64,896]{2,1,0:T(8,128)(2,1)S(1)}, u32[]{:S(2)}, u32[]{:S(2)}) collective-permute-start(bf16[2,64,896]{2,1,0:T(8,128)(2,1)S(1)} %get-tuple-element.35), channel_id=1, source_target_pairs={{0,6},{2,4},{4,2},{6,0},{1,7},{3,5},{5,3},{7,1},{8,14},{10,12},{12... | collective-permute-start | bytes 688136 | tf_op jit(solution)/shard_map/ppermute | solution.py:319
  54.5 20.3 %collective-permute-start.14 = (bf16[256,512]{1,0:T(8,128)(2,1)S(1)}, bf16[256,512]{1,0:T(8,128)(2,1)S(1)}, u32[]{:S(2)}, u32[]{:S(2)}) collective-permute-start(bf16[256,512]{1,0:T(8,128)(2,1)S(1)} %shard_map.79), channel_id=1, source_target_pairs={{0,2},{2,0},{1,3},{3,1},{4,6},{6,4},{5,7},{7,5},{8,10},{10,8},{9,1... | collective-permute-start | bytes 786440 | tf_op jit(solution)/shard_map/ppermute | solution.py:37
  70.0 24.9 %collective-permute-start.13 = (bf16[2,2,2,64,896]{4,3,2,1,0:T(8,128)(2,1)S(1)}, bf16[2,2,2,64,896]{4,3,2,1,0:T(8,128)(2,1)S(1)}, u32[]{:S(2)}, u32[]{:S(2)}) collective-permute-start(bf16[2,2,2,64,896]{4,3,2,1,0:T(8,128)(2,1)S(1)} %pad_maximum_fusion.1.refs_6_.refs_2_), channel_id=1, source_target_pairs={{0,1},{1,0},{2,3},{3,2},{4,5},{5,4},{6,7},{7,6},{8,9},{9,8},{10,11... | collective-permute-start | bytes 2752520 | tf_op jit(solution)/shard_map/ppermute | solution.py:37
  70.0 13.8 %collective-permute-start.10 = (bf16[256,512]{1,0:T(8,128)(2,1)S(1)}, bf16[256,512]{1,0:T(8,128)(2,1)S(1)}, u32[]{:S(2)}, u32[]{:S(2)}) collective-permute-start(bf16[256,512]{1,0:T(8,128)(2,1)S(1)} %shard_map.77), channel_id=1, source_target_pairs={{0,2},{2,0},{1,3},{3,1},{4,6},{6,4},{5,7},{7,5},{8,10},{10,8},{9,1... | collective-permute-start | bytes 786440 | tf_op jit(solution)/shard_map/ppermute | solution.py:37
  75.0 19.9 %copy-start.4 = (bf16[1,512,896]{2,1,0:T(8,128)(2,1)S(1)}, bf16[1,512,896]{2,1,0:T(8,128)(2,1)}, u32[]{:S(2)}) copy-start(bf16[1,512,896]{2,1,0:T(8,128)(2,1)} %param.13) | copy-start | bytes 2752516
  75.0 11.5 %collective-permute-start.15 = (bf16[256,256]{1,0:T(8,128)(2,1)S(1)}, bf16[256,256]{1,0:T(8,128)(2,1)S(1)}, u32[]{:S(2)}, u32[]{:S(2)}) collective-permute-start(bf16[256,256]{1,0:T(8,128)(2,1)S(1)} %fusion.refs_0_), channel_id=1, source_target_pairs={{0,2},{2,0},{1,3},{3,1},{4,6},{6,4},{5,7},{7,5},{8,10},{10,8},{9,1... | collective-permute-start | bytes 393224 | tf_op jit(solution)/shard_map/ppermute | solution.py:37
  75.1 12.1 %collective-permute-start.16 = (bf16[256,256]{1,0:T(8,128)(2,1)S(1)}, bf16[256,256]{1,0:T(8,128)(2,1)S(1)}, u32[]{:S(2)}, u32[]{:S(2)}) collective-permute-start(bf16[256,256]{1,0:T(8,128)(2,1)S(1)} %fusion.refs_0_), channel_id=1, source_target_pairs={{0,4},{4,0},{1,5},{5,1},{2,6},{6,2},{3,7},{7,3},{8,12},{12,8},{9,1... | collective-permute-start | bytes 393224 | tf_op jit(solution)/shard_map/ppermute | solution.py:37
  78.0 13.9 %collective-permute-start.17 = (bf16[256,256]{1,0:T(8,128)(2,1)S(1)}, bf16[256,256]{1,0:T(8,128)(2,1)S(1)}, u32[]{:S(2)}, u32[]{:S(2)}) collective-permute-start(bf16[256,256]{1,0:T(8,128)(2,1)S(1)} %fusion.refs_0_), channel_id=1, source_target_pairs={{0,6},{2,4},{4,2},{6,0},{1,7},{3,5},{5,3},{7,1},{8,14},{10,12},{12... | collective-permute-start | bytes 393224 | tf_op jit(solution)/shard_map/ppermute | solution.py:294
  84.0 10.8 %collective-permute-start.18 = (bf16[256,256]{1,0:T(8,128)(2,1)S(1)}, bf16[256,256]{1,0:T(8,128)(2,1)S(1)}, u32[]{:S(2)}, u32[]{:S(2)}) collective-permute-start(bf16[256,256]{1,0:T(8,128)(2,1)S(1)} %fusion.1.refs_4_), channel_id=1, source_target_pairs={{0,2},{2,0},{1,3},{3,1},{4,6},{6,4},{5,7},{7,5},{8,10},{10,8},{9,1... | collective-permute-start | bytes 393224 | tf_op jit(solution)/shard_map/ppermute | solution.py:37
  86.5 13.5 %collective-permute-start.11 = (bf16[256,256]{1,0:T(8,128)(2,1)S(1)}, bf16[256,256]{1,0:T(8,128)(2,1)S(1)}, u32[]{:S(2)}, u32[]{:S(2)}) collective-permute-start(bf16[256,256]{1,0:T(8,128)(2,1)S(1)} %fusion.1.refs_4_), channel_id=1, source_target_pairs={{0,4},{4,0},{1,5},{5,1},{2,6},{6,2},{3,7},{7,3},{8,12},{12,8},{9,1... | collective-permute-start | bytes 393224 | tf_op jit(solution)/shard_map/ppermute | solution.py:37
  87.1 12.9 %collective-permute-start.12 = (bf16[256,256]{1,0:T(8,128)(2,1)S(1)}, bf16[256,256]{1,0:T(8,128)(2,1)S(1)}, u32[]{:S(2)}, u32[]{:S(2)}) collective-permute-start(bf16[256,256]{1,0:T(8,128)(2,1)S(1)} %fusion.1.refs_4_), channel_id=1, source_target_pairs={{0,6},{2,4},{4,2},{6,0},{1,7},{3,5},{5,3},{7,1},{8,14},{10,12},{12... | collective-permute-start | bytes 393224 | tf_op jit(solution)/shard_map/ppermute | solution.py:294
  (2 other events, 1.3 us)

commit v8 on v7

--- a/solution.py
+++ b/solution.py
@@ -290,10 +290,7 @@
         hidden = (jax.nn.silu(pre[:, :half]) * pre[:, half:]).astype(BF16)
         across = swapped(hidden, "hi")
         beside = [swapped(hidden, "lo", d) for d in range(1, side)]
-        corners = [
-            lax.ppermute(hidden, ("hi", "lo"), [(s, s ^ (side + d)) for s in range(2 * side)])
-            for d in range(1, side)
-        ]
+        corners = [swapped(across, "lo", d) for d in range(1, side)]
         return [hidden, *beside, across, *corners]
 
     y = [send_y[0]] + [swapped(send_y[d], "node", d) for d in range(1, nodes)]
@@ -320,11 +317,11 @@
     came_m = [swapped(send, "lo", d) for d, send in enumerate(sends_m, 1)]
     keep_m = partial_second(*margs, (0,), F32)[0]
     first = spread_hidden(keep_m, came_m)
+    own_y = jnp.stack([jnp.stack(row) for row in y])
+    other_y = swapped(own_y, "rep")
+    first[0], theirs = lax.optimization_barrier((first[0], theirs))
     targs = (lo, own_x, other_x, acc_theirs, theirs, cuts, nodes, side)
     sends_t = partial_second(*targs, range(1, side), BF16)
-    y, sends_t = lax.optimization_barrier((y, sends_t))
-    own_y = jnp.stack([jnp.stack(row) for row in y])
-    other_y = swapped(own_y, "rep")
     came_t = [swapped(send, "lo", d) for d, send in enumerate(sends_t, 1)]
     keep_t = partial_second(*targs, (0,), F32)[0]
     second = spread_hidden(keep_t, came_t)

time: 102 us -> 102 us (level)
    ppermute x3, waiting for transfers between devices: 0.01 us -> 14.3 us  [local(): y[h][l] = lax.ppermute(y[h][l], ('hi', 'lo'), pairs)]
    ppermute x11 -> x13, waiting for transfers between devices: 38.2 us -> 26.5 us  [swapped(): return lax.ppermute(value, axis, pairs)]
    ppermute x11 -> x13, starting transfers between devices: 15.2 us -> 19.4 us  [swapped(): return lax.ppermute(value, axis, pairs)]
    ppermute x2 -> x0, starting transfers between devices: 3.21 us -> none  [spread_hidden(): lax.ppermute(hidden, ('hi', 'lo'), [(s, s ^ side + d) for s in range(2 *...]
    ppermute x2 -> x0, waiting for transfers between devices: 2.99 us -> none  [spread_hidden(): lax.ppermute(hidden, ('hi', 'lo'), [(s, s ^ side + d) for s in range(2 *...]
  transfers between devices with their start and end apart: 19 -> 19, of which waited for: 10 -> 12; matrix products, arithmetic and copies ran while one was open for 1% -> 1% of each run, Pallas kernels for 5% -> 5%
where the time goes in v8:
time: 102 us
  waiting for transfers between devices  62.5 us (61%)
  starting transfers between devices  27.5 us (27%)
  Pallas kernels  8.89 us (9%)
  local copies, waits for them, and re-layouts  2.02 us (2%)
    ppermute x13, waiting for transfers between devices, swapped(): return lax.ppermute(value, axis, pairs)  26.5 us
    ppermute x3, waiting for transfers between devices, local(): x[d][n] = lax.ppermute(x[d][n], ('node', 'lo'), pairs)  21.7 us
    ppermute x13, starting transfers between devices, swapped(): return lax.ppermute(value, axis, pairs)  19.4 us
    ppermute x3, waiting for transfers between devices, local(): y[h][l] = lax.ppermute(y[h][l], ('hi', 'lo'), pairs)  14.3 us
    ppermute x3, starting transfers between devices, local(): y[h][l] = lax.ppermute(y[h][l], ('hi', 'lo'), pairs)  4.5 us
    pallas_call x6, Pallas kernels, call(): pl.pallas_call(kernel, out_shape=outs, in_specs=[SMEM] * len(scalars) + [...  3.96 us
    ppermute x3, starting transfers between devices, local(): x[d][n] = lax.ppermute(x[d][n], ('node', 'lo'), pairs)  3.62 us
    pallas_call x1, Pallas kernels, pick_weights(): pl.pallas_call(pick_kernel, out_shape=shape(gate.shape, BF16), in_specs=[...  2.17 us
  transfers between devices with their start and end apart: 19, of which 12 were waited for; matrix products, arithmetic and copies ran while one was open for 1% of the time, Pallas kernels for 5%

profile of v8, /device:TPU:0, one launch (start us, length us, event | category | flops | bytes accessed | tf_op | source)
XLA Modules:
  0.0 101.9 jit_solution(6760273420617970927)
XLA Ops:
  0.0 2.2 %shard_map.74 = bf16[896,512]{1,0:T(8,128)(2,1)} custom-call(s32[1]{0:T(128)} %bitcast.1.group_ref, bf16[896,512]{1,0:T(8,128)(2,1)} %bitcast.47, bf16[896,512]{1,0:T(8,128)(2,1)} %bitcast.49), custom_call_target="tpu_custom_call" | custom-call | bytes 1835008 | tf_op jit(solution)/shard_map/pallas_call | solution.py:65
  2.2 4.1 %collective-permute-start.3 = (bf16[896,512]{1,0:T(8,128)(2,1)}, bf16[896,512]{1,0:T(8,128)(2,1)S(1)}, u32[]{:S(2)}, u32[]{:S(2)}) collective-permute-start(bf16[896,512]{1,0:T(8,128)(2,1)} %shard_map.74), channel_id=1, source_target_pairs={{0,4},{4,0},{1,5},{5,1},{2,6},{6,2},{3,7},{7,3},{8,12},{12,8},{9,1... | collective-permute-start | bytes 2752520 | tf_op jit(solution)/shard_map/ppermute | solution.py:37
  9.2 2.6 %collective-permute-start.2 = (bf16[2,64,896]{2,1,0:T(8,128)(2,1)S(1)}, bf16[2,64,896]{2,1,0:T(8,128)(2,1)S(1)}, u32[]{:S(2)}, u32[]{:S(2)}) collective-permute-start(bf16[2,64,896]{2,1,0:T(8,128)(2,1)S(1)} %get-tuple-element.50), channel_id=1, source_target_pairs={{0,10},{2,8},{8,2},{10,0},{1,11},{3,9},{9,3},{11,1},{4,14},{6,12},... | collective-permute-start | bytes 688136 | tf_op jit(solution)/shard_map/ppermute | solution.py:303
  12.8 1.5 %collective-permute-start.5 = (bf16[2,2,64,896]{3,2,1,0:T(8,128)(2,1)S(1)}, bf16[2,2,64,896]{3,2,1,0:T(8,128)(2,1)S(1)}, u32[]{:S(2)}, u32[]{:S(2)}) collective-permute-start(bf16[2,2,64,896]{3,2,1,0:T(8,128)(2,1)S(1)} %get-tuple-element.28), channel_id=1, source_target_pairs={{0,8},{8,0},{1,9},{9,1},{2,10},{10,2},{3,11},{11,3},{4,12},{12,4},... | collective-permute-start | bytes 1376264 | tf_op jit(solution)/shard_map/ppermute | solution.py:37
  14.3 17.9 %collective-permute-done.2 = bf16[2,64,896]{2,1,0:T(8,128)(2,1)S(1)} collective-permute-done((bf16[2,64,896]{2,1,0:T(8,128)(2,1)S(1)}, bf16[2,64,896]{2,1,0:T(8,128)(2,1)S(1)}, u32[]{:S(2)}, u32[]{:S(2)}) %collective-permute-start.2) | collective-permute-done | bytes 229408 | tf_op jit(solution)/shard_map/ppermute | solution.py:303
  32.2 3.8 %collective-permute-done.1 = bf16[2,64,896]{2,1,0:T(8,128)(2,1)S(1)} collective-permute-done((bf16[2,64,896]{2,1,0:T(8,128)(2,1)S(1)}, bf16[2,64,896]{2,1,0:T(8,128)(2,1)S(1)}, u32[]{:S(2)}, u32[]{:S(2)}) %collective-permute-start.1) | collective-permute-done | bytes 229408 | tf_op jit(solution)/shard_map/ppermute | solution.py:303
  36.2 10.3 %collective-permute-done.3.refs_0_ = bf16[896,512]{1,0:T(8,128)(2,1)S(1)} collective-permute-done((bf16[896,512]{1,0:T(8,128)(2,1)}, bf16[896,512]{1,0:T(8,128)(2,1)S(1)}, u32[]{:S(2)}, u32[]{:S(2)}) %collective-permute-start.3) | collective-permute-done | bytes 917536 | tf_op jit(solution)/shard_map/ppermute | solution.py:37
  46.7 3.6 %collective-permute-start.13 = (bf16[2,64,896]{2,1,0:T(8,128)(2,1)S(1)}, bf16[2,64,896]{2,1,0:T(8,128)(2,1)S(1)}, u32[]{:S(2)}, u32[]{:S(2)}) collective-permute-start(bf16[2,64,896]{2,1,0:T(8,128)(2,1)S(1)} %get-tuple-element.35), channel_id=1, source_target_pairs={{0,6},{2,4},{4,2},{6,0},{1,7},{3,5},{5,3},{7,1},{8,14},{10,12},{12... | collective-permute-start | bytes 688136 | tf_op jit(solution)/shard_map/ppermute | solution.py:316
  50.4 1.5 %collective-permute-start.7 = (bf16[896,512]{1,0:T(8,128)(2,1)S(1)}, bf16[896,512]{1,0:T(8,128)(2,1)S(1)}, u32[]{:S(2)}, u32[]{:S(2)}) collective-permute-start(bf16[896,512]{1,0:T(8,128)(2,1)S(1)} %collective-permute-done.3.refs_0_), channel_id=1, source_target_pairs={{0,16},{16,0},{1,17},{17,1},{2,18},{18,2},{3,19},{19,3},{4,20},{20... | collective-permute-start | bytes 2752520 | tf_op jit(solution)/shard_map/ppermute | solution.py:37
  52.8 1.2 %shard_map.75 = (f32[2,256,512]{2,1,0:T(8,128)S(1)}, f32[2,256,512]{2,1,0:T(8,128)S(1)}) custom-call(s32[1]{0:T(128)} %bitcast.lo_ref, s32[1]{0:T(128)} %bitcast.1.group_ref, bf16[2,2,2,64,896]{4,3,2,1,0:T(8,128)(2,1)S(1)} %pad_maximum_fusion.own_ref, bf16[2,2,2,64,896]{4,3,2,1,0:T(8,128)(2,1)S(1)} %collective-permute-done.4.other_ref, ...), custom_call_target="tpu_custom_call" | custom-call | flops 939524096 | bytes 5767168 | tf_op jit(solution)/shard_map/pallas_call | solution.py:21
  55.7 1.5 %collective-permute-done.13 = bf16[2,64,896]{2,1,0:T(8,128)(2,1)S(1)} collective-permute-done((bf16[2,64,896]{2,1,0:T(8,128)(2,1)S(1)}, bf16[2,64,896]{2,1,0:T(8,128)(2,1)S(1)}, u32[]{:S(2)}, u32[]{:S(2)}) %collective-permute-start.13) | collective-permute-done | bytes 229408 | tf_op jit(solution)/shard_map/ppermute | solution.py:316
  57.2 12.8 %collective-permute-done.12 = bf16[2,64,896]{2,1,0:T(8,128)(2,1)S(1)} collective-permute-done((bf16[2,64,896]{2,1,0:T(8,128)(2,1)S(1)}, bf16[2,64,896]{2,1,0:T(8,128)(2,1)S(1)}, u32[]{:S(2)}, u32[]{:S(2)}) %collective-permute-start.12) | collective-permute-done | bytes 229408 | tf_op jit(solution)/shard_map/ppermute | solution.py:316
  70.5 1.7 %collective-permute-done.6 = bf16[256,512]{1,0:T(8,128)(2,1)S(1)} collective-permute-done((bf16[256,512]{1,0:T(8,128)(2,1)S(1)}, bf16[256,512]{1,0:T(8,128)(2,1)S(1)}, u32[]{:S(2)}, u32[]{:S(2)}) %collective-permute-start.6) | collective-permute-done | bytes 262176 | tf_op jit(solution)/shard_map/ppermute | solution.py:37
  73.3 1.3 %collective-permute-start.8 = (bf16[256,512]{1,0:T(8,128)(2,1)S(1)}, bf16[256,512]{1,0:T(8,128)(2,1)S(1)}, u32[]{:S(2)}, u32[]{:S(2)}) collective-permute-start(bf16[256,512]{1,0:T(8,128)(2,1)S(1)} %shard_map.79), channel_id=1, source_target_pairs={{0,2},{2,0},{1,3},{3,1},{4,6},{6,4},{5,7},{7,5},{8,10},{10,8},{9,1... | collective-permute-start | bytes 786440 | tf_op jit(solution)/shard_map/ppermute | solution.py:37
  74.8 2.4 %collective-permute-start.16 = (bf16[256,256]{1,0:T(8,128)(2,1)S(1)}, bf16[256,256]{1,0:T(8,128)(2,1)S(1)}, u32[]{:S(2)}, u32[]{:S(2)}) collective-permute-start(bf16[256,256]{1,0:T(8,128)(2,1)S(1)} %fusion.1.refs_0_), channel_id=1, source_target_pairs={{0,4},{4,0},{1,5},{5,1},{2,6},{6,2},{3,7},{7,3},{8,12},{12,8},{9,1... | collective-permute-start | bytes 393224 | tf_op jit(solution)/shard_map/ppermute | solution.py:37
  77.7 6.2 %collective-permute-done.8 = bf16[256,512]{1,0:T(8,128)(2,1)S(1)} collective-permute-done((bf16[256,512]{1,0:T(8,128)(2,1)S(1)}, bf16[256,512]{1,0:T(8,128)(2,1)S(1)}, u32[]{:S(2)}, u32[]{:S(2)}) %collective-permute-start.8) | collective-permute-done | bytes 262176 | tf_op jit(solution)/shard_map/ppermute | solution.py:37
  84.1 1.7 %collective-permute-start.9 = (bf16[256,256]{1,0:T(8,128)(2,1)S(1)}, bf16[256,256]{1,0:T(8,128)(2,1)S(1)}, u32[]{:S(2)}, u32[]{:S(2)}) collective-permute-start(bf16[256,256]{1,0:T(8,128)(2,1)S(1)} %fusion.refs_4_), channel_id=1, source_target_pairs={{0,4},{4,0},{1,5},{5,1},{2,6},{6,2},{3,7},{7,3},{8,12},{12,8},{9,1... | collective-permute-start | bytes 393224 | tf_op jit(solution)/shard_map/ppermute | solution.py:37
  85.7 2.5 %collective-permute-start.15 = (bf16[256,256]{1,0:T(8,128)(2,1)S(1)}, bf16[256,256]{1,0:T(8,128)(2,1)S(1)}, u32[]{:S(2)}, u32[]{:S(2)}) collective-permute-start(bf16[256,256]{1,0:T(8,128)(2,1)S(1)} %fusion.1.refs_0_), channel_id=1, source_target_pairs={{0,2},{2,0},{1,3},{3,1},{4,6},{6,4},{5,7},{7,5},{8,10},{10,8},{9,1... | collective-permute-start | bytes 393224 | tf_op jit(solution)/shard_map/ppermute | solution.py:37
  88.3 2.0 %collective-permute-start.18 = (bf16[256,256]{1,0:T(8,128)(2,1)S(1)}, bf16[256,256]{1,0:T(8,128)(2,1)S(1)}, u32[]{:S(2)}, u32[]{:S(2)}) collective-permute-start(bf16[256,256]{1,0:T(8,128)(2,1)S(1)} %fusion.refs_4_), channel_id=1, source_target_pairs={{0,2},{2,0},{1,3},{3,1},{4,6},{6,4},{5,7},{7,5},{8,10},{10,8},{9,1... | collective-permute-start | bytes 393224 | tf_op jit(solution)/shard_map/ppermute | solution.py:37
  90.3 1.3 %collective-permute-done.9.refs_0_ = bf16[256,256]{1,0:T(8,128)(2,1)S(1)} collective-permute-done((bf16[256,256]{1,0:T(8,128)(2,1)S(1)}, bf16[256,256]{1,0:T(8,128)(2,1)S(1)}, u32[]{:S(2)}, u32[]{:S(2)}) %collective-permute-start.9) | collective-permute-done | bytes 131104 | tf_op jit(solution)/shard_map/ppermute | solution.py:37
  93.6 2.8 %collective-permute-done.17.refs_3_ = bf16[256,256]{1,0:T(8,128)(2,1)S(1)} collective-permute-done((bf16[256,256]{1,0:T(8,128)(2,1)S(1)}, bf16[256,256]{1,0:T(8,128)(2,1)S(1)}, u32[]{:S(2)}, u32[]{:S(2)}) %collective-permute-start.17) | collective-permute-done | bytes 131104 | tf_op jit(solution)/shard_map/ppermute | solution.py:37
  96.4 2.8 %collective-permute-done.18.refs_5_ = bf16[256,256]{1,0:T(8,128)(2,1)S(1)} collective-permute-done((bf16[256,256]{1,0:T(8,128)(2,1)S(1)}, bf16[256,256]{1,0:T(8,128)(2,1)S(1)}, u32[]{:S(2)}, u32[]{:S(2)}) %collective-permute-start.18) | collective-permute-done | bytes 131104 | tf_op jit(solution)/shard_map/ppermute | solution.py:37
  99.1 1.5 %shard_map.80 = (bf16[512,896]{1,0:T(8,128)(2,1)}, f32[256,896]{1,0:T(8,128)S(1)}) custom-call(s32[1]{0:T(128)} %bitcast.lo_ref, s32[1]{0:T(128)} %bitcast.1.group_ref, bf16[256,256]{1,0:T(8,128)(2,1)S(1)} %fusion.1.refs_0_, bf16[256,256]{1,0:T(8,128)(2,1)S(1)} %collective-permute-done.15.refs_1_, bf16[256,256]{1,0:T(8,128)(2,1)S(1)} %collective-permute-done.16.refs_2_, ...), custom_call_target="tpu_custom_call" | custom-call | flops 704643072 | bytes 1835008 | tf_op jit(solution)/shard_map/pallas_call | solution.py:234
  100.7 1.2 %shard_map.81 = bf16[512,896]{1,0:T(8,128)(2,1)} custom-call(s32[1]{0:T(128)} %bitcast.lo_ref, s32[1]{0:T(128)} %bitcast.1.group_ref, bf16[256,256]{1,0:T(8,128)(2,1)S(1)} %collective-permute-done.9.refs_0_, bf16[256,256]{1,0:T(8,128)(2,1)S(1)} %collective-permute-done.10.refs_1_, ...), custom_call_target="tpu_custom_call", output_to_operand_aliasing={{}: (7, {})} | custom-call | flops 234881024 | bytes 1835008 | tf_op jit(solution)/shard_map/pallas_call | solution.py:243
  (53 shorter events, 11.2 us)
Async XLA Ops:
  0.0 6.3 %copy-start.2 = (bf16[128,3584]{1,0:T(8,128)(2,1)S(1)}, bf16[128,3584]{1,0:T(8,128)(2,1)}, u32[]{:S(2)}) copy-start(bf16[128,3584]{1,0:T(8,128)(2,1)} %x_ref.1) | copy-start | bytes 2752516
  2.2 44.3 %collective-permute-start.3 = (bf16[896,512]{1,0:T(8,128)(2,1)}, bf16[896,512]{1,0:T(8,128)(2,1)S(1)}, u32[]{:S(2)}, u32[]{:S(2)}) collective-permute-start(bf16[896,512]{1,0:T(8,128)(2,1)} %shard_map.74), channel_id=1, source_target_pairs={{0,4},{4,0},{1,5},{5,1},{2,6},{6,2},{3,7},{7,3},{8,12},{12,8},{9,1... | collective-permute-start | bytes 2752520 | tf_op jit(solution)/shard_map/ppermute | solution.py:37
  7.0 1.2 %copy-start.3 = (bf16[128,3584]{1,0:T(8,128)(2,1)S(1)}, bf16[128,3584]{1,0:T(8,128)(2,1)}, u32[]{:S(2)}) copy-start(bf16[128,3584]{1,0:T(8,128)(2,1)} %c_ref.1) | copy-start | bytes 2752516
  9.2 23.1 %collective-permute-start.2 = (bf16[2,64,896]{2,1,0:T(8,128)(2,1)S(1)}, bf16[2,64,896]{2,1,0:T(8,128)(2,1)S(1)}, u32[]{:S(2)}, u32[]{:S(2)}) collective-permute-start(bf16[2,64,896]{2,1,0:T(8,128)(2,1)S(1)} %get-tuple-element.50), channel_id=1, source_target_pairs={{0,10},{2,8},{8,2},{10,0},{1,11},{3,9},{9,3},{11,1},{4,14},{6,12},... | collective-permute-start | bytes 688136 | tf_op jit(solution)/shard_map/ppermute | solution.py:303
  11.8 24.2 %collective-permute-start.1 = (bf16[2,64,896]{2,1,0:T(8,128)(2,1)S(1)}, bf16[2,64,896]{2,1,0:T(8,128)(2,1)S(1)}, u32[]{:S(2)}, u32[]{:S(2)}) collective-permute-start(bf16[2,64,896]{2,1,0:T(8,128)(2,1)S(1)} %get-tuple-element.48), channel_id=1, source_target_pairs={{0,2},{2,0},{8,10},{10,8},{1,3},{3,1},{9,11},{11,9},{4,6},{6,4},{1... | collective-permute-start | bytes 688136 | tf_op jit(solution)/shard_map/ppermute | solution.py:303
  12.3 23.8 %collective-permute-start = (bf16[2,64,896]{2,1,0:T(8,128)(2,1)S(1)}, bf16[2,64,896]{2,1,0:T(8,128)(2,1)S(1)}, u32[]{:S(2)}, u32[]{:S(2)}) collective-permute-start(bf16[2,64,896]{2,1,0:T(8,128)(2,1)S(1)} %get-tuple-element.49), channel_id=1, source_target_pairs={{0,8},{2,10},{8,0},{10,2},{1,9},{3,11},{9,1},{11,3},{4,12},{6,14},... | collective-permute-start | bytes 688136 | tf_op jit(solution)/shard_map/ppermute | solution.py:303
  12.8 33.7 %collective-permute-start.5 = (bf16[2,2,64,896]{3,2,1,0:T(8,128)(2,1)S(1)}, bf16[2,2,64,896]{3,2,1,0:T(8,128)(2,1)S(1)}, u32[]{:S(2)}, u32[]{:S(2)}) collective-permute-start(bf16[2,2,64,896]{3,2,1,0:T(8,128)(2,1)S(1)} %get-tuple-element.28), channel_id=1, source_target_pairs={{0,8},{8,0},{1,9},{9,1},{2,10},{10,2},{3,11},{11,3},{4,12},{12,4},... | collective-permute-start | bytes 1376264 | tf_op jit(solution)/shard_map/ppermute | solution.py:37
  46.5 6.3 %collective-permute-start.4 = (bf16[2,2,2,64,896]{4,3,2,1,0:T(8,128)(2,1)S(1)}, bf16[2,2,2,64,896]{4,3,2,1,0:T(8,128)(2,1)S(1)}, u32[]{:S(2)}, u32[]{:S(2)}) collective-permute-start(bf16[2,2,2,64,896]{4,3,2,1,0:T(8,128)(2,1)S(1)} %pad_maximum_fusion.own_ref), channel_id=1, source_target_pairs={{0,1},{1,0},{2,3},{3,2},{4,5},{5,4},{6,7},{7,6},{8,9},{9,8},{10,11... | collective-permute-start | bytes 2752520 | tf_op jit(solution)/shard_map/ppermute | solution.py:37
  46.6 6.2 %copy-start = (bf16[1,896,512]{2,1,0:T(8,128)(2,1)S(1)}, bf16[1,896,512]{2,1,0:T(8,128)(2,1)}, u32[]{:S(2)}) copy-start(bf16[1,896,512]{2,1,0:T(8,128)(2,1)} %param.11) | copy-start | bytes 2752516
  46.6 6.2 %copy-start.1 = (bf16[1,896,512]{2,1,0:T(8,128)(2,1)S(1)}, bf16[1,896,512]{2,1,0:T(8,128)(2,1)}, u32[]{:S(2)}) copy-start(bf16[1,896,512]{2,1,0:T(8,128)(2,1)} %param.12) | copy-start | bytes 2752516
  46.7 10.4 %collective-permute-start.13 = (bf16[2,64,896]{2,1,0:T(8,128)(2,1)S(1)}, bf16[2,64,896]{2,1,0:T(8,128)(2,1)S(1)}, u32[]{:S(2)}, u32[]{:S(2)}) collective-permute-start(bf16[2,64,896]{2,1,0:T(8,128)(2,1)S(1)} %get-tuple-element.35), channel_id=1, source_target_pairs={{0,6},{2,4},{4,2},{6,0},{1,7},{3,5},{5,3},{7,1},{8,14},{10,12},{12... | collective-permute-start | bytes 688136 | tf_op jit(solution)/shard_map/ppermute | solution.py:316
  50.4 19.6 %collective-permute-start.12 = (bf16[2,64,896]{2,1,0:T(8,128)(2,1)S(1)}, bf16[2,64,896]{2,1,0:T(8,128)(2,1)S(1)}, u32[]{:S(2)}, u32[]{:S(2)}) collective-permute-start(bf16[2,64,896]{2,1,0:T(8,128)(2,1)S(1)} %get-tuple-element.34), channel_id=1, source_target_pairs={{0,4},{2,6},{4,0},{6,2},{1,5},{3,7},{5,1},{7,3},{8,12},{10,14},{12... | collective-permute-start | bytes 688136 | tf_op jit(solution)/shard_map/ppermute | solution.py:316
  50.4 22.5 %collective-permute-start.7 = (bf16[896,512]{1,0:T(8,128)(2,1)S(1)}, bf16[896,512]{1,0:T(8,128)(2,1)S(1)}, u32[]{:S(2)}, u32[]{:S(2)}) collective-permute-start(bf16[896,512]{1,0:T(8,128)(2,1)S(1)} %collective-permute-done.3.refs_0_), channel_id=1, source_target_pairs={{0,16},{16,0},{1,17},{17,1},{2,18},{18,2},{3,19},{19,3},{4,20},{20... | collective-permute-start | bytes 2752520 | tf_op jit(solution)/shard_map/ppermute | solution.py:37
  51.9 18.1 %collective-permute-start.11 = (bf16[2,64,896]{2,1,0:T(8,128)(2,1)S(1)}, bf16[2,64,896]{2,1,0:T(8,128)(2,1)S(1)}, u32[]{:S(2)}, u32[]{:S(2)}) collective-permute-start(bf16[2,64,896]{2,1,0:T(8,128)(2,1)S(1)} %get-tuple-element.33), channel_id=1, source_target_pairs={{0,2},{2,0},{4,6},{6,4},{1,3},{3,1},{5,7},{7,5},{8,10},{10,8},{12,... | collective-permute-start | bytes 688136 | tf_op jit(solution)/shard_map/ppermute | solution.py:316
  54.5 17.7 %collective-permute-start.6 = (bf16[256,512]{1,0:T(8,128)(2,1)S(1)}, bf16[256,512]{1,0:T(8,128)(2,1)S(1)}, u32[]{:S(2)}, u32[]{:S(2)}) collective-permute-start(bf16[256,512]{1,0:T(8,128)(2,1)S(1)} %shard_map.77), channel_id=1, source_target_pairs={{0,2},{2,0},{1,3},{3,1},{4,6},{6,4},{5,7},{7,5},{8,10},{10,8},{9,1... | collective-permute-start | bytes 786440 | tf_op jit(solution)/shard_map/ppermute | solution.py:37
  73.3 10.6 %collective-permute-start.8 = (bf16[256,512]{1,0:T(8,128)(2,1)S(1)}, bf16[256,512]{1,0:T(8,128)(2,1)S(1)}, u32[]{:S(2)}, u32[]{:S(2)}) collective-permute-start(bf16[256,512]{1,0:T(8,128)(2,1)S(1)} %shard_map.79), channel_id=1, source_target_pairs={{0,2},{2,0},{1,3},{3,1},{4,6},{6,4},{5,7},{7,5},{8,10},{10,8},{9,1... | collective-permute-start | bytes 786440 | tf_op jit(solution)/shard_map/ppermute | solution.py:37
  74.7 18.0 %collective-permute-start.14 = (bf16[2,2,2,64,896]{4,3,2,1,0:T(8,128)(2,1)S(1)}, bf16[2,2,2,64,896]{4,3,2,1,0:T(8,128)(2,1)S(1)}, u32[]{:S(2)}, u32[]{:S(2)}) collective-permute-start(bf16[2,2,2,64,896]{4,3,2,1,0:T(8,128)(2,1)S(1)} %pad_maximum_fusion.1.refs_6_.refs_2_), channel_id=1, source_target_pairs={{0,1},{1,0},{2,3},{3,2},{4,5},{5,4},{6,7},{7,6},{8,9},{9,8},{10,11... | collective-permute-start | bytes 2752520 | tf_op jit(solution)/shard_map/ppermute | solution.py:37
  74.8 13.5 %collective-permute-start.16 = (bf16[256,256]{1,0:T(8,128)(2,1)S(1)}, bf16[256,256]{1,0:T(8,128)(2,1)S(1)}, u32[]{:S(2)}, u32[]{:S(2)}) collective-permute-start(bf16[256,256]{1,0:T(8,128)(2,1)S(1)} %fusion.1.refs_0_), channel_id=1, source_target_pairs={{0,4},{4,0},{1,5},{5,1},{2,6},{6,2},{3,7},{7,3},{8,12},{12,8},{9,1... | collective-permute-start | bytes 393224 | tf_op jit(solution)/shard_map/ppermute | solution.py:37
  77.6 21.5 %copy-start.4 = (bf16[1,512,896]{2,1,0:T(8,128)(2,1)S(1)}, bf16[1,512,896]{2,1,0:T(8,128)(2,1)}, u32[]{:S(2)}) copy-start(bf16[1,512,896]{2,1,0:T(8,128)(2,1)} %param.13) | copy-start | bytes 2752516
  84.1 7.6 %collective-permute-start.9 = (bf16[256,256]{1,0:T(8,128)(2,1)S(1)}, bf16[256,256]{1,0:T(8,128)(2,1)S(1)}, u32[]{:S(2)}, u32[]{:S(2)}) collective-permute-start(bf16[256,256]{1,0:T(8,128)(2,1)S(1)} %fusion.refs_4_), channel_id=1, source_target_pairs={{0,4},{4,0},{1,5},{5,1},{2,6},{6,2},{3,7},{7,3},{8,12},{12,8},{9,1... | collective-permute-start | bytes 393224 | tf_op jit(solution)/shard_map/ppermute | solution.py:37
  85.7 7.8 %collective-permute-start.15 = (bf16[256,256]{1,0:T(8,128)(2,1)S(1)}, bf16[256,256]{1,0:T(8,128)(2,1)S(1)}, u32[]{:S(2)}, u32[]{:S(2)}) collective-permute-start(bf16[256,256]{1,0:T(8,128)(2,1)S(1)} %fusion.1.refs_0_), channel_id=1, source_target_pairs={{0,2},{2,0},{1,3},{3,1},{4,6},{6,4},{5,7},{7,5},{8,10},{10,8},{9,1... | collective-permute-start | bytes 393224 | tf_op jit(solution)/shard_map/ppermute | solution.py:37
  88.2 8.1 %collective-permute-start.17 = (bf16[256,256]{1,0:T(8,128)(2,1)S(1)}, bf16[256,256]{1,0:T(8,128)(2,1)S(1)}, u32[]{:S(2)}, u32[]{:S(2)}) collective-permute-start(bf16[256,256]{1,0:T(8,128)(2,1)S(1)} %collective-permute-done.16.refs_2_), channel_id=1, source_target_pairs={{0,2},{2,0},{1,3},{3,1},{4,6},{6,4},{5,7},{7,5},{8,10},{10,8},{9,1... | collective-permute-start | bytes 393224 | tf_op jit(solution)/shard_map/ppermute | solution.py:37
  88.3 10.9 %collective-permute-start.18 = (bf16[256,256]{1,0:T(8,128)(2,1)S(1)}, bf16[256,256]{1,0:T(8,128)(2,1)S(1)}, u32[]{:S(2)}, u32[]{:S(2)}) collective-permute-start(bf16[256,256]{1,0:T(8,128)(2,1)S(1)} %fusion.refs_4_), channel_id=1, source_target_pairs={{0,2},{2,0},{1,3},{3,1},{4,6},{6,4},{5,7},{7,5},{8,10},{10,8},{9,1... | collective-permute-start | bytes 393224 | tf_op jit(solution)/shard_map/ppermute | solution.py:37
  91.6 9.1 %collective-permute-start.10 = (bf16[256,256]{1,0:T(8,128)(2,1)S(1)}, bf16[256,256]{1,0:T(8,128)(2,1)S(1)}, u32[]{:S(2)}, u32[]{:S(2)}) collective-permute-start(bf16[256,256]{1,0:T(8,128)(2,1)S(1)} %collective-permute-done.9.refs_0_), channel_id=1, source_target_pairs={{0,2},{2,0},{1,3},{3,1},{4,6},{6,4},{5,7},{7,5},{8,10},{10,8},{9,1... | collective-permute-start | bytes 393224 | tf_op jit(solution)/shard_map/ppermute | solution.py:37
  (2 other events, 1.3 us)
